TPU v7x, 128 devices: a whole 4x4x4 slice. The times are simulated.
128 devices in a mesh: grp: 8 (over x_lo, y), blk: 16 (over z, x_hi, core).
Axes of the slice: x: 4 (x_hi: 2, x_lo: 2; x = x_hi * 2 + x_lo), y: 4, z: 4, core: 2. Of those that a mesh axis runs over, the one named last changes fastest.
Arguments:
- features: bfloat16 [16384, 4096], P('blk', 'grp'), may hold values from -6 to 6
- grad_out: bfloat16 [16384, 4096], P('blk', 'grp'), may hold values from -6 to 6
- scores: float32 [16384], P('blk'), may hold values from 0.05 to 1
- counts: int32 [16, 2], P('blk'), may hold values from 0 to 1024, as said below
- w_gate: bfloat16 [2, 1536, 4096], P(None, 'grp', 'blk'), may hold values from -0.09375 to 0.09375
- w_up: bfloat16 [2, 1536, 4096], P(None, 'grp', 'blk'), may hold values from -0.09375 to 0.09375
- w_down: bfloat16 [2, 1536, 4096], P(None, 'grp', 'blk'), may hold values from -0.15625 to 0.15625
Outputs:
- grad_features: bfloat16 [16384, 4096], P('blk', 'grp')
- grad_scores: float32 [16384], P('blk')
- grad_gate: float32 [2, 1536, 4096], P(None, 'grp', 'blk')
- grad_up: float32 [2, 1536, 4096], P(None, 'grp', 'blk')
- grad_down: float32 [2, 1536, 4096], P(None, 'grp', 'blk')
Inputs may be any that keep to these rules, and one draw needn't show every extreme that they name: Every count is a multiple of 128; the counts of one row block sum to at most 1024, and in every draw some row block sends all 1024 rows to one expert.
All inputs are finite; a program needn't handle non-finite values.
Results may differ from a plain program's by a relative error of at most 0.019.
Values may be sent and summed in bfloat16 or wider, within the bound.
No kernel may reach another device: no remote copies, remote signals or barrier semaphores. Data moves between devices by JAX's collectives and lax.ppermute only.
A program may use at most 256 MiB of HBM per device.

v0:
```python
import jax
import jax.numpy as jnp
from jax import lax
from jax.sharding import PartitionSpec as P

EXP = 2
BLOCK = 128


def block_grads(row_block, grad_block, score_block, gate_mat, up_mat, down_mat, live_flag):
    contract = (((1,), (1,)), ((), ()))
    gate_pre = lax.dot_general(row_block, gate_mat, contract, preferred_element_type=jnp.float32)
    up_pre = lax.dot_general(row_block, up_mat, contract, preferred_element_type=jnp.float32)
    back_grad = lax.dot_general(grad_block, down_mat, contract, preferred_element_type=jnp.float32)
    sig_gate = jax.nn.sigmoid(gate_pre)
    act_gate = gate_pre * sig_gate
    hidden = lax.optimization_barrier((act_gate * up_pre).astype(jnp.bfloat16))
    hidden_wide = hidden.astype(jnp.float32)
    row_mask = jnp.where(live_flag, 1.0, 0.0).astype(jnp.float32)
    row_scale = score_block * row_mask
    score_grad = jnp.sum(hidden_wide * back_grad, axis=1) * row_mask
    hid_grad = row_scale[:, None] * back_grad
    gate_grad = (hid_grad * up_pre * sig_gate * (1.0 + gate_pre * (1.0 - sig_gate))).astype(
        jnp.bfloat16
    )
    up_grad = (hid_grad * act_gate).astype(jnp.bfloat16)
    scaled = (row_scale[:, None] * hidden_wide).astype(jnp.bfloat16)
    return (score_grad, gate_grad, up_grad, scaled)


def add_expert(accum, part, expert_id):
    current = lax.dynamic_index_in_dim(accum, expert_id, 0, False)
    return lax.dynamic_update_index_in_dim(accum, current + part, expert_id, 0)


def on_device(features, grad_out, scores, counts, w_gate, w_up, w_down):
    row_feats, grad_feats = (
        lax.all_gather(features, "grp", axis=1, tiled=True),
        lax.all_gather(grad_out, "grp", axis=1, tiled=True),
    )
    gate_all, up_all, down_all = (
        lax.all_gather(w_gate, "blk", axis=2, tiled=True),
        lax.all_gather(w_up, "blk", axis=2, tiled=True),
        lax.all_gather(w_down, "blk", axis=2, tiled=True),
    )
    row_count, feat_width = row_feats.shape
    block_count = row_count // BLOCK
    bounds = jnp.cumsum(counts[0])
    starts = jnp.arange(block_count, dtype=jnp.int32) * BLOCK
    above = (starts[:, None] >= bounds[None, :]).astype(jnp.int32)
    expert_ids = jnp.minimum(jnp.sum(above, axis=1), EXP - 1)
    live_flags = starts < bounds[EXP - 1]
    tcon = (((0,), (0,)), ((), ()))

    def block_work(row_block, grad_block, score_block, expert_id, live_flag):
        gate_mat = lax.dynamic_index_in_dim(gate_all, expert_id, 0, False)
        up_mat = lax.dynamic_index_in_dim(up_all, expert_id, 0, False)
        down_mat = lax.dynamic_index_in_dim(down_all, expert_id, 0, False)
        score_grad, gate_grad, up_grad, scaled = block_grads(
            row_block, grad_block, score_block, gate_mat, up_mat, down_mat, live_flag
        )
        part_gate = lax.dot_general(gate_grad, row_block, tcon, preferred_element_type=jnp.float32)
        part_up = lax.dot_general(up_grad, row_block, tcon, preferred_element_type=jnp.float32)
        part_down = lax.dot_general(scaled, grad_block, tcon, preferred_element_type=jnp.float32)
        input_part = jnp.dot(gate_grad, gate_mat, preferred_element_type=jnp.float32) + jnp.dot(
            up_grad, up_mat, preferred_element_type=jnp.float32
        )
        return (score_grad, gate_grad, up_grad, part_gate, part_up, part_down, input_part)

    def block_step(carried, inputs):
        row_block, grad_block, score_block, expert_id, live_flag = inputs
        results = block_work(row_block, grad_block, score_block, expert_id, live_flag)
        carried = (
            add_expert(carried[0], results[3], expert_id),
            add_expert(carried[1], results[4], expert_id),
            add_expert(carried[2], results[5], expert_id),
        )
        return (carried, (results[0], results[1], results[2], results[6]))

    zeros_acc = jnp.zeros(gate_all.shape, jnp.float32)
    block_inputs = (
        row_feats.reshape(block_count, BLOCK, feat_width),
        grad_feats.reshape(block_count, BLOCK, feat_width),
        scores.reshape(block_count, BLOCK),
        expert_ids,
        live_flags,
    )
    accums, (score_grads, gate_grads, up_grads, input_parts) = lax.scan(
        block_step, (zeros_acc, zeros_acc, zeros_acc), block_inputs
    )
    grad_scores = lax.psum(score_grads.reshape(row_count), "grp")
    grad_gate, grad_up, grad_down = (
        lax.psum_scatter(
            accums[0].astype(jnp.bfloat16), "blk", scatter_dimension=2, tiled=True
        ).astype(jnp.float32),
        lax.psum_scatter(
            accums[1].astype(jnp.bfloat16), "blk", scatter_dimension=2, tiled=True
        ).astype(jnp.float32),
        lax.psum_scatter(
            accums[2].astype(jnp.bfloat16), "blk", scatter_dimension=2, tiled=True
        ).astype(jnp.float32),
    )
    summed = lax.psum_scatter(
        input_parts.reshape(row_count, feat_width).astype(jnp.bfloat16),
        "grp",
        scatter_dimension=1,
        tiled=True,
    )
    return (summed, grad_scores, grad_gate, grad_up, grad_down)


def solution(mesh):
    placed = (
        P("blk", "grp"),
        P("blk", "grp"),
        P("blk"),
        P("blk", None),
        P(None, "grp", "blk"),
        P(None, "grp", "blk"),
        P(None, "grp", "blk"),
    )
    return jax.shard_map(
        on_device,
        mesh=mesh,
        in_specs=placed,
        out_specs=(
            P("blk", "grp"),
            P("blk"),
            P(None, "grp", "blk"),
            P(None, "grp", "blk"),
            P(None, "grp", "blk"),
        ),
        check_vma=False,
    )
```

profile of v0, /device:TPU:3, one launch (start us, length us, event | category | flops | bytes accessed | tf_op | source)
XLA Modules:
  0.0 941.0 jit_solution(6971167129024486651)
XLA Ops:
  12.8 51.5 %all-gather.14.cloned.1.call-done = bf16[2,192,4096]{2,1,0:T(8,128)(2,1)} async-done(((bf16[2,192,256]{2,1,0:T(8,128)(2,1)}), bf16[2,192,4096]{2,1,0:T(8,128)(2,1)}) %all-gather.14.cloned.1.call-update) | async-done | bytes 3145744 | tf_op jit(solution)/shard_map/all_gather | solution.py:42
  64.2 52.0 %all-gather.12.cloned.1.call-done = bf16[2,192,4096]{2,1,0:T(8,128)(2,1)} async-done(((bf16[2,192,256]{2,1,0:T(8,128)(2,1)}), bf16[2,192,4096]{2,1,0:T(8,128)(2,1)}) %all-gather.12.cloned.1.call-update) | async-done | bytes 3145744 | tf_op jit(solution)/shard_map/all_gather | solution.py:43
  116.3 52.1 %all-gather.8.cloned.1.call-done = bf16[2,192,4096]{2,1,0:T(8,128)(2,1)} async-done(((bf16[2,192,256]{2,1,0:T(8,128)(2,1)}), bf16[2,192,4096]{2,1,0:T(8,128)(2,1)}) %all-gather.8.cloned.1.call-update) | async-done | bytes 3145744 | tf_op jit(solution)/shard_map/all_gather | solution.py:44
  168.4 90.7 %all-gather.10.cloned.1.call-done = bf16[1024,4096]{1,0:T(8,128)(2,1)} async-done(((bf16[1024,512]{1,0:T(8,128)(2,1)}), bf16[1024,4096]{1,0:T(8,128)(2,1)}) %all-gather.10.cloned.1.call-update) | async-done | bytes 8388624 | tf_op jit(solution)/shard_map/all_gather | solution.py:38
  259.0 92.2 %all-gather.6.cloned.1.call-done = bf16[1024,4096]{1,0:T(8,128)(2,1)} async-done(((bf16[1024,512]{1,0:T(8,128)(2,1)}), bf16[1024,4096]{1,0:T(8,128)(2,1)}) %all-gather.6.cloned.1.call-update) | async-done | bytes 8388624 | tf_op jit(solution)/shard_map/all_gather | solution.py:39
  351.3 3.4 broadcast_in_dim.29.clone.1
  354.6 3.5 broadcast_in_dim.29.clone
  358.1 3.5 broadcast_in_dim.29
  361.6 242.4 %while.18 = (s32[]{:T(128)}, f32[2,192,4096]{2,1,0:T(8,128)}, f32[2,192,4096]{2,1,0:T(8,128)}, f32[2,192,4096]{2,1,0:T(8,128)}, f32[8,128]{1,0:T(8,128)S(1)}, /*...) while((s32[]{:T(128)}, f32[2,192,4096]{2,1,0:T(8,128)}, ...), condition=%wide.region_4.5_spmd, body=%wide.region_2.4_spmd.sunk | while | flops 1614037120 | bytes 216519792 | solution.py:88
  368.7 2.3 fusion.92
  377.4 2.6 fusion.94
  386.6 2.6 fusion.96
  389.3 2.6 copy-done.1
  399.0 2.3 fusion.92
  407.7 2.6 fusion.94
  416.9 2.6 fusion.96
  419.6 2.6 copy-done.1
  429.3 2.3 fusion.92
  438.0 2.6 fusion.94
  447.2 2.6 fusion.96
  449.9 2.6 copy-done.1
  459.6 2.3 fusion.92
  468.3 2.6 fusion.94
  477.5 2.6 fusion.96
  480.2 2.6 copy-done.1
  489.9 2.3 fusion.92
  498.6 2.6 fusion.94
  507.8 2.6 fusion.96
  510.5 2.6 copy-done.1
  520.2 2.3 fusion.92
  528.9 2.6 fusion.94
  538.1 2.6 fusion.96
  540.8 2.6 copy-done.1
  559.2 2.6 fusion.94
  568.4 2.6 fusion.96
  571.1 2.6 copy-done.1
  580.8 2.3 fusion.92
  589.5 2.6 fusion.94
  598.7 2.6 fusion.96
  601.4 2.6 copy-done.1
  604.0 4.9 convert_element_type.45
  609.0 4.9 convert_element_type.47
  614.0 5.0 convert_element_type.49
  619.7 14.4 %psum.7 = f32[1024]{0:T(1024)} all-reduce(f32[1024]{0:T(1024)S(1)} %bitcast.132), channel_id=1, replica_groups=mesh['grp'=8,'blk'=16] {'grp'}, use_global_device_ids=true, to_apply=%region_6.7 | all-reduce | flops 1024 | bytes 8192 | tf_op jit(solution)/shard_map/psum | solution.py:91
  634.1 48.1 %reduce-scatter.7.cloned.1.call-done = bf16[2,192,256]{2,1,0:T(8,128)(2,1)} async-done(((bf16[2,192,4096]{2,1,0:T(8,128)(2,1)}), bf16[2,192,256]{2,1,0:T(8,128)(2,1)}) %reduce-scatter.7.cloned.1.call-update) | async-done | bytes 196624 | tf_op jit(solution)/shard_map/reduce_scatter | solution.py:93
  683.9 76.6 %reduce-scatter.9.cloned.1.call-done = bf16[2,192,256]{2,1,0:T(8,128)(2,1)} async-done(((bf16[2,192,4096]{2,1,0:T(8,128)(2,1)}), bf16[2,192,256]{2,1,0:T(8,128)(2,1)}) %reduce-scatter.9.cloned.1.call-update) | async-done | bytes 196624 | tf_op jit(solution)/shard_map/reduce_scatter | solution.py:96
  762.2 76.6 %reduce-scatter.11.cloned.1.call-done = bf16[2,192,256]{2,1,0:T(8,128)(2,1)} async-done(((bf16[2,192,4096]{2,1,0:T(8,128)(2,1)}), bf16[2,192,256]{2,1,0:T(8,128)(2,1)}) %reduce-scatter.11.cloned.1.call-update) | async-done | bytes 196624 | tf_op jit(solution)/shard_map/reduce_scatter | solution.py:99
  840.5 94.0 %reduce-scatter.5.cloned.1.call-done = bf16[1024,512]{1,0:T(8,128)(2,1)} async-done(((bf16[1024,4096]{1,0:T(8,128)(2,1)}), bf16[1024,512]{1,0:T(8,128)(2,1)}) %reduce-scatter.5.cloned.1.call-update) | async-done | bytes 1048592 | tf_op jit(solution)/shard_map/reduce_scatter | solution.py:103
  (326 shorter events, 150.5 us)
Async XLA Ops:
  7.2 57.1 %all-gather.14.cloned.1.call-start = ((), (), s32[]{:S(2)}) async-start(), calls=%async_computation.8 | async-start | bytes 3342336 | tf_op jit(solution)/shard_map/all_gather | solution.py:42
  7.9 108.4 %all-gather.12.cloned.1.call-start = ((), (), s32[]{:S(2)}) async-start(), calls=%async_computation.7 | async-start | bytes 3342336 | tf_op jit(solution)/shard_map/all_gather | solution.py:43
  8.6 159.7 %all-gather.8.cloned.1.call-start = ((), (), s32[]{:S(2)}) async-start(), calls=%async_computation.5 | async-start | bytes 3342336 | tf_op jit(solution)/shard_map/all_gather | solution.py:44
  9.4 249.6 %all-gather.10.cloned.1.call-start = ((), (), s32[]{:S(2)}) async-start(), calls=%async_computation.6 | async-start | bytes 9437184 | tf_op jit(solution)/shard_map/all_gather | solution.py:38
  10.0 341.3 %all-gather.6.cloned.1.call-start = ((), (), s32[]{:S(2)}) async-start(), calls=%async_computation.4 | async-start | bytes 9437184 | tf_op jit(solution)/shard_map/all_gather | solution.py:39
  10.5 671.6 %reduce-scatter.7.cloned.1.call-start = ((), (), s32[]{:S(2)}) async-start(), calls=%async_computation.10 | async-start | bytes 3342336 | tf_op jit(solution)/shard_map/reduce_scatter | solution.py:93
  364.2 6.9 copy-start.4
  371.0 6.4 slice-start
  375.1 6.4 slice-start.2
  375.1 6.4 slice-start.4
  377.4 6.6 slice-start.5
  394.4 6.9 copy-start.4
  401.3 6.4 slice-start
  405.4 6.4 slice-start.2
  405.4 6.4 slice-start.4
  407.7 6.6 slice-start.5
  424.7 6.9 copy-start.4
  431.6 6.4 slice-start
  435.7 6.4 slice-start.2
  435.7 6.4 slice-start.4
  438.0 6.6 slice-start.5
  455.0 6.9 copy-start.4
  461.9 6.4 slice-start
  466.0 6.4 slice-start.2
  468.3 6.6 slice-start.5
  485.3 6.9 copy-start.4
  492.2 6.4 slice-start
  496.3 6.4 slice-start.2
  496.3 6.4 slice-start.4
  498.6 6.6 slice-start.5
  515.6 6.9 copy-start.4
  522.5 6.4 slice-start
  526.6 6.4 slice-start.2
  526.6 6.4 slice-start.4
  528.9 6.6 slice-start.5
  545.9 6.9 copy-start.4
  552.8 6.4 slice-start
  556.9 6.4 slice-start.2
  556.9 6.4 slice-start.4
  559.2 6.6 slice-start.5
  576.2 6.9 copy-start.4
  583.1 6.4 slice-start
  587.2 6.5 slice-start.2
  587.2 6.5 slice-start.4
  589.5 6.6 slice-start.5
  608.9 151.6 %reduce-scatter.9.cloned.1.call-start = ((), (), s32[]{:S(2)}) async-start(), calls=%async_computation.11 | async-start | bytes 3342336 | tf_op jit(solution)/shard_map/reduce_scatter | solution.py:96
  613.9 224.8 %reduce-scatter.11.cloned.1.call-start = ((), (), s32[]{:S(2)}) async-start(), calls=%async_computation.12 | async-start | bytes 3342336 | tf_op jit(solution)/shard_map/reduce_scatter | solution.py:99
  619.0 315.5 %reduce-scatter.5.cloned.1.call-start = ((), (), s32[]{:S(2)}) async-start(), calls=%async_computation.9 | async-start | bytes 9437184 | tf_op jit(solution)/shard_map/reduce_scatter | solution.py:103
  (49 other events, 196.9 us)
Sparse Core Ops, SparseCore 0:
  10.3 53.8 all-gather.13
  66.6 49.6 all-gather.11
  118.6 49.6 all-gather.7
  169.9 89.1 all-gather.9
  260.5 90.6 all-gather.5
  609.0 73.1 reduce-scatter.6
  686.2 74.1 reduce-scatter.8
  764.5 74.1 reduce-scatter.10
  841.8 92.6 reduce-scatter.4
where the time goes:
time: 945 us; the launch traced here: 941 us
  waiting for transfers between devices  638 us (68%)
  matrix products  136 us (14%)
  local copies, waits for them, and re-layouts  86.3 us (9%)
  other arithmetic  27.5 us (3%)
  loops' own time  24.7 us (3%)
  blocking collectives  14.4 us (2%)
  between operations  13.9 us (1%)
    reduce_scatter x1, waiting for transfers between devices, on_device(): lax.psum_scatter(input_parts.reshape(row_count, feat_width).astype(jnp.bf...  94 us
    all_gather x1, waiting for transfers between devices, on_device(): lax.all_gather(grad_out, 'grp', axis=1, tiled=True)  92.2 us
    all_gather x1, waiting for transfers between devices, on_device(): lax.all_gather(features, 'grp', axis=1, tiled=True)  90.7 us
    reduce_scatter x1, waiting for transfers between devices, on_device(): lax.psum_scatter(accums[1].astype(jnp.bfloat16), 'blk', scatter_dimension...  76.6 us
    reduce_scatter x1, waiting for transfers between devices, on_device(): lax.psum_scatter(accums[2].astype(jnp.bfloat16), 'blk', scatter_dimension...  76.6 us
    all_gather x1, waiting for transfers between devices, on_device(): lax.all_gather(w_down, 'blk', axis=2, tiled=True)  52.1 us
    all_gather x1, waiting for transfers between devices, on_device(): lax.all_gather(w_up, 'blk', axis=2, tiled=True)  52 us
    all_gather x1, waiting for transfers between devices, on_device(): lax.all_gather(w_gate, 'blk', axis=2, tiled=True)  51.5 us
  transfers between devices with their start and end apart: 9, of which 9 were waited for; matrix products, arithmetic and copies ran while one was open for 2% of the time, Pallas kernels for 0%

commit v1 on v0

v1 whole, which is shorter than its diff:
```python
import functools

import jax
import jax.numpy as jnp
from jax import lax
from jax.experimental import pallas as pl
from jax.experimental.pallas import tpu as pltpu
from jax.sharding import Mesh
from jax.sharding import PartitionSpec as P

EXP = 2
BLOCK = 128
TILE = 256
BF = jnp.bfloat16
F32 = jnp.float32
NT = (((1,), (1,)), ((), ()))
OFFS = (0, 3, 1, 2)
ANY = pl.BlockSpec(memory_space=pl.ANY)
VM = pl.BlockSpec(memory_space=pltpu.VMEM)
SM = pl.BlockSpec(memory_space=pltpu.SMEM)


def ring(n, k):
    return [(i, (i + k) % n) for i in range(n)]


def home(xl, z):
    return (xl, z) if z // 2 == xl else (1 - xl, (z + 2) % 4)


def swap_pairs(flip):
    pairs = []
    for xl in range(2):
        for z in range(4):
            for xh in range(2):
                a, b = home(xl, z)
                pairs.append(((xl * 4 + z) * 2 + xh, (a * 4 + b) * 2 + (xh ^ flip)))
    return pairs


def y_of(sc, p):
    return lax.rem(sc[0] + OFFS[p], 4)


def load_rows(sc, pieces, dst, sem):
    rows, width = pieces[0].shape
    half = rows // 2
    copies = []
    for p in range(3):
        at = pl.ds(pl.multiple_of(y_of(sc, p) * width, width), width)
        copies.append(pltpu.make_async_copy(pieces[p], dst.at[:, at], sem.at[p]))
    at = pl.ds(pl.multiple_of(y_of(sc, 3) * width, width), width)
    copies.append(pltpu.make_async_copy(pieces[3], dst.at[pl.ds(0, half), at], sem.at[3]))
    copies.append(pltpu.make_async_copy(pieces[4], dst.at[pl.ds(half, half), at], sem.at[4]))
    return copies


def load_weights(w_ref, lo, nw, dst, sem):
    hid, cols = w_ref.shape[4], w_ref.shape[5]
    copies = []
    for w in range(nw):
        for h in range(2):
            for cb in range(8):
                at = (w * 2 + h) * hid
                copies.append(
                    pltpu.make_async_copy(
                        w_ref.at[h, cb, lo + w],
                        dst.at[:, pl.ds(at, hid), pl.ds(cb * cols, cols)],
                        sem.at[(w * 2 + h) * 8 + cb],
                    )
                )
    return copies


def expert_of(sc, block):
    return (block * BLOCK >= sc[2]).astype(jnp.int32)


def by_tile(sc, tile, work):
    low, high = expert_of(sc, 2 * tile), expert_of(sc, 2 * tile + 1)
    start = tile * TILE

    @pl.when(low == high)
    def _():
        work(pl.multiple_of(start, TILE), TILE, low)

    @pl.when(low != high)
    def _():
        work(pl.multiple_of(start, BLOCK), BLOCK, low)
        work(pl.multiple_of(start + BLOCK, BLOCK), BLOCK, high)


def pre_kernel(lo, nw, sc, x0, x1, x2, x3, x4, w_ref, own, send, xv, wv, xsem, wsem):
    copies = load_rows(sc, (x0, x1, x2, x3, x4), xv, xsem) + load_weights(w_ref, lo, nw, wv, wsem)
    for c in copies:
        c.start()
    for c in copies:
        c.wait()

    def work(start, size, expert):
        at = pl.ds(start, size)
        part = lax.dot_general(xv[at, :], wv[expert], NT, preferred_element_type=F32)
        own[at, :] = part
        send[at, :] = part.astype(BF)

    @pl.loop(0, xv.shape[0] // TILE)
    def _(t):
        by_tile(sc, t, work)


def pre_part(sc, pieces, w_all, lo, nw):
    rows, width = pieces[0].shape
    n = nw * 384
    return pl.pallas_call(
        functools.partial(pre_kernel, lo, nw),
        out_shape=(
            jax.ShapeDtypeStruct((rows, n), F32),
            jax.ShapeDtypeStruct((rows, n), BF),
        ),
        in_specs=[SM] + [ANY] * 6,
        out_specs=(VM, VM),
        scratch_shapes=[
            pltpu.VMEM((rows, 4 * width), BF),
            pltpu.VMEM((EXP, n, 4 * width), BF),
            pltpu.SemaphoreType.DMA((5,)),
            pltpu.SemaphoreType.DMA((nw * 16,)),
        ],
        compiler_params=pltpu.CompilerParams(vmem_limit_bytes=40 << 20),
        cost_estimate=pl.CostEstimate(
            flops=2 * rows * n * 4 * width, bytes_accessed=12 << 20, transcendentals=0
        ),
    )(sc, *pieces, w_all)


def back_kernel(
    sc, scores, own_gu, got_gu, own_b, got_b,
    x0, x1, x2, x3, x4, g0, g1, g2, g3, g4, w_ref,
    sgrad, dx, keep, away,
    xv, gv, wv, gu, gut, st, dxv, dgu, dd, xsem, gsem, wsem, osem, dsem,
):
    rows, wide = xv.shape
    width = wide // 4
    hid = 192
    wload = load_weights(w_ref, 0, 2, wv, wsem)
    gload = load_rows(sc, (g0, g1, g2, g3, g4), gv, gsem)
    xload = load_rows(sc, (x0, x1, x2, x3, x4), xv, xsem)
    for c in wload + gload + xload:
        c.start()

    @pl.loop(0, rows // BLOCK)
    def _(b):
        at = pl.ds(pl.multiple_of(b * BLOCK, BLOCK), BLOCK)
        live = (b * BLOCK < sc[3]).astype(F32)
        both = own_gu[at, :] + got_gu[at, :].astype(F32)
        gate, up = both[:, :384], both[:, 384:]
        back = own_b[at, :] + got_b[at, :].astype(F32)
        sig = jax.nn.sigmoid(gate)
        act = gate * sig
        hidden = (act * up).astype(BF).astype(F32)
        mine = (lax.broadcasted_iota(jnp.int32, hidden.shape, 1) >= hid).astype(jnp.int32) == sc[1]
        total = jnp.sum(jnp.where(mine, hidden * back, 0.0), axis=1, keepdims=True) * live
        sgrad[pl.ds(b, 1), :] = jnp.transpose(jnp.broadcast_to(total, (BLOCK, BLOCK)))[:1]
        scale = jnp.transpose(jnp.broadcast_to(scores[pl.ds(b, 1), :], (BLOCK, BLOCK)))[:, :1] * live
        hid_grad = scale * back
        gate_grad = (hid_grad * up * sig * (1.0 + gate * (1.0 - sig))).astype(BF)
        up_grad = (hid_grad * act).astype(BF)
        scaled = (scale * hidden).astype(BF)
        gu[at, :384] = gate_grad
        gu[at, 384:] = up_grad
        tg, tu, ts = jnp.transpose(gate_grad), jnp.transpose(up_grad), jnp.transpose(scaled)
        expert = expert_of(sc, b)
        other = 1 - expert
        gut[expert, :384, at] = tg
        gut[expert, 384:, at] = tu
        st[expert, :, at] = ts
        gut[other, :, at] = jnp.zeros((768, BLOCK), BF)
        st[other, :, at] = jnp.zeros((384, BLOCK), BF)

    for c in gload + xload:
        c.wait()

    def weight_out(src, w, e, h, slot):
        outs = []
        for rel, out in enumerate((keep, away)):
            for zz in range(2):
                for xh in range(2):
                    core = sc[4] if rel == 0 else 1 - sc[4]
                    cols = pl.ds(pl.multiple_of(((zz * 2 + xh) * 2 + core) * 256, 256), 256)
                    outs.append(
                        pltpu.make_async_copy(
                            src.at[e, pl.ds(h * hid, hid), cols],
                            out.at[h * 2 + zz, xh, w, e],
                            dsem.at[slot * 8 + rel * 4 + zz * 2 + xh],
                        )
                    )
        return outs

    outs = []
    for e in range(EXP):
        for n in range(4):
            at = pl.ds(n * width, width)
            dd[e, :, at] = jnp.dot(st[e], gv[:, at], preferred_element_type=F32).astype(BF)
        for h in range(2):
            now = weight_out(dd, 2, e, h, (2 * EXP + e) * 2 + h)
            for c in now:
                c.start()
            outs += now
    for e in range(EXP):
        for n in range(4):
            at = pl.ds(n * width, width)
            dgu[e, :, at] = jnp.dot(gut[e], xv[:, at], preferred_element_type=F32).astype(BF)
        for w in range(2):
            for h in range(2):
                now = []
                for c in weight_out(dgu.at[:, pl.ds(w * 384, 384), :], w, e, h, (w * EXP + e) * 2 + h):
                    c.start()
                    now.append(c)
                outs += now

    for c in wload:
        c.wait()

    def work(start, size, expert):
        at = pl.ds(start, size)
        dxv[at, :] = jnp.dot(gu[at, :], wv[expert], preferred_element_type=F32).astype(BF)

    @pl.loop(0, rows // TILE)
    def _(t):
        by_tile(sc, t, work)

    for p in range(4):
        at = pl.ds(pl.multiple_of(y_of(sc, p) * width, width), width)
        c = pltpu.make_async_copy(dxv.at[:, at], dx.at[p], osem.at[p])
        c.start()
        outs.append(c)
    for c in outs:
        c.wait()


def back_part(sc, scores, own_gu, got_gu, own_b, got_b, feats, grads, w_all):
    rows, width = feats[0].shape
    wide = 4 * width
    return pl.pallas_call(
        back_kernel,
        out_shape=(
            jax.ShapeDtypeStruct((rows // BLOCK, BLOCK), F32),
            jax.ShapeDtypeStruct((4, rows, width), BF),
            jax.ShapeDtypeStruct((4, 2, 3, EXP, 192, 256), BF),
            jax.ShapeDtypeStruct((4, 2, 3, EXP, 192, 256), BF),
        ),
        in_specs=[SM] + [VM] * 5 + [ANY] * 11,
        out_specs=(VM, ANY, ANY, ANY),
        scratch_shapes=[
            pltpu.VMEM((rows, wide), BF),
            pltpu.VMEM((rows, wide), BF),
            pltpu.VMEM((EXP, 768, wide), BF),
            pltpu.VMEM((rows, 768), BF),
            pltpu.VMEM((EXP, 768, rows), BF),
            pltpu.VMEM((EXP, 384, rows), BF),
            pltpu.VMEM((rows, wide), BF),
            pltpu.VMEM((EXP, 768, wide), BF),
            pltpu.VMEM((EXP, 384, wide), BF),
            pltpu.SemaphoreType.DMA((5,)),
            pltpu.SemaphoreType.DMA((5,)),
            pltpu.SemaphoreType.DMA((32,)),
            pltpu.SemaphoreType.DMA((4,)),
            pltpu.SemaphoreType.DMA((96,)),
        ],
        compiler_params=pltpu.CompilerParams(vmem_limit_bytes=56 << 20),
        cost_estimate=pl.CostEstimate(
            flops=2 * rows * 768 * wide * 4, bytes_accessed=40 << 20, transcendentals=rows * 384
        ),
    )(sc, scores, own_gu, got_gu, own_b, got_b, *feats, *grads, w_all)


def spread_rows(x):
    half = x.shape[0] // 2
    below = lax.ppermute(x, "y", ring(4, 1))
    above = lax.ppermute(x, "y", ring(4, 3))
    return (
        x,
        below,
        above,
        lax.ppermute(below[:half], "y", ring(4, 1)),
        lax.ppermute(above[half:], "y", ring(4, 3)),
    )


def on_device(features, grad_out, scores, counts, w_gate, w_up, w_down):
    rows = features.shape[0]
    xl, y, xh, core = (lax.axis_index(a) for a in ("xl", "y", "xh", "core"))
    sc = jnp.stack(
        [y, xl, counts[0, 0], counts[0, 0] + counts[0, 1], core]
    ).astype(jnp.int32)
    shard = jnp.stack([w_gate, w_up, w_down])
    shard = lax.ppermute(shard, ("xl", "z", "xh"), swap_pairs(0))
    w_all = lax.all_gather(shard, ("z", "xh", "core"), axis=0, tiled=False)
    w_all = w_all.reshape(2, 8, 3, EXP, 192, 256)
    feats = spread_rows(features)
    grads = spread_rows(grad_out)

    own_gu, send_gu = pre_part(sc, feats, w_all, 0, 2)
    got_gu = lax.ppermute(send_gu, "xl", ring(2, 1))
    own_b, send_b = pre_part(sc, grads, w_all, 2, 1)
    got_b = lax.ppermute(send_b, "xl", ring(2, 1))
    sgrad, dx, keep, away = back_part(
        sc, scores.reshape(rows // BLOCK, BLOCK), own_gu, got_gu, own_b, got_b, feats, grads, w_all
    )

    got = lax.ppermute(away, "core", ring(2, 1))
    both = (keep.astype(F32) + got.astype(F32)).astype(BF)
    part = lax.psum_scatter(both, "z", scatter_dimension=0, tiled=False)
    straight = lax.dynamic_index_in_dim(part, xh, 0, False)
    crossed = lax.dynamic_index_in_dim(part, 1 - xh, 0, False)
    straight = lax.ppermute(straight, ("xl", "z", "xh"), swap_pairs(0))
    crossed = lax.ppermute(crossed, ("xl", "z", "xh"), swap_pairs(1))
    weights = straight.astype(F32) + crossed.astype(F32)

    from_below = lax.ppermute(dx[2], "y", ring(4, 1))
    from_above = lax.ppermute(dx[1], "y", ring(4, 3))
    opposite = lax.ppermute(dx[3], "y", ring(4, 2))
    grad_features = (
        (dx[0].astype(F32) + from_below.astype(F32)) + (from_above.astype(F32) + opposite.astype(F32))
    ).astype(BF)

    total = sgrad
    total = total + lax.ppermute(total, "xl", ring(2, 1))
    total = total + lax.ppermute(total, "y", [(i, i ^ 1) for i in range(4)])
    total = total + lax.ppermute(total, "y", [(i, i ^ 2) for i in range(4)])
    return grad_features, total.reshape(rows), weights[0], weights[1], weights[2]


def solution(mesh):
    fine = Mesh(mesh.devices.reshape(2, 4, 4, 2, 2), ("xl", "y", "z", "xh", "core"))
    grp, blk = ("xl", "y"), ("z", "xh", "core")
    weight = P(None, grp, blk)
    return jax.shard_map(
        on_device,
        mesh=fine,
        in_specs=(P(blk, grp), P(blk, grp), P(blk), P(blk, None), weight, weight, weight),
        out_specs=(P(blk, grp), P(blk), weight, weight, weight),
        check_vma=False,
    )
```

time: 945 us -> 312 us (0.33)
  waiting for transfers between devices: 638 us -> 194 us
  matrix products: 136 us -> 0 us
  local copies, waits for them, and re-layouts: 86.3 us -> 16.7 us
  Pallas kernels: 0 us -> 42.4 us
  starting transfers between devices: 0.35 us -> 32.5 us
  loops' own time: 24.7 us -> 0 us
  other arithmetic: 27.5 us -> 11 us
  blocking collectives: 14.4 us -> 0 us
    all_gather x5 -> x1, waiting for transfers between devices: 338 us -> 21.9 us  [on_device(): w_all = lax.all_gather(shard, ('z', 'xh', 'core'), axis=0, tiled=False)]
    reduce_scatter x4 -> x1, waiting for transfers between devices: 295 us -> 0.01 us  [on_device(): part = lax.psum_scatter(both, 'z', scatter_dimension=0, tiled=False)]
    ppermute x0 -> x20, waiting for transfers between devices: none -> 172 us  [the longest x1 40.7 us: on_device(): total = total + lax.ppermute(total, 'y', [(i, i ^ 1) for i in range(4)])]
    dot_general x64 -> x0, matrix products: 136 us -> none  [the longest x8 20.7 us: block_work(): lax.dot_general(scaled, grad_block, tcon, preferred_element_type=jnp.floa...]
    pallas_call x0 -> x3, Pallas kernels: none -> 42.4 us  [the longest x1 26.2 us: back_part(): pl.pallas_call(back_kernel, out_shape=(jax.ShapeDtypeStruct((rows // BLOC...]
    while x176 -> x0, local copies, waits for them, and re-layouts: 42.2 us -> none
    dynamic_slice x32 -> x0, local copies, waits for them, and re-layouts: 32.9 us -> none  [the longest x16 23.5 us: add_expert(): current = lax.dynamic_index_in_dim(accum, expert_id, 0, False)]
    ppermute x0 -> x20, starting transfers between devices: none -> 32.4 us  [the longest x1 5.48 us: on_device(): shard = lax.ppermute(shard, ('xl', 'z', 'xh'), swap_pairs(0))]
  transfers between devices with their start and end apart: 9 -> 22, of which waited for: 9 -> 12; matrix products, arithmetic and copies ran while one was open for 2% -> 4% of each run, Pallas kernels for 0% -> 5%
where the time goes in v1:
time: 312 us
  waiting for transfers between devices  194 us (62%)
  Pallas kernels  42.4 us (14%)
  starting transfers between devices  32.5 us (10%)
  local copies, waits for them, and re-layouts  16.7 us (5%)
  between operations  15.5 us (5%)
  other arithmetic  11 us (4%)
    ppermute x1, waiting for transfers between devices, on_device(): total = total + lax.ppermute(total, 'y', [(i, i ^ 1) for i in range(4)])  40.7 us
    ppermute x2, waiting for transfers between devices, spread_rows(): lax.ppermute(below[:half], 'y', ring(4, 1))  37 us
    ppermute x1, waiting for transfers between devices, on_device(): got_b = lax.ppermute(send_b, 'xl', ring(2, 1))  28.2 us
    pallas_call x1, Pallas kernels, back_part(): pl.pallas_call(back_kernel, out_shape=(jax.ShapeDtypeStruct((rows // BLOC...  26.2 us
    all_gather x1, waiting for transfers between devices, on_device(): w_all = lax.all_gather(shard, ('z', 'xh', 'core'), axis=0, tiled=False)  21.9 us
    ppermute x2, waiting for transfers between devices, spread_rows(): below = lax.ppermute(x, 'y', ring(4, 1))  19.2 us
    pallas_call x2, Pallas kernels, pre_part(): pl.pallas_call(functools.partial(pre_kernel, lo, nw), out_shape=(jax.Shap...  16.2 us
    ppermute x1, waiting for transfers between devices, on_device(): crossed = lax.ppermute(crossed, ('xl', 'z', 'xh'), swap_pairs(1))  14.8 us
  transfers between devices with their start and end apart: 22, of which 12 were waited for; matrix products, arithmetic and copies ran while one was open for 4% of the time, Pallas kernels for 5%

profile of v1, /device:TPU:3, one launch (start us, length us, event | category | flops | bytes accessed | tf_op | source)
XLA Modules:
  0.0 312.0 jit_solution(13820631769532299229)
XLA Ops:
  7.2 1.2 pad_maximum_fusion
  8.4 5.5 %collective-permute-start.4 = (bf16[3,2,192,256]{3,2,1,0:T(8,128)(2,1)S(1)}, bf16[3,2,192,256]{3,2,1,0:T(8,128)(2,1)S(1)}, u32[]{:S(2)}, u32[]{:S(2)}) collective-permute-start(bf16[3,2,192,256]{3,2,1,0:T(8,128)(2,1)S(1)} %pad_maximum_fusion), channel_id=1, source_target_pairs={{0,0},{2,2},{4,4},{6,6},{8,64},{10,66},{12,68},{14,70},{64,8},{66,... | collective-permute-start | bytes 1769480 | tf_op jit(solution)/shard_map/ppermute | solution.py:296
  13.9 13.0 %collective-permute-done.4 = bf16[3,2,192,256]{3,2,1,0:T(8,128)(2,1)S(1)} collective-permute-done((bf16[3,2,192,256]{3,2,1,0:T(8,128)(2,1)S(1)}, bf16[3,2,192,256]{3,2,1,0:T(8,128)(2,1)S(1)}, u32[]{:S(2)}, u32[]{:S(2)}) %collective-permute-start.4) | collective-permute-done | bytes 589856 | tf_op jit(solution)/shard_map/ppermute | solution.py:296
  26.9 0.8 copy-done.10
  27.8 1.4 collective-permute-start
  29.2 1.5 collective-permute-start.1
  30.7 2.7 collective-permute-start.7
  33.4 19.2 %collective-permute-done.x1 = bf16[1024,512]{1,0:T(8,128)(2,1)S(1)} collective-permute-done((bf16[1024,512]{1,0:T(8,128)(2,1)}, bf16[1024,512]{1,0:T(8,128)(2,1)S(1)}, u32[]{:S(2)}, u32[]{:S(2)}) %collective-permute-start) | collective-permute-done | bytes 1048608 | tf_op jit(solution)/shard_map/ppermute | solution.py:278
  52.5 0.9 slice.53
  53.5 0.9 slice.54
  54.4 2.6 collective-permute-start.3
  57.1 0.6 fusion.2
  58.9 0.7 stack.31.sc
  59.7 26.7 %collective-permute-done.2.x3 = bf16[512,512]{1,0:T(8,128)(2,1)} collective-permute-done((bf16[512,512]{1,0:T(8,128)(2,1)}, bf16[512,512]{1,0:T(8,128)(2,1)}, u32[]{:S(2)}, u32[]{:S(2)}) %collective-permute-start.2) | collective-permute-done | bytes 524320 | tf_op jit(solution)/shard_map/ppermute | solution.py:284
  86.4 21.9 %all-gather.3.cloned.1.call-done = bf16[48,2,192,256]{3,2,1,0:T(8,128)(2,1)} async-done(((bf16[3,2,192,256]{3,2,1,0:T(8,128)(2,1)}), bf16[48,2,192,256]{3,2,1,0:T(8,128)(2,1)}) %all-gather.3.cloned.1.call-update) | async-done | bytes 9437200 | tf_op jit(solution)/shard_map/all_gather | solution.py:297
  108.3 1.2 copy-done.3
  109.5 9.7 %shard_map.110 = (f32[1024,768]{1,0:T(8,128)S(1)}, bf16[1024,768]{1,0:T(8,128)(2,1)S(1)}) custom-call(s32[5]{0:T(128)S(1)} %stack.31.sc, bf16[1024,512]{1,0:T(8,128)(2,1)S(1)} %copy-done.3, bf16[1024,512]{1,0:T(8,128)(2,1)S(1)} %collective-permute-done.x1, bf16[1024,512]{1,0:T(8,128)(2,1)S(1)} %collective-permute-done.1.x2, ...), custom_call_target="tpu_custom_call" | custom-call | flops 3221225472 | bytes 12582912 | tf_op jit(solution)/shard_map/pallas_call | solution.py:114
  119.2 1.7 copy-done.8
  120.9 1.2 collective-permute-start.5
  122.1 1.3 collective-permute-start.8
  123.4 1.1 slice.56
  124.5 1.6 collective-permute-start.9
  126.1 10.3 %collective-permute-done.8.x3.g3 = bf16[512,512]{1,0:T(8,128)(2,1)S(1)} collective-permute-done((bf16[512,512]{1,0:T(8,128)(2,1)S(1)}, bf16[512,512]{1,0:T(8,128)(2,1)S(1)}, u32[]{:S(2)}, u32[]{:S(2)}) %collective-permute-start.8) | collective-permute-done | bytes 524320 | tf_op jit(solution)/shard_map/ppermute | solution.py:284
  136.4 0.8 collective-permute-done.9.x4.g4
  137.2 6.5 %shard_map.111 = (f32[1024,384]{1,0:T(8,128)S(1)}, bf16[1024,384]{1,0:T(8,128)(2,1)S(1)}) custom-call(s32[5]{0:T(128)S(1)} %stack.31.sc, bf16[1024,512]{1,0:T(8,128)(2,1)S(1)} %copy-done.4, bf16[1024,512]{1,0:T(8,128)(2,1)S(1)} %collective-permute-done.6.x1.g1, bf16[1024,512]{1,0:T(8,128)(2,1)} %collective-permute-done.7.x2.g2, ...), custom_call_target="tpu_custom_call" | custom-call | flops 1610612736 | bytes 12582912 | tf_op jit(solution)/shard_map/pallas_call | solution.py:114
  143.8 1.2 copy-done.9
  145.3 28.2 %collective-permute-done.10.got_b = bf16[1024,384]{1,0:T(8,128)(2,1)S(1)} collective-permute-done((bf16[1024,384]{1,0:T(8,128)(2,1)S(1)}, bf16[1024,384]{1,0:T(8,128)(2,1)S(1)}, u32[]{:S(2)}, u32[]{:S(2)}) %collective-permute-start.10) | collective-permute-done | bytes 786464 | tf_op jit(solution)/shard_map/ppermute | solution.py:305
  173.5 0.9 copy-done.14
  174.9 26.2 %shard_map.112 = (f32[8,128]{1,0:T(8,128)}, bf16[4,1024,512]{2,1,0:T(8,128)(2,1)}, bf16[4,2,3,2,192,256]{5,4,3,2,1,0:T(8,128)(2,1)}, bf16[4,2,3,2,192,256]{5,4,3,2,1,0:T(8,128)(2,1)}) custom-call(s32[5]{0:T(128)} %copy-done.7, f32[8,128]{1,0:T(8,128)} %bitcast.37, f32[1024,768]{1,0:T(8,128)} %copy-done.8, bf16[1024,768]{1,0:T(8,128)(2,1)} %copy-done.13, ...), custom_call_target="tpu_custom_call" | custom-call | flops 12884901888 | bytes 41943040 | tf_op jit(solution)/shard_map/pallas_call | solution.py:243
  201.1 1.2 collective-permute-start.17
  202.3 7.7 %collective-permute-done.17 = bf16[4,2,3,2,192,256]{5,4,3,2,1,0:T(8,128)(2,1)S(1)} collective-permute-done((bf16[4,2,3,2,192,256]{5,4,3,2,1,0:T(8,128)(2,1)}, bf16[4,2,3,2,192,256]{5,4,3,2,1,0:T(8,128)(2,1)S(1)}, u32[]{:S(2)}, u32[]{:S(2)}) %collective-permute-start.17) | collective-permute-done | bytes 4718624 | tf_op jit(solution)/shard_map/ppermute | solution.py:310
  210.0 6.3 %add_convert_fusion = bf16[4,2,3,2,192,256]{5,4,3,2,1,0:T(8,128)(2,1)} fusion(bf16[4,2,3,2,192,256]{5,4,3,2,1,0:T(8,128)(2,1)S(1)} %collective-permute-done.17, bf16[4,2,3,2,192,256]{5,4,3,2,1,0:T(8,128)(2,1)} %get-tuple-element.19), kind=kLoop, calls=%fused_computation | loop fusion | flops 9437184 | bytes 14155776 | tf_op jit(solution)/shard_map/convert_element_type | solution.py:311
  216.4 3.7 %slice_bitcast_fusion.2 = (bf16[1024,512]{1,0:T(8,128)(2,1)}, bf16[1024,512]{1,0:T(8,128)(2,1)}, bf16[1024,512]{1,0:T(8,128)(2,1)}) fusion(bf16[4,1024,512]{2,1,0:T(8,128)(2,1)} %get-tuple-element.17), kind=kLoop, calls=%fused_computation.7 | loop fusion | bytes 6291456 | tf_op jit(solution)/shard_map/squeeze | solution.py:319
  220.0 1.2 collective-permute-start.11
  221.2 1.5 collective-permute-start.12
  222.7 1.5 collective-permute-start.13
  224.2 1.2 collective-permute-start.14
  225.4 1.7 collective-permute-done.14
  227.4 40.7 %collective-permute-done.15 = f32[8,128]{1,0:T(8,128)S(1)} collective-permute-done((f32[8,128]{1,0:T(8,128)S(1)}, f32[8,128]{1,0:T(8,128)S(1)}, u32[]{:S(2)}, u32[]{:S(2)}) %collective-permute-start.15) | collective-permute-done | bytes 4128 | tf_op jit(solution)/shard_map/ppermute | solution.py:328
  268.1 2.4 collective-permute-start.16
  270.5 1.3 dynamic-slice_bitcast_fusion.1
  271.8 2.7 collective-permute-start.18
  274.6 2.4 collective-permute-start.19
  277.0 0.6 add_bitcast_fusion
  277.6 2.8 fusion.1
  280.4 8.8 %collective-permute-done.18 = bf16[3,2,192,256]{3,2,1,0:T(8,128)(2,1)S(1)} collective-permute-done((bf16[3,2,192,256]{3,2,1,0:T(8,128)(2,1)S(1)}, bf16[3,2,192,256]{3,2,1,0:T(8,128)(2,1)S(1)}, u32[]{:S(2)}, u32[]{:S(2)}) %collective-permute-start.18) | collective-permute-done | bytes 589856 | tf_op jit(solution)/shard_map/ppermute | solution.py:315
  289.2 14.8 %collective-permute-done.19 = bf16[3,2,192,256]{3,2,1,0:T(8,128)(2,1)S(1)} collective-permute-done((bf16[3,2,192,256]{3,2,1,0:T(8,128)(2,1)S(1)}, bf16[3,2,192,256]{3,2,1,0:T(8,128)(2,1)S(1)}, u32[]{:S(2)}, u32[]{:S(2)}) %collective-permute-start.19) | collective-permute-done | bytes 589856 | tf_op jit(solution)/shard_map/ppermute | solution.py:316
  304.1 1.0 slice_bitcast_fusion.3
  (47 shorter events, 1.5 us)
Async XLA Ops:
  7.2 49.9 %copy-start.12 = (s32[1,2]{1,0:T(1,128)S(1)}, s32[1,2]{1,0:T(1,128)}, u32[]{:S(2)}) copy-start(s32[1,2]{1,0:T(1,128)} %param.10) | copy-start | bytes 28
  7.2 101.1 %all-gather.3.cloned.1.call-start = ((), (), s32[]{:S(2)}) async-start(), calls=%async_computation.2 | async-start | bytes 10027008 | tf_op jit(solution)/shard_map/all_gather | solution.py:297
  8.4 18.5 %collective-permute-start.4 = (bf16[3,2,192,256]{3,2,1,0:T(8,128)(2,1)S(1)}, bf16[3,2,192,256]{3,2,1,0:T(8,128)(2,1)S(1)}, u32[]{:S(2)}, u32[]{:S(2)}) collective-permute-start(bf16[3,2,192,256]{3,2,1,0:T(8,128)(2,1)S(1)} %pad_maximum_fusion), channel_id=1, source_target_pairs={{0,0},{2,2},{4,4},{6,6},{8,64},{10,66},{12,68},{14,70},{64,8},{66,... | collective-permute-start | bytes 1769480 | tf_op jit(solution)/shard_map/ppermute | solution.py:296
  26.9 0.8 copy-start.10
  27.8 242.7 %reduce-scatter.2.cloned.1.call-start = ((), (), s32[]{:S(2)}) async-start(), calls=%async_computation.1 | async-start | bytes 5898240 | tf_op jit(solution)/shard_map/reduce_scatter | solution.py:312
  27.8 24.7 %collective-permute-start = (bf16[1024,512]{1,0:T(8,128)(2,1)}, bf16[1024,512]{1,0:T(8,128)(2,1)S(1)}, u32[]{:S(2)}, u32[]{:S(2)}) collective-permute-start(bf16[1024,512]{1,0:T(8,128)(2,1)} %x0.5), channel_id=1, source_target_pairs={{0,16},{16,32},{32,48},{48,0},{1,17},{17,33},{33,49},{49,1},{2,18}... | collective-permute-start | bytes 3145736 | tf_op jit(solution)/shard_map/ppermute | solution.py:278
  29.2 24.3 %collective-permute-start.1 = (bf16[1024,512]{1,0:T(8,128)(2,1)}, bf16[1024,512]{1,0:T(8,128)(2,1)S(1)}, u32[]{:S(2)}, u32[]{:S(2)}) collective-permute-start(bf16[1024,512]{1,0:T(8,128)(2,1)} %x0.5), channel_id=1, source_target_pairs={{0,48},{16,0},{32,16},{48,32},{1,49},{17,1},{33,17},{49,33},{2,50}... | collective-permute-start | bytes 3145736 | tf_op jit(solution)/shard_map/ppermute | solution.py:279
  30.7 91.4 %collective-permute-start.6 = (bf16[1024,512]{1,0:T(8,128)(2,1)}, bf16[1024,512]{1,0:T(8,128)(2,1)S(1)}, u32[]{:S(2)}, u32[]{:S(2)}) collective-permute-start(bf16[1024,512]{1,0:T(8,128)(2,1)} %g0.1), channel_id=1, source_target_pairs={{0,16},{16,32},{32,48},{48,0},{1,17},{17,33},{33,49},{49,1},{2,18}... | collective-permute-start | bytes 3145736 | tf_op jit(solution)/shard_map/ppermute | solution.py:278
  30.7 92.7 %collective-permute-start.7 = (bf16[1024,512]{1,0:T(8,128)(2,1)}, bf16[1024,512]{1,0:T(8,128)(2,1)}, u32[]{:S(2)}, u32[]{:S(2)}) collective-permute-start(bf16[1024,512]{1,0:T(8,128)(2,1)} %g0.1), channel_id=1, source_target_pairs={{0,48},{16,0},{32,16},{48,32},{1,49},{17,1},{33,17},{49,33},{2,50}... | collective-permute-start | bytes 3145736 | tf_op jit(solution)/shard_map/ppermute | solution.py:279
  52.5 66.6 %copy-start = (bf16[1024,512]{1,0:T(8,128)(2,1)}, bf16[1024,512]{1,0:T(8,128)(2,1)S(1)}, u32[]{:S(2)}) copy-start(bf16[1024,512]{1,0:T(8,128)(2,1)S(1)} %collective-permute-done.x1) | copy-start | bytes 3145732
  53.5 32.9 %collective-permute-start.2 = (bf16[512,512]{1,0:T(8,128)(2,1)}, bf16[512,512]{1,0:T(8,128)(2,1)}, u32[]{:S(2)}, u32[]{:S(2)}) collective-permute-start(bf16[512,512]{1,0:T(8,128)(2,1)} %slice.53), channel_id=1, source_target_pairs={{0,16},{16,32},{32,48},{48,0},{1,17},{17,33},{33,49},{49,1},{2,18}... | collective-permute-start | bytes 1572872 | tf_op jit(solution)/shard_map/ppermute | solution.py:284
  53.5 65.7 %copy-start.1 = (bf16[1024,512]{1,0:T(8,128)(2,1)}, bf16[1024,512]{1,0:T(8,128)(2,1)S(1)}, u32[]{:S(2)}) copy-start(bf16[1024,512]{1,0:T(8,128)(2,1)S(1)} %collective-permute-done.1.x2) | copy-start | bytes 3145732
  54.4 31.9 %collective-permute-start.3 = (bf16[512,512]{1,0:T(8,128)(2,1)}, bf16[512,512]{1,0:T(8,128)(2,1)}, u32[]{:S(2)}, u32[]{:S(2)}) collective-permute-start(bf16[512,512]{1,0:T(8,128)(2,1)} %slice.54), channel_id=1, source_target_pairs={{0,48},{16,0},{32,16},{48,32},{1,49},{17,1},{33,17},{49,33},{2,50}... | collective-permute-start | bytes 1572872 | tf_op jit(solution)/shard_map/ppermute | solution.py:285
  59.7 77.5 %copy-start.7 = (s32[5]{0:T(128)}, s32[5]{0:T(128)S(1)}, u32[]{:S(2)}) copy-start(s32[5]{0:T(128)S(1)} %stack.31.sc) | copy-start | bytes 64
  108.3 1.2 copy-start.3
  119.2 1.7 copy-start.8
  120.9 16.3 %copy-start.4 = (bf16[1024,512]{1,0:T(8,128)(2,1)S(1)}, bf16[1024,512]{1,0:T(8,128)(2,1)}, u32[]{:S(2)}) copy-start(bf16[1024,512]{1,0:T(8,128)(2,1)} %g0.1) | copy-start | bytes 3145732
  120.9 52.6 %collective-permute-start.5 = (bf16[1024,768]{1,0:T(8,128)(2,1)S(1)}, bf16[1024,768]{1,0:T(8,128)(2,1)S(1)}, u32[]{:S(2)}, u32[]{:S(2)}) collective-permute-start(bf16[1024,768]{1,0:T(8,128)(2,1)S(1)} %get-tuple-element.14), channel_id=1, source_target_pairs={{0,64},{64,0},{1,65},{65,1},{2,66},{66,2},{3,67},{67,3},{4,68},{68... | collective-permute-start | bytes 4718600 | tf_op jit(solution)/shard_map/ppermute | solution.py:303
  122.1 21.6 %copy-start.2 = (bf16[1024,512]{1,0:T(8,128)(2,1)}, bf16[1024,512]{1,0:T(8,128)(2,1)S(1)}, u32[]{:S(2)}) copy-start(bf16[1024,512]{1,0:T(8,128)(2,1)S(1)} %collective-permute-done.6.x1.g1) | copy-start | bytes 3145732
  122.1 14.2 %collective-permute-start.8 = (bf16[512,512]{1,0:T(8,128)(2,1)S(1)}, bf16[512,512]{1,0:T(8,128)(2,1)S(1)}, u32[]{:S(2)}, u32[]{:S(2)}) collective-permute-start(bf16[512,512]{1,0:T(8,128)(2,1)S(1)} %slice.55), channel_id=1, source_target_pairs={{0,16},{16,32},{32,48},{48,0},{1,17},{17,33},{33,49},{49,1},{2,18}... | collective-permute-start | bytes 1572872 | tf_op jit(solution)/shard_map/ppermute | solution.py:284
  124.5 12.7 %collective-permute-start.9 = (bf16[512,512]{1,0:T(8,128)(2,1)S(1)}, bf16[512,512]{1,0:T(8,128)(2,1)S(1)}, u32[]{:S(2)}, u32[]{:S(2)}) collective-permute-start(bf16[512,512]{1,0:T(8,128)(2,1)S(1)} %slice.56), channel_id=1, source_target_pairs={{0,48},{16,0},{32,16},{48,32},{1,49},{17,1},{33,17},{49,33},{2,50}... | collective-permute-start | bytes 1572872 | tf_op jit(solution)/shard_map/ppermute | solution.py:285
  136.4 7.4 %copy-start.5 = (bf16[512,512]{1,0:T(8,128)(2,1)}, bf16[512,512]{1,0:T(8,128)(2,1)S(1)}, u32[]{:S(2)}) copy-start(bf16[512,512]{1,0:T(8,128)(2,1)S(1)} %collective-permute-done.8.x3.g3) | copy-start | bytes 1572868
  137.2 6.5 %copy-start.6 = (bf16[512,512]{1,0:T(8,128)(2,1)}, bf16[512,512]{1,0:T(8,128)(2,1)S(1)}, u32[]{:S(2)}) copy-start(bf16[512,512]{1,0:T(8,128)(2,1)S(1)} %collective-permute-done.9.x4.g4) | copy-start | bytes 1572868
  143.8 1.2 copy-start.9
  145.0 28.5 %collective-permute-start.10 = (bf16[1024,384]{1,0:T(8,128)(2,1)S(1)}, bf16[1024,384]{1,0:T(8,128)(2,1)S(1)}, u32[]{:S(2)}, u32[]{:S(2)}) collective-permute-start(bf16[1024,384]{1,0:T(8,128)(2,1)S(1)} %get-tuple-element.16), channel_id=1, source_target_pairs={{0,64},{64,0},{1,65},{65,1},{2,66},{66,2},{3,67},{67,3},{4,68},{68... | collective-permute-start | bytes 2359304 | tf_op jit(solution)/shard_map/ppermute | solution.py:305
  173.5 0.9 copy-start.14
  173.5 1.4 copy-start.13
  201.1 8.9 %collective-permute-start.17 = (bf16[4,2,3,2,192,256]{5,4,3,2,1,0:T(8,128)(2,1)}, bf16[4,2,3,2,192,256]{5,4,3,2,1,0:T(8,128)(2,1)S(1)}, u32[]{:S(2)}, u32[]{:S(2)}) collective-permute-start(bf16[4,2,3,2,192,256]{5,4,3,2,1,0:T(8,128)(2,1)} %get-tuple-element.20), channel_id=1, source_target_pairs={{0,1},{1,0},{2,3},{3,2},{4,5},{5,4},{6,7},{7,6},{8,9},{9,8},{10,11... | collective-permute-start | bytes 14155784 | tf_op jit(solution)/shard_map/ppermute | solution.py:310
  216.3 7.9 %copy-start.11 = (f32[8,128]{1,0:T(8,128)S(1)}, f32[8,128]{1,0:T(8,128)}, u32[]{:S(2)}) copy-start(f32[8,128]{1,0:T(8,128)} %get-tuple-element.18) | copy-start | bytes 12292
  220.0 57.6 %collective-permute-start.11 = (bf16[1024,512]{1,0:T(8,128)(2,1)}, bf16[1024,512]{1,0:T(8,128)(2,1)S(1)}, u32[]{:S(2)}, u32[]{:S(2)}) collective-permute-start(bf16[1024,512]{1,0:T(8,128)(2,1)} %get-tuple-element.21), channel_id=1, source_target_pairs={{0,16},{16,32},{32,48},{48,0},{1,17},{17,33},{33,49},{49,1},{2,18}... | collective-permute-start | bytes 3145736 | tf_op jit(solution)/shard_map/ppermute | solution.py:319
  221.2 56.4 %collective-permute-start.12 = (bf16[1024,512]{1,0:T(8,128)(2,1)}, bf16[1024,512]{1,0:T(8,128)(2,1)S(1)}, u32[]{:S(2)}, u32[]{:S(2)}) collective-permute-start(bf16[1024,512]{1,0:T(8,128)(2,1)} %get-tuple-element.23), channel_id=1, source_target_pairs={{0,48},{16,0},{32,16},{48,32},{1,49},{17,1},{33,17},{49,33},{2,50}... | collective-permute-start | bytes 3145736 | tf_op jit(solution)/shard_map/ppermute | solution.py:320
  222.7 54.9 %collective-permute-start.13 = (bf16[1024,512]{1,0:T(8,128)(2,1)}, bf16[1024,512]{1,0:T(8,128)(2,1)S(1)}, u32[]{:S(2)}, u32[]{:S(2)}) collective-permute-start(bf16[1024,512]{1,0:T(8,128)(2,1)} %get-tuple-element.22), channel_id=1, source_target_pairs={{0,32},{16,48},{32,0},{48,16},{1,33},{17,49},{33,1},{49,17},{2,34}... | collective-permute-start | bytes 3145736 | tf_op jit(solution)/shard_map/ppermute | solution.py:321
  224.2 2.9 collective-permute-start.14
  227.1 41.0 %collective-permute-start.15 = (f32[8,128]{1,0:T(8,128)S(1)}, f32[8,128]{1,0:T(8,128)S(1)}, u32[]{:S(2)}, u32[]{:S(2)}) collective-permute-start(f32[8,128]{1,0:T(8,128)S(1)} %add.42), channel_id=1, source_target_pairs={{0,16},{16,0},{32,48},{48,32},{1,17},{17,1},{33,49},{49,33},{2,18}... | collective-permute-start | bytes 12296 | tf_op jit(solution)/shard_map/ppermute | solution.py:328
  268.1 6.4 %collective-permute-start.16 = (f32[8,128]{1,0:T(8,128)S(1)}, f32[8,128]{1,0:T(8,128)S(1)}, u32[]{:S(2)}, u32[]{:S(2)}) collective-permute-start(f32[8,128]{1,0:T(8,128)S(1)} %add.43), channel_id=1, source_target_pairs={{0,32},{16,48},{32,0},{48,16},{1,33},{17,49},{33,1},{49,17},{2,34}... | collective-permute-start | bytes 12296 | tf_op jit(solution)/shard_map/ppermute | solution.py:329
  271.8 17.4 %collective-permute-start.18 = (bf16[3,2,192,256]{3,2,1,0:T(8,128)(2,1)S(1)}, bf16[3,2,192,256]{3,2,1,0:T(8,128)(2,1)S(1)}, u32[]{:S(2)}, u32[]{:S(2)}) collective-permute-start(bf16[3,2,192,256]{3,2,1,0:T(8,128)(2,1)S(1)} %get-tuple-element.27), channel_id=1, source_target_pairs={{0,0},{2,2},{4,4},{6,6},{8,64},{10,66},{12,68},{14,70},{64,8},{66,... | collective-permute-start | bytes 1769480 | tf_op jit(solution)/shard_map/ppermute | solution.py:315
  274.6 29.4 %collective-permute-start.19 = (bf16[3,2,192,256]{3,2,1,0:T(8,128)(2,1)S(1)}, bf16[3,2,192,256]{3,2,1,0:T(8,128)(2,1)S(1)}, u32[]{:S(2)}, u32[]{:S(2)}) collective-permute-start(bf16[3,2,192,256]{3,2,1,0:T(8,128)(2,1)S(1)} %get-tuple-element.28), channel_id=1, source_target_pairs={{0,2},{2,0},{4,6},{6,4},{8,66},{10,64},{12,70},{14,68},{64,10},{66... | collective-permute-start | bytes 1769480 | tf_op jit(solution)/shard_map/ppermute | solution.py:316
Sparse Core Ops, SparseCore 0:
  27.9 80.3 all-gather.2
  216.5 49.0 reduce-scatter.1

commit v2 on v1

v2 whole, which is shorter than its diff:
```python
import functools

import jax
import jax.numpy as jnp
from jax import lax
from jax.experimental import pallas as pl
from jax.experimental.pallas import tpu as pltpu
from jax.sharding import Mesh
from jax.sharding import PartitionSpec as P

EXP = 2
BLOCK = 128
TILE = 256
HID = 192
COLS = 256
BF = jnp.bfloat16
F32 = jnp.float32
NT = (((1,), (1,)), ((), ()))
OFFS = (0, 3, 1, 2)
SLOTS = ((0, 0), (0, 1), (3, 0), (3, 1), (1, 0), (1, 1), (2, 0), (2, 1))
ANY = pl.BlockSpec(memory_space=pl.ANY)
VM = pl.BlockSpec(memory_space=pltpu.VMEM)
SM = pl.BlockSpec(memory_space=pltpu.SMEM)
Y, XL, FIRST, LIVE, CORE, Z, XH = range(7)


def ring(n, k):
    return [(i, (i + k) % n) for i in range(n)]


def home(xl, z):
    return (xl, z) if z // 2 == xl else (1 - xl, (z + 2) % 4)


def swap_pairs(flip):
    pairs = []
    for xl in range(2):
        for z in range(4):
            for xh in range(2):
                a, b = home(xl, z)
                pairs.append(((xl * 4 + z) * 2 + xh, (a * 4 + b) * 2 + (xh ^ flip)))
    return pairs


def after(x, *others):
    return lax.optimization_barrier((x, *others))[0]


def aligned(i, unit):
    return pl.ds(pl.multiple_of(i * unit, unit), unit)


def y_of(sc, p):
    return lax.rem(sc[Y] + OFFS[p], 4)


def load_rows(sc, pieces, dst, sem):
    rows, width = pieces[0].shape
    half = rows // 2
    copies = []
    for p in range(3):
        at = aligned(y_of(sc, p), width)
        copies.append(pltpu.make_async_copy(pieces[p], dst.at[:, at], sem.at[p]))
    at = aligned(y_of(sc, 3), width)
    copies.append(pltpu.make_async_copy(pieces[3], dst.at[pl.ds(0, half), at], sem.at[3]))
    copies.append(pltpu.make_async_copy(pieces[4], dst.at[pl.ds(half, half), at], sem.at[4]))
    return copies


def load_weight(sc, pair, row, dst, sem, at_sem):
    copies = []
    for c, ref in enumerate(pair):
        core = sc[CORE] if c == 0 else 1 - sc[CORE]
        for i, (step, flip) in enumerate(SLOTS):
            slot = lax.rem(sc[Z] + step, 4)
            xh = 1 - sc[XH] if flip else sc[XH]
            cb = lax.rem(slot, 2) * 4 + xh * 2 + core
            rows = pl.ds(pl.multiple_of(row + lax.div(slot, 2) * HID, 64), HID)
            copies.append(
                pltpu.make_async_copy(
                    ref.at[i], dst.at[:, rows, aligned(cb, COLS)], sem.at[at_sem + c * 8 + i]
                )
            )
    return copies


def expert_of(sc, block):
    return (block * BLOCK >= sc[FIRST]).astype(jnp.int32)


def by_tile(sc, tile, work):
    low, high = expert_of(sc, 2 * tile), expert_of(sc, 2 * tile + 1)
    start = tile * TILE

    @pl.when(low == high)
    def _():
        work(pl.multiple_of(start, TILE), TILE, low)

    @pl.when(low != high)
    def _():
        work(pl.multiple_of(start, BLOCK), BLOCK, low)
        work(pl.multiple_of(start + BLOCK, BLOCK), BLOCK, high)


def start_all(copies):
    for c in copies:
        c.start()
    return copies


def wait_all(copies):
    for c in copies:
        c.wait()


def pre_kernel(sc, x0, x1, x2, x3, x4, w0, w1, own, send, xv, wv, xsem, wsem):
    wait_all(
        start_all(
            load_weight(sc, (w0, w1), 0, wv, wsem, 0) + load_rows(sc, (x0, x1, x2, x3, x4), xv, xsem)
        )
    )

    def work(start, size, expert):
        at = pl.ds(start, size)
        part = lax.dot_general(xv[at, :], wv[expert], NT, preferred_element_type=F32)
        own[at, :] = part
        send[at, :] = part.astype(BF)

    @pl.loop(0, xv.shape[0] // TILE)
    def _(t):
        by_tile(sc, t, work)


def pre_part(sc, pieces, weight):
    rows, width = pieces[0].shape
    wide, n = 4 * width, 2 * HID
    return pl.pallas_call(
        pre_kernel,
        out_shape=(jax.ShapeDtypeStruct((rows, n), F32), jax.ShapeDtypeStruct((rows, n), BF)),
        in_specs=[SM] + [ANY] * 7,
        out_specs=(VM, VM),
        scratch_shapes=[
            pltpu.VMEM((rows, wide), BF),
            pltpu.VMEM((EXP, n, wide), BF),
            pltpu.SemaphoreType.DMA((5,)),
            pltpu.SemaphoreType.DMA((16,)),
        ],
        compiler_params=pltpu.CompilerParams(vmem_limit_bytes=32 << 20),
        cost_estimate=pl.CostEstimate(
            flops=4 * rows * n * wide, bytes_accessed=10 << 20, transcendentals=0
        ),
    )(sc, *pieces, *weight)


def column(row):
    return jnp.transpose(jnp.broadcast_to(row, (BLOCK, BLOCK)))[:, :1]


def transposed_into(dst, sc, b, at, rows, value):
    expert = expert_of(sc, b)
    dst[expert, rows, at] = jnp.transpose(value)
    dst[1 - expert, rows, at] = jnp.zeros((rows.stop - rows.start, BLOCK), value.dtype)


def weight_out(sc, src, row, e, keep, away, w, sem):
    outs = []
    for rel, out in enumerate((keep, away)):
        core = sc[CORE] if rel == 0 else 1 - sc[CORE]
        for h in range(2):
            for zz in range(2):
                for xh in range(2):
                    i = (((w * EXP + e) * 2 + rel) * 2 + h) * 4 + zz * 2 + xh
                    outs.append(
                        pltpu.make_async_copy(
                            src.at[e, pl.ds(row + h * HID, HID), aligned((zz * 2 + xh) * 2 + core, COLS)],
                            out.at[h * 2 + zz, xh, w, e],
                            sem.at[i],
                        )
                    )
    return outs


def down_kernel(
    sc, scores, own_g, got_g, own_u, got_u, g0, g1, g2, g3, g4, keep, away, gv, st, dd, gsem, dsem
):
    rows, width = g0.shape
    gload = start_all(load_rows(sc, (g0, g1, g2, g3, g4), gv, gsem))

    @pl.loop(0, rows // BLOCK)
    def _(b):
        at = aligned(b, BLOCK)
        live = (b * BLOCK < sc[LIVE]).astype(F32)
        gate = own_g[at, :] + got_g[at, :].astype(F32)
        up = own_u[at, :] + got_u[at, :].astype(F32)
        hidden = (gate * jax.nn.sigmoid(gate) * up).astype(BF).astype(F32)
        scaled = (column(scores[pl.ds(b, 1), :]) * live * hidden).astype(BF)
        transposed_into(st, sc, b, at, slice(0, 2 * HID), scaled)

    wait_all(gload)
    outs = []
    for e in range(EXP):
        for n in range(4):
            at = pl.ds(n * width, width)
            dd[e, :, at] = jnp.dot(st[e], gv[:, at], preferred_element_type=F32).astype(BF)
        outs += start_all(weight_out(sc, dd, 0, e, keep, away, 0, dsem))
    wait_all(outs)


def down_part(sc, scores, own_g, got_g, own_u, got_u, grads):
    rows, width = grads[0].shape
    out = jax.ShapeDtypeStruct((4, 2, 1, EXP, HID, COLS), BF)
    return pl.pallas_call(
        down_kernel,
        out_shape=(out, out),
        in_specs=[SM] + [VM] * 5 + [ANY] * 5,
        out_specs=(ANY, ANY),
        scratch_shapes=[
            pltpu.VMEM((rows, 4 * width), BF),
            pltpu.VMEM((EXP, 2 * HID, rows), BF),
            pltpu.VMEM((EXP, 2 * HID, 4 * width), BF),
            pltpu.SemaphoreType.DMA((5,)),
            pltpu.SemaphoreType.DMA((32,)),
        ],
        compiler_params=pltpu.CompilerParams(vmem_limit_bytes=40 << 20),
        cost_estimate=pl.CostEstimate(
            flops=8 * rows * HID * 4 * width, bytes_accessed=14 << 20, transcendentals=rows * 384
        ),
    )(sc, scores, own_g, got_g, own_u, got_u, *grads)


def gate_up_kernel(
    sc, scores, own_g, got_g, own_u, got_u, own_b, got_b, x0, x1, x2, x3, x4,
    sgrad, gu, keep, away, xv, gut, dgu, xsem, dsem,
):
    rows, width = x0.shape
    n = 2 * HID
    xload = start_all(load_rows(sc, (x0, x1, x2, x3, x4), xv, xsem))

    @pl.loop(0, rows // BLOCK)
    def _(b):
        at = aligned(b, BLOCK)
        live = (b * BLOCK < sc[LIVE]).astype(F32)
        gate = own_g[at, :] + got_g[at, :].astype(F32)
        up = own_u[at, :] + got_u[at, :].astype(F32)
        back = own_b[at, :] + got_b[at, :].astype(F32)
        sig = jax.nn.sigmoid(gate)
        act = gate * sig
        hidden = (act * up).astype(BF).astype(F32)
        mine = (lax.broadcasted_iota(jnp.int32, hidden.shape, 1) >= HID).astype(jnp.int32) == sc[XL]
        total = jnp.sum(jnp.where(mine, hidden * back, 0.0), axis=1, keepdims=True) * live
        sgrad[pl.ds(b, 1), :] = jnp.transpose(jnp.broadcast_to(total, (BLOCK, BLOCK)))[:1]
        hid_grad = column(scores[pl.ds(b, 1), :]) * live * back
        gate_grad = (hid_grad * up * sig * (1.0 + gate * (1.0 - sig))).astype(BF)
        up_grad = (hid_grad * act).astype(BF)
        gu[at, :n] = gate_grad
        gu[at, n:] = up_grad
        transposed_into(gut, sc, b, at, slice(0, n), gate_grad)
        transposed_into(gut, sc, b, at, slice(n, 2 * n), up_grad)

    wait_all(xload)
    outs = []
    for e in range(EXP):
        for k in range(4):
            at = pl.ds(k * width, width)
            dgu[e, :, at] = jnp.dot(gut[e], xv[:, at], preferred_element_type=F32).astype(BF)
        for w in range(2):
            outs += start_all(weight_out(sc, dgu, w * n, e, keep, away, w, dsem))
    wait_all(outs)


def gate_up_part(sc, scores, own_g, got_g, own_u, got_u, own_b, got_b, feats):
    rows, width = feats[0].shape
    out = jax.ShapeDtypeStruct((4, 2, 2, EXP, HID, COLS), BF)
    return pl.pallas_call(
        gate_up_kernel,
        out_shape=(
            jax.ShapeDtypeStruct((rows // BLOCK, BLOCK), F32),
            jax.ShapeDtypeStruct((rows, 4 * HID), BF),
            out,
            out,
        ),
        in_specs=[SM] + [VM] * 7 + [ANY] * 5,
        out_specs=(VM, VM, ANY, ANY),
        scratch_shapes=[
            pltpu.VMEM((rows, 4 * width), BF),
            pltpu.VMEM((EXP, 4 * HID, rows), BF),
            pltpu.VMEM((EXP, 4 * HID, 4 * width), BF),
            pltpu.SemaphoreType.DMA((5,)),
            pltpu.SemaphoreType.DMA((64,)),
        ],
        compiler_params=pltpu.CompilerParams(vmem_limit_bytes=48 << 20),
        cost_estimate=pl.CostEstimate(
            flops=16 * rows * HID * 4 * width, bytes_accessed=20 << 20, transcendentals=rows * 384
        ),
    )(sc, scores, own_g, got_g, own_u, got_u, own_b, got_b, *feats)


def rows_kernel(sc, gu, g0, g1, u0, u1, dx, wv, dxv, wsem, osem):
    rows, wide = dxv.shape
    width = wide // 4
    wait_all(
        start_all(
            load_weight(sc, (g0, g1), 0, wv, wsem, 0) + load_weight(sc, (u0, u1), 2 * HID, wv, wsem, 16)
        )
    )

    def work(start, size, expert):
        at = pl.ds(start, size)
        dxv[at, :] = jnp.dot(gu[at, :], wv[expert], preferred_element_type=F32).astype(BF)

    @pl.loop(0, rows // TILE)
    def _(t):
        by_tile(sc, t, work)

    wait_all(
        start_all(
            [
                pltpu.make_async_copy(dxv.at[:, aligned(y_of(sc, p), width)], dx.at[p], osem.at[p])
                for p in range(4)
            ]
        )
    )


def rows_part(sc, gu, w_gate, w_up):
    rows, width = gu.shape[0], 512
    return pl.pallas_call(
        rows_kernel,
        out_shape=jax.ShapeDtypeStruct((4, rows, width), BF),
        in_specs=[SM, VM] + [ANY] * 4,
        out_specs=ANY,
        scratch_shapes=[
            pltpu.VMEM((EXP, 4 * HID, 4 * width), BF),
            pltpu.VMEM((rows, 4 * width), BF),
            pltpu.SemaphoreType.DMA((32,)),
            pltpu.SemaphoreType.DMA((4,)),
        ],
        compiler_params=pltpu.CompilerParams(vmem_limit_bytes=32 << 20),
        cost_estimate=pl.CostEstimate(
            flops=8 * rows * HID * 4 * width, bytes_accessed=14 << 20, transcendentals=0
        ),
    )(sc, gu, *w_gate, *w_up)


def spread_rows(x):
    half = x.shape[0] // 2
    below = lax.ppermute(x, "y", ring(4, 1))
    above = lax.ppermute(x, "y", ring(4, 3))
    return (
        x,
        below,
        above,
        lax.ppermute(below[:half], "y", ring(4, 1)),
        lax.ppermute(above[half:], "y", ring(4, 3)),
    )


def spread_weight(w, *before):
    straight = lax.ppermute(w, ("xl", "z", "xh"), swap_pairs(0))
    crossed = lax.ppermute(w, ("xl", "z", "xh"), swap_pairs(1))
    pair = jnp.stack([straight, crossed])
    if before:
        pair = after(pair, *before)
    below = lax.ppermute(pair, "z", ring(4, 1))
    above = lax.ppermute(pair, "z", ring(4, 3))
    far0 = lax.ppermute(below[:1], "z", ring(4, 1))
    far1 = lax.ppermute(above[1:], "z", ring(4, 3))
    here = jnp.concatenate([pair, below, above, far0, far1])
    return (here, lax.ppermute(here, "core", ring(2, 1))), below


def sum_weights(keep, away, xh):
    got = lax.ppermute(away, "core", ring(2, 1))
    both = (keep.astype(F32) + got.astype(F32)).astype(BF)
    part = lax.psum_scatter(both, "z", scatter_dimension=0, tiled=False)
    straight = lax.dynamic_index_in_dim(part, xh, 0, False)
    crossed = lax.dynamic_index_in_dim(part, 1 - xh, 0, False)
    straight = lax.ppermute(straight, ("xl", "z", "xh"), swap_pairs(0))
    crossed = lax.ppermute(crossed, ("xl", "z", "xh"), swap_pairs(1))
    return straight.astype(F32) + crossed.astype(F32)


def on_device(features, grad_out, scores, counts, w_gate, w_up, w_down):
    rows = features.shape[0]
    xh = lax.axis_index("xh")
    y, xl, core, z = (lax.axis_index(a) for a in ("y", "xl", "core", "z"))
    sc = jnp.stack([y, xl, counts[0, 0], counts[0, 0] + counts[0, 1], core, z, xh]).astype(jnp.int32)
    scores = scores.reshape(rows // BLOCK, BLOCK)

    feats = spread_rows(features)
    gate_all, gate_step = spread_weight(w_gate)
    up_all, up_step = spread_weight(w_up, gate_step)
    down_all, _ = spread_weight(w_down, up_step)
    grads = spread_rows(after(grad_out, feats[3], feats[4]))

    own_g, send_g = pre_part(sc, feats, gate_all)
    got_g = lax.ppermute(send_g, "xl", ring(2, 1))
    own_u, send_u = pre_part(sc, feats, up_all)
    got_u = lax.ppermute(after(send_u, got_g), "xl", ring(2, 1))
    own_b, send_b = pre_part(sc, grads, down_all)
    got_b = lax.ppermute(after(send_b, got_u), "xl", ring(2, 1))

    down = down_part(sc, scores, own_g, got_g, own_u, got_u, grads)
    grad_down = sum_weights(*down, xh)
    sgrad, gu, keep, away = gate_up_part(
        sc, scores, own_g, got_g, own_u, got_u, own_b, got_b, feats
    )
    grad_gate_up = sum_weights(keep, away, xh)

    dx = rows_part(sc, gu, gate_all, up_all)
    from_below = lax.ppermute(dx[2], "y", ring(4, 1))
    from_above = lax.ppermute(dx[1], "y", ring(4, 3))
    opposite = lax.ppermute(dx[3], "y", ring(4, 2))
    grad_features = (
        (dx[0].astype(F32) + from_below.astype(F32)) + (from_above.astype(F32) + opposite.astype(F32))
    ).astype(BF)

    total = sgrad
    total = total + lax.ppermute(total, "xl", ring(2, 1))
    total = total + lax.ppermute(total, "y", [(i, i ^ 1) for i in range(4)])
    total = total + lax.ppermute(total, "y", [(i, i ^ 2) for i in range(4)])
    return grad_features, total.reshape(rows), grad_gate_up[0], grad_gate_up[1], grad_down[0]


def solution(mesh):
    fine = Mesh(mesh.devices.reshape(2, 4, 4, 2, 2), ("xl", "y", "z", "xh", "core"))
    grp, blk = ("xl", "y"), ("z", "xh", "core")
    weight = P(None, grp, blk)
    return jax.shard_map(
        on_device,
        mesh=fine,
        in_specs=(P(blk, grp), P(blk, grp), P(blk), P(blk, None), weight, weight, weight),
        out_specs=(P(blk, grp), P(blk), weight, weight, weight),
        check_vma=False,
    )
```

time: 312 us -> 320 us (1.026)
  waiting for transfers between devices: 194 us -> 139 us
  starting transfers between devices: 32.5 us -> 80.6 us
  Pallas kernels: 42.4 us -> 48.2 us
  local copies, waits for them, and re-layouts: 16.7 us -> 21.1 us
    ppermute x6 -> x30, starting transfers between devices: 13.3 us -> 62.7 us  [the longest x3 14.6 us: spread_weight(): straight = lax.ppermute(w, ('xl', 'z', 'xh'), swap_pairs(0))]
    ppermute x2, waiting for transfers between devices: 37 us -> 6.46 us  [spread_rows(): lax.ppermute(below[:half], 'y', ring(4, 1))]
    all_gather x1 -> x0, waiting for transfers between devices: 21.9 us -> none  [on_device(): w_all = lax.all_gather(shard, ('z', 'xh', 'core'), axis=0, tiled=False)]
    ppermute x2, waiting for transfers between devices: 19.2 us -> 0.01 us  [spread_rows(): below = lax.ppermute(x, 'y', ring(4, 1))]
    ppermute x6 -> x30, waiting for transfers between devices: 72.6 us -> 86.9 us  [the longest x1 18.8 us: on_device(): got_b = lax.ppermute(after(send_b, got_u), 'xl', ring(2, 1))]
    pallas_call x3 -> x6, Pallas kernels: 42.4 us -> 48.2 us  [the longest x3 16.5 us: pre_part(): pl.pallas_call(pre_kernel, out_shape=(jax.ShapeDtypeStruct((rows, n), F32...]
    unnamed x30 -> x45, local copies, waits for them, and re-layouts: 6.41 us -> 10.3 us
    convert_element_type x1 -> x2, other arithmetic: 6.28 us -> 8.79 us  [sum_weights(): both = (keep.astype(F32) + got.astype(F32)).astype(BF)]
  transfers between devices with their start and end apart: 22 -> 46, of which waited for: 12 -> 18; matrix products, arithmetic and copies ran while one was open for 4% -> 8% of each run, Pallas kernels for 5% -> 15%
where the time goes in v2:
time: 320 us; the launch traced here: 319 us
  waiting for transfers between devices  139 us (43%)
  starting transfers between devices  80.6 us (25%)
  Pallas kernels  48.2 us (15%)
  local copies, waits for them, and re-layouts  21.1 us (7%)
  between operations  15.8 us (5%)
  other arithmetic  14.1 us (4%)
    ppermute x1, waiting for transfers between devices, on_device(): total = total + lax.ppermute(total, 'y', [(i, i ^ 1) for i in range(4)])  41.2 us
    ppermute x1, waiting for transfers between devices, on_device(): got_b = lax.ppermute(after(send_b, got_u), 'xl', ring(2, 1))  18.8 us
    pallas_call x3, Pallas kernels, pre_part(): pl.pallas_call(pre_kernel, out_shape=(jax.ShapeDtypeStruct((rows, n), F32...  16.5 us
    pallas_call x1, Pallas kernels, gate_up_part(): pl.pallas_call(gate_up_kernel, out_shape=(jax.ShapeDtypeStruct((rows // B...  16.1 us
    ppermute x2, waiting for transfers between devices, sum_weights(): crossed = lax.ppermute(crossed, ('xl', 'z', 'xh'), swap_pairs(1))  16.1 us
    ppermute x3, starting transfers between devices, spread_weight(): straight = lax.ppermute(w, ('xl', 'z', 'xh'), swap_pairs(0))  14.6 us
    ppermute x3, waiting for transfers between devices, spread_weight(): below = lax.ppermute(pair, 'z', ring(4, 1))  14.1 us
    ppermute x3, waiting for transfers between devices, spread_weight(): crossed = lax.ppermute(w, ('xl', 'z', 'xh'), swap_pairs(1))  13 us
  transfers between devices with their start and end apart: 46, of which 18 were waited for; matrix products, arithmetic and copies ran while one was open for 8% of the time, Pallas kernels for 15%

profile of v2, /device:TPU:3, one launch (start us, length us, event | category | flops | bytes accessed | tf_op | source)
XLA Modules:
  0.0 318.8 jit_solution(9269050902014127802)
XLA Ops:
  7.2 5.5 %collective-permute-start.4 = (bf16[2,192,256]{2,1,0:T(8,128)(2,1)}, bf16[2,192,256]{2,1,0:T(8,128)(2,1)S(1)}, u32[]{:S(2)}, u32[]{:S(2)}) collective-permute-start(bf16[2,192,256]{2,1,0:T(8,128)(2,1)} %param.11), channel_id=1, source_target_pairs={{0,0},{2,2},{4,4},{6,6},{8,64},{10,66},{12,68},{14,70},{64,8},{66,... | collective-permute-start | bytes 589832 | tf_op jit(solution)/shard_map/ppermute | solution.py:359
  13.7 6.4 %collective-permute-start.12 = (bf16[2,192,256]{2,1,0:T(8,128)(2,1)}, bf16[2,192,256]{2,1,0:T(8,128)(2,1)S(1)}, u32[]{:S(2)}, u32[]{:S(2)}) collective-permute-start(bf16[2,192,256]{2,1,0:T(8,128)(2,1)} %param.12), channel_id=1, source_target_pairs={{0,0},{2,2},{4,4},{6,6},{8,64},{10,66},{12,68},{14,70},{64,8},{66,... | collective-permute-start | bytes 589832 | tf_op jit(solution)/shard_map/ppermute | solution.py:359
  21.6 8.3 %collective-permute-done.5 = bf16[2,192,256]{2,1,0:T(8,128)(2,1)S(1)} collective-permute-done((bf16[2,192,256]{2,1,0:T(8,128)(2,1)}, bf16[2,192,256]{2,1,0:T(8,128)(2,1)S(1)}, u32[]{:S(2)}, u32[]{:S(2)}) %collective-permute-start.5) | collective-permute-done | bytes 196640 | tf_op jit(solution)/shard_map/ppermute | solution.py:360
  30.9 1.7 collective-permute-start.7
  32.6 2.8 collective-permute-start.1
  35.4 2.8 collective-permute-start.24
  38.3 3.6 %collective-permute-done.6 = bf16[2,2,192,256]{3,2,1,0:T(8,128)(2,1)S(1)} collective-permute-done((bf16[2,2,192,256]{3,2,1,0:T(8,128)(2,1)S(1)}, bf16[2,2,192,256]{3,2,1,0:T(8,128)(2,1)S(1)}, u32[]{:S(2)}, u32[]{:S(2)}) %collective-permute-start.6) | collective-permute-done | bytes 393248 | tf_op jit(solution)/shard_map/ppermute | solution.py:364
  42.0 4.0 %collective-permute-start.9 = (bf16[1,2,192,256]{3,2,1,0:T(8,128)(2,1)S(1)}, bf16[1,2,192,256]{3,2,1,0:T(8,128)(2,1)S(1)}, u32[]{:S(2)}, u32[]{:S(2)}) collective-permute-start(bf16[1,2,192,256]{3,2,1,0:T(8,128)(2,1)S(1)} %slice.76), channel_id=1, source_target_pairs={{0,12},{4,0},{8,4},{12,8},{1,13},{5,1},{9,5},{13,9},{2,14},{6,2},{... | collective-permute-start | bytes 589832 | tf_op jit(solution)/shard_map/ppermute | solution.py:367
  46.0 4.5 %collective-permute-done.8 = bf16[1,2,192,256]{3,2,1,0:T(8,128)(2,1)S(1)} collective-permute-done((bf16[1,2,192,256]{3,2,1,0:T(8,128)(2,1)S(1)}, bf16[1,2,192,256]{3,2,1,0:T(8,128)(2,1)S(1)}, u32[]{:S(2)}, u32[]{:S(2)}) %collective-permute-start.8) | collective-permute-done | bytes 196640 | tf_op jit(solution)/shard_map/ppermute | solution.py:366
  50.5 4.6 %collective-permute-start.25 = (bf16[2,192,256]{2,1,0:T(8,128)(2,1)S(1)}, bf16[2,192,256]{2,1,0:T(8,128)(2,1)S(1)}, u32[]{:S(2)}, u32[]{:S(2)}) collective-permute-start(bf16[2,192,256]{2,1,0:T(8,128)(2,1)S(1)} %copy-done.15), channel_id=1, source_target_pairs={{0,2},{2,0},{4,6},{6,4},{8,66},{10,64},{12,70},{14,68},{64,10},{66... | collective-permute-start | bytes 589832 | tf_op jit(solution)/shard_map/ppermute | solution.py:360
  55.2 2.7 collective-permute-start.15
  57.9 4.7 %collective-permute-done.25 = bf16[2,192,256]{2,1,0:T(8,128)(2,1)S(1)} collective-permute-done((bf16[2,192,256]{2,1,0:T(8,128)(2,1)S(1)}, bf16[2,192,256]{2,1,0:T(8,128)(2,1)S(1)}, u32[]{:S(2)}, u32[]{:S(2)}) %collective-permute-start.25) | collective-permute-done | bytes 196640 | tf_op jit(solution)/shard_map/ppermute | solution.py:360
  63.3 7.8 %collective-permute-done.14 = bf16[2,2,192,256]{3,2,1,0:T(8,128)(2,1)S(1)} collective-permute-done((bf16[2,2,192,256]{3,2,1,0:T(8,128)(2,1)S(1)}, bf16[2,2,192,256]{3,2,1,0:T(8,128)(2,1)S(1)}, u32[]{:S(2)}, u32[]{:S(2)}) %collective-permute-start.14) | collective-permute-done | bytes 393248 | tf_op jit(solution)/shard_map/ppermute | solution.py:364
  71.2 2.7 collective-permute-start.17
  74.0 4.3 %collective-permute-done.16 = bf16[1,2,192,256]{3,2,1,0:T(8,128)(2,1)S(1)} collective-permute-done((bf16[1,2,192,256]{3,2,1,0:T(8,128)(2,1)S(1)}, bf16[1,2,192,256]{3,2,1,0:T(8,128)(2,1)S(1)}, u32[]{:S(2)}, u32[]{:S(2)}) %collective-permute-start.16) | collective-permute-done | bytes 196640 | tf_op jit(solution)/shard_map/ppermute | solution.py:366
  84.1 2.0 collective-permute-start.3
  86.1 2.8 collective-permute-done.26
  93.4 4.8 %collective-permute-done.27 = bf16[2,2,192,256]{3,2,1,0:T(8,128)(2,1)} collective-permute-done((bf16[2,2,192,256]{3,2,1,0:T(8,128)(2,1)S(1)}, bf16[2,2,192,256]{3,2,1,0:T(8,128)(2,1)}, u32[]{:S(2)}, u32[]{:S(2)}) %collective-permute-start.27) | collective-permute-done | bytes 393248 | tf_op jit(solution)/shard_map/ppermute | solution.py:365
  100.2 2.7 collective-permute-start.29
  102.9 2.7 collective-permute-start.21
  106.9 5.8 %shard_map.110 = (f32[1024,384]{1,0:T(8,128)S(1)}, bf16[1024,384]{1,0:T(8,128)(2,1)S(1)}) custom-call(s32[7]{0:T(128)S(1)} %stack.54.sc, bf16[1024,512]{1,0:T(8,128)(2,1)S(1)} %copy-done.7, bf16[1024,512]{1,0:T(8,128)(2,1)S(1)} %copy-done.3, bf16[1024,512]{1,0:T(8,128)(2,1)S(1)} %copy-done.5, bf16[512,512]{1,0:T(8,128)(2,1)} %collective-permute-done.2.x3, ...), custom_call_target="tpu_custom_call" | custom-call | flops 3221225472 | bytes 10485760 | tf_op jit(solution)/shard_map/pallas_call | solution.py:137
  114.2 4.8 %collective-permute-start.30 = (bf16[8,2,192,256]{3,2,1,0:T(8,128)(2,1)S(1)}, bf16[8,2,192,256]{3,2,1,0:T(8,128)(2,1)S(1)}, u32[]{:S(2)}, u32[]{:S(2)}) collective-permute-start(bf16[8,2,192,256]{3,2,1,0:T(8,128)(2,1)S(1)} %constant_dynamic-update-slice_fusion.11.w0), channel_id=1, source_target_pairs={{0,1},{1,0},{2,3},{3,2},{4,5},{5,4},{6,7},{7,6},{8,9},{9,8},{10,11... | collective-permute-start | bytes 4718600 | tf_op jit(solution)/shard_map/ppermute | solution.py:369
  119.0 5.8 %shard_map.111 = (f32[1024,384]{1,0:T(8,128)S(1)}, bf16[1024,384]{1,0:T(8,128)(2,1)S(1)}) custom-call(s32[7]{0:T(128)S(1)} %stack.54.sc, bf16[1024,512]{1,0:T(8,128)(2,1)S(1)} %copy-done.7, bf16[1024,512]{1,0:T(8,128)(2,1)S(1)} %copy-done.3, bf16[1024,512]{1,0:T(8,128)(2,1)S(1)} %copy-done.5, bf16[512,512]{1,0:T(8,128)(2,1)} %collective-permute-done.2.x3, ...), custom_call_target="tpu_custom_call" | custom-call | flops 3221225472 | bytes 10485760 | tf_op jit(solution)/shard_map/pallas_call | solution.py:137
  124.9 2.4 collective-permute-done.11.got_g
  127.8 2.7 collective-permute-start.23
  130.5 6.5 %collective-permute-done.22.x3.g3 = bf16[512,512]{1,0:T(8,128)(2,1)S(1)} collective-permute-done((bf16[512,512]{1,0:T(8,128)(2,1)S(1)}, bf16[512,512]{1,0:T(8,128)(2,1)S(1)}, u32[]{:S(2)}, u32[]{:S(2)}) %collective-permute-start.22) | collective-permute-done | bytes 524320 | tf_op jit(solution)/shard_map/ppermute | solution.py:353
  136.9 6.4 %collective-permute-done.19.got_u = bf16[1024,384]{1,0:T(8,128)(2,1)S(1)} collective-permute-done((bf16[1024,384]{1,0:T(8,128)(2,1)S(1)}, bf16[1024,384]{1,0:T(8,128)(2,1)S(1)}, u32[]{:S(2)}, u32[]{:S(2)}) %collective-permute-start.19) | collective-permute-done | bytes 786464 | tf_op jit(solution)/shard_map/ppermute | solution.py:399
  143.3 7.8 %shard_map.115 = (bf16[4,2,1,2,192,256]{5,4,3,2,1,0:T(8,128)(2,1)S(1)}, bf16[4,2,1,2,192,256]{5,4,3,2,1,0:T(8,128)(2,1)S(1)}) custom-call(s32[7]{0:T(128)S(1)} %stack.54.sc, f32[8,128]{1,0:T(8,128)S(1)} %bitcast.43, f32[1024,384]{1,0:T(8,128)S(1)} %get-tuple-element.22.own_g, bf16[1024,384]{1,0:T(8,128)(2,1)S(1)} %collective-permute-done.11.got_g, ...), custom_call_target="tpu_custom_call" | custom-call | flops 3221225472 | bytes 14680064 | tf_op jit(solution)/shard_map/pallas_call | solution.py:212
  151.1 6.4 %collective-permute-start.41 = (bf16[4,2,1,2,192,256]{5,4,3,2,1,0:T(8,128)(2,1)S(1)}, bf16[4,2,1,2,192,256]{5,4,3,2,1,0:T(8,128)(2,1)}, u32[]{:S(2)}, u32[]{:S(2)}) collective-permute-start(bf16[4,2,1,2,192,256]{5,4,3,2,1,0:T(8,128)(2,1)S(1)} %get-tuple-element.38), channel_id=1, source_target_pairs={{0,1},{1,0},{2,3},{3,2},{4,5},{5,4},{6,7},{7,6},{8,9},{9,8},{10,11... | collective-permute-start | bytes 4718600 | tf_op jit(solution)/shard_map/ppermute | solution.py:373
  157.5 4.8 %shard_map.112 = (f32[1024,384]{1,0:T(8,128)S(1)}, bf16[1024,384]{1,0:T(8,128)(2,1)S(1)}) custom-call(s32[7]{0:T(128)S(1)} %stack.54.sc, bf16[1024,512]{1,0:T(8,128)(2,1)S(1)} %copy-done.6, bf16[1024,512]{1,0:T(8,128)(2,1)S(1)} %collective-permute-done.20.x1.g1, bf16[1024,512]{1,0:T(8,128)(2,1)S(1)} %collective-permute-done.21.x2.g2, ...), custom_call_target="tpu_custom_call" | custom-call | flops 3221225472 | bytes 10485760 | tf_op jit(solution)/shard_map/pallas_call | solution.py:137
  163.5 18.8 %collective-permute-done.31.got_b = bf16[1024,384]{1,0:T(8,128)(2,1)S(1)} collective-permute-done((bf16[1024,384]{1,0:T(8,128)(2,1)S(1)}, bf16[1024,384]{1,0:T(8,128)(2,1)S(1)}, u32[]{:S(2)}, u32[]{:S(2)}) %collective-permute-start.31) | collective-permute-done | bytes 786464 | tf_op jit(solution)/shard_map/ppermute | solution.py:401
  182.3 16.1 %shard_map.113 = (f32[8,128]{1,0:T(8,128)S(1)}, bf16[1024,768]{1,0:T(8,128)(2,1)}, bf16[4,2,2,2,192,256]{5,4,3,2,1,0:T(8,128)(2,1)}, bf16[4,2,2,2,192,256]{5,4,3,2,1,0:T(8,128)(2,1)}) custom-call(s32[7]{0:T(128)S(1)} %stack.54.sc, f32[8,128]{1,0:T(8,128)S(1)} %bitcast.44, f32[1024,384]{1,0:T(8,128)} %copy-done.10, ...), custom_call_target="tpu_custom_call" | custom-call | flops 6442450944 | bytes 20971520 | tf_op jit(solution)/shard_map/pallas_call | solution.py:274
  199.7 3.0 add_convert_fusion.1
  202.8 2.5 collective-permute-done.38
  205.3 5.7 %add_convert_fusion = bf16[4,2,2,2,192,256]{5,4,3,2,1,0:T(8,128)(2,1)} fusion(bf16[4,2,2,2,192,256]{5,4,3,2,1,0:T(8,128)(2,1)} %collective-permute-done.38, bf16[4,2,2,2,192,256]{5,4,3,2,1,0:T(8,128)(2,1)} %get-tuple-element.35), kind=kLoop, calls=%fused_computation | loop fusion | flops 6291456 | bytes 9437184 | tf_op jit(solution)/shard_map/convert_element_type | solution.py:374
  212.5 7.8 %shard_map.114 = bf16[4,1024,512]{2,1,0:T(8,128)(2,1)S(1)} custom-call(s32[7]{0:T(128)S(1)} %stack.54.sc, bf16[1024,768]{1,0:T(8,128)(2,1)S(1)} %copy-done.1, bf16[8,2,192,256]{3,2,1,0:T(8,128)(2,1)S(1)} %constant_dynamic-update-slice_fusion.w0.g0, bf16[8,2,192,256]{3,2,1,0:T(8,128)(2,1)} %collective-permute-done.10.w1.g1, ...), custom_call_target="tpu_custom_call" | custom-call | flops 3221225472 | bytes 14680064 | tf_op jit(solution)/shard_map/pallas_call | solution.py:327
  220.3 1.8 slice_bitcast_fusion.2
  223.3 2.7 collective-permute-start.33
  226.0 2.7 collective-permute-done.35
  229.3 41.2 %collective-permute-done.36 = f32[8,128]{1,0:T(8,128)S(1)} collective-permute-done((f32[8,128]{1,0:T(8,128)S(1)}, f32[8,128]{1,0:T(8,128)S(1)}, u32[]{:S(2)}, u32[]{:S(2)}) %collective-permute-start.36) | collective-permute-done | bytes 4128 | tf_op jit(solution)/shard_map/ppermute | solution.py:420
  270.5 2.2 collective-permute-start.37
  276.8 3.6 %collective-permute-start.42 = (bf16[1,2,192,256]{3,2,1,0:T(8,128)(2,1)}, bf16[1,2,192,256]{3,2,1,0:T(8,128)(2,1)S(1)}, u32[]{:S(2)}, u32[]{:S(2)}) collective-permute-start(bf16[1,2,192,256]{3,2,1,0:T(8,128)(2,1)} %get-tuple-element.46), channel_id=1, source_target_pairs={{0,0},{2,2},{4,4},{6,6},{8,64},{10,66},{12,68},{14,70},{64,8},{66,... | collective-permute-start | bytes 589832 | tf_op jit(solution)/shard_map/ppermute | solution.py:378
  280.3 2.9 collective-permute-start.43
  284.5 2.9 collective-permute-start.39
  287.4 2.9 collective-permute-start.40
  290.3 2.8 fusion.1
  293.0 8.8 %collective-permute-done.43 = bf16[1,2,192,256]{3,2,1,0:T(8,128)(2,1)} collective-permute-done((bf16[1,2,192,256]{3,2,1,0:T(8,128)(2,1)S(1)}, bf16[1,2,192,256]{3,2,1,0:T(8,128)(2,1)}, u32[]{:S(2)}, u32[]{:S(2)}) %collective-permute-start.43) | collective-permute-done | bytes 196640 | tf_op jit(solution)/shard_map/ppermute | solution.py:379
  303.6 7.3 %collective-permute-done.40 = bf16[2,2,192,256]{3,2,1,0:T(8,128)(2,1)S(1)} collective-permute-done((bf16[2,2,192,256]{3,2,1,0:T(8,128)(2,1)S(1)}, bf16[2,2,192,256]{3,2,1,0:T(8,128)(2,1)S(1)}, u32[]{:S(2)}, u32[]{:S(2)}) %collective-permute-start.40) | collective-permute-done | bytes 393248 | tf_op jit(solution)/shard_map/ppermute | solution.py:379
  (127 shorter events, 32.5 us)
Async XLA Ops:
  7.2 267.9 %reduce-scatter.5.cloned.1.call-start = ((), (), s32[]{:S(2)}) async-start(), calls=%async_computation.3 | async-start | bytes 1966080 | tf_op jit(solution)/shard_map/reduce_scatter | solution.py:375
  7.2 14.4 %collective-permute-start.4 = (bf16[2,192,256]{2,1,0:T(8,128)(2,1)}, bf16[2,192,256]{2,1,0:T(8,128)(2,1)S(1)}, u32[]{:S(2)}, u32[]{:S(2)}) collective-permute-start(bf16[2,192,256]{2,1,0:T(8,128)(2,1)} %param.11), channel_id=1, source_target_pairs={{0,0},{2,2},{4,4},{6,6},{8,64},{10,66},{12,68},{14,70},{64,8},{66,... | collective-permute-start | bytes 589832 | tf_op jit(solution)/shard_map/ppermute | solution.py:359
  12.7 17.1 %collective-permute-start.5 = (bf16[2,192,256]{2,1,0:T(8,128)(2,1)}, bf16[2,192,256]{2,1,0:T(8,128)(2,1)S(1)}, u32[]{:S(2)}, u32[]{:S(2)}) collective-permute-start(bf16[2,192,256]{2,1,0:T(8,128)(2,1)} %param.11), channel_id=1, source_target_pairs={{0,2},{2,0},{4,6},{6,4},{8,66},{10,64},{12,70},{14,68},{64,10},{66... | collective-permute-start | bytes 589832 | tf_op jit(solution)/shard_map/ppermute | solution.py:360
  13.7 18.9 %collective-permute-start.12 = (bf16[2,192,256]{2,1,0:T(8,128)(2,1)}, bf16[2,192,256]{2,1,0:T(8,128)(2,1)S(1)}, u32[]{:S(2)}, u32[]{:S(2)}) collective-permute-start(bf16[2,192,256]{2,1,0:T(8,128)(2,1)} %param.12), channel_id=1, source_target_pairs={{0,0},{2,2},{4,4},{6,6},{8,64},{10,66},{12,68},{14,70},{64,8},{66,... | collective-permute-start | bytes 589832 | tf_op jit(solution)/shard_map/ppermute | solution.py:359
  20.1 15.3 %collective-permute-start.13 = (bf16[2,192,256]{2,1,0:T(8,128)(2,1)}, bf16[2,192,256]{2,1,0:T(8,128)(2,1)S(1)}, u32[]{:S(2)}, u32[]{:S(2)}) collective-permute-start(bf16[2,192,256]{2,1,0:T(8,128)(2,1)} %param.12), channel_id=1, source_target_pairs={{0,2},{2,0},{4,6},{6,4},{8,66},{10,64},{12,70},{14,68},{64,10},{66... | collective-permute-start | bytes 589832 | tf_op jit(solution)/shard_map/ppermute | solution.py:360
  20.2 59.6 %collective-permute-start = (bf16[1024,512]{1,0:T(8,128)(2,1)}, bf16[1024,512]{1,0:T(8,128)(2,1)S(1)}, u32[]{:S(2)}, u32[]{:S(2)}) collective-permute-start(bf16[1024,512]{1,0:T(8,128)(2,1)} %x0.6), channel_id=1, source_target_pairs={{0,16},{16,32},{32,48},{48,0},{1,17},{17,33},{33,49},{49,1},{2,18}... | collective-permute-start | bytes 3145736 | tf_op jit(solution)/shard_map/ppermute | solution.py:347
  29.9 12.0 %collective-permute-start.6 = (bf16[2,2,192,256]{3,2,1,0:T(8,128)(2,1)S(1)}, bf16[2,2,192,256]{3,2,1,0:T(8,128)(2,1)S(1)}, u32[]{:S(2)}, u32[]{:S(2)}) collective-permute-start(bf16[2,2,192,256]{3,2,1,0:T(8,128)(2,1)S(1)} %pad_maximum_fusion), channel_id=1, source_target_pairs={{0,4},{4,8},{8,12},{12,0},{1,5},{5,9},{9,13},{13,1},{2,6},{6,10},{... | collective-permute-start | bytes 1179656 | tf_op jit(solution)/shard_map/ppermute | solution.py:364
  30.9 11.1 %collective-permute-start.7 = (bf16[2,2,192,256]{3,2,1,0:T(8,128)(2,1)S(1)}, bf16[2,2,192,256]{3,2,1,0:T(8,128)(2,1)S(1)}, u32[]{:S(2)}, u32[]{:S(2)}) collective-permute-start(bf16[2,2,192,256]{3,2,1,0:T(8,128)(2,1)S(1)} %pad_maximum_fusion), channel_id=1, source_target_pairs={{0,12},{4,0},{8,4},{12,8},{1,13},{5,1},{9,5},{13,9},{2,14},{6,2},{... | collective-permute-start | bytes 1179656 | tf_op jit(solution)/shard_map/ppermute | solution.py:365
  32.6 49.6 %collective-permute-start.1 = (bf16[1024,512]{1,0:T(8,128)(2,1)}, bf16[1024,512]{1,0:T(8,128)(2,1)S(1)}, u32[]{:S(2)}, u32[]{:S(2)}) collective-permute-start(bf16[1024,512]{1,0:T(8,128)(2,1)} %x0.6), channel_id=1, source_target_pairs={{0,48},{16,0},{32,16},{48,32},{1,49},{17,1},{33,17},{49,33},{2,50}... | collective-permute-start | bytes 3145736 | tf_op jit(solution)/shard_map/ppermute | solution.py:348
  35.4 19.7 %collective-permute-start.24 = (bf16[2,192,256]{2,1,0:T(8,128)(2,1)}, bf16[2,192,256]{2,1,0:T(8,128)(2,1)S(1)}, u32[]{:S(2)}, u32[]{:S(2)}) collective-permute-start(bf16[2,192,256]{2,1,0:T(8,128)(2,1)} %param.13), channel_id=1, source_target_pairs={{0,0},{2,2},{4,4},{6,6},{8,64},{10,66},{12,68},{14,70},{64,8},{66,... | collective-permute-start | bytes 589832 | tf_op jit(solution)/shard_map/ppermute | solution.py:359
  41.9 8.7 %collective-permute-start.8 = (bf16[1,2,192,256]{3,2,1,0:T(8,128)(2,1)S(1)}, bf16[1,2,192,256]{3,2,1,0:T(8,128)(2,1)S(1)}, u32[]{:S(2)}, u32[]{:S(2)}) collective-permute-start(bf16[1,2,192,256]{3,2,1,0:T(8,128)(2,1)S(1)} %slice.75), channel_id=1, source_target_pairs={{0,4},{4,8},{8,12},{12,0},{1,5},{5,9},{9,13},{13,1},{2,6},{6,10},{... | collective-permute-start | bytes 589832 | tf_op jit(solution)/shard_map/ppermute | solution.py:366
  42.0 13.2 %collective-permute-start.9 = (bf16[1,2,192,256]{3,2,1,0:T(8,128)(2,1)S(1)}, bf16[1,2,192,256]{3,2,1,0:T(8,128)(2,1)S(1)}, u32[]{:S(2)}, u32[]{:S(2)}) collective-permute-start(bf16[1,2,192,256]{3,2,1,0:T(8,128)(2,1)S(1)} %slice.76), channel_id=1, source_target_pairs={{0,12},{4,0},{8,4},{12,8},{1,13},{5,1},{9,5},{13,9},{2,14},{6,2},{... | collective-permute-start | bytes 589832 | tf_op jit(solution)/shard_map/ppermute | solution.py:367
  50.5 12.1 %collective-permute-start.25 = (bf16[2,192,256]{2,1,0:T(8,128)(2,1)S(1)}, bf16[2,192,256]{2,1,0:T(8,128)(2,1)S(1)}, u32[]{:S(2)}, u32[]{:S(2)}) collective-permute-start(bf16[2,192,256]{2,1,0:T(8,128)(2,1)S(1)} %copy-done.15), channel_id=1, source_target_pairs={{0,2},{2,0},{4,6},{6,4},{8,66},{10,64},{12,70},{14,68},{64,10},{66... | collective-permute-start | bytes 589832 | tf_op jit(solution)/shard_map/ppermute | solution.py:360
  55.1 15.9 %collective-permute-start.14 = (bf16[2,2,192,256]{3,2,1,0:T(8,128)(2,1)S(1)}, bf16[2,2,192,256]{3,2,1,0:T(8,128)(2,1)S(1)}, u32[]{:S(2)}, u32[]{:S(2)}) collective-permute-start(bf16[2,2,192,256]{3,2,1,0:T(8,128)(2,1)S(1)} %pad_maximum_fusion.1), channel_id=1, source_target_pairs={{0,4},{4,8},{8,12},{12,0},{1,5},{5,9},{9,13},{13,1},{2,6},{6,10},{... | collective-permute-start | bytes 1179656 | tf_op jit(solution)/shard_map/ppermute | solution.py:364
  55.2 15.9 %collective-permute-start.15 = (bf16[2,2,192,256]{3,2,1,0:T(8,128)(2,1)S(1)}, bf16[2,2,192,256]{3,2,1,0:T(8,128)(2,1)S(1)}, u32[]{:S(2)}, u32[]{:S(2)}) collective-permute-start(bf16[2,2,192,256]{3,2,1,0:T(8,128)(2,1)S(1)} %pad_maximum_fusion.1), channel_id=1, source_target_pairs={{0,12},{4,0},{8,4},{12,8},{1,13},{5,1},{9,5},{13,9},{2,14},{6,2},{... | collective-permute-start | bytes 1179656 | tf_op jit(solution)/shard_map/ppermute | solution.py:365
  62.6 40.3 %collective-permute-start.10 = (bf16[8,2,192,256]{3,2,1,0:T(8,128)(2,1)S(1)}, bf16[8,2,192,256]{3,2,1,0:T(8,128)(2,1)}, u32[]{:S(2)}, u32[]{:S(2)}) collective-permute-start(bf16[8,2,192,256]{3,2,1,0:T(8,128)(2,1)S(1)} %constant_dynamic-update-slice_fusion.w0.g0), channel_id=1, source_target_pairs={{0,1},{1,0},{2,3},{3,2},{4,5},{5,4},{6,7},{7,6},{8,9},{9,8},{10,11... | collective-permute-start | bytes 4718600 | tf_op jit(solution)/shard_map/ppermute | solution.py:369
  71.1 7.3 %collective-permute-start.16 = (bf16[1,2,192,256]{3,2,1,0:T(8,128)(2,1)S(1)}, bf16[1,2,192,256]{3,2,1,0:T(8,128)(2,1)S(1)}, u32[]{:S(2)}, u32[]{:S(2)}) collective-permute-start(bf16[1,2,192,256]{3,2,1,0:T(8,128)(2,1)S(1)} %slice.77), channel_id=1, source_target_pairs={{0,4},{4,8},{8,12},{12,0},{1,5},{5,9},{9,13},{13,1},{2,6},{6,10},{... | collective-permute-start | bytes 589832 | tf_op jit(solution)/shard_map/ppermute | solution.py:366
  71.2 7.2 %collective-permute-start.17 = (bf16[1,2,192,256]{3,2,1,0:T(8,128)(2,1)S(1)}, bf16[1,2,192,256]{3,2,1,0:T(8,128)(2,1)S(1)}, u32[]{:S(2)}, u32[]{:S(2)}) collective-permute-start(bf16[1,2,192,256]{3,2,1,0:T(8,128)(2,1)S(1)} %slice.78), channel_id=1, source_target_pairs={{0,12},{4,0},{8,4},{12,8},{1,13},{5,1},{9,5},{13,9},{2,14},{6,2},{... | collective-permute-start | bytes 589832 | tf_op jit(solution)/shard_map/ppermute | solution.py:367
  78.3 10.6 %collective-permute-start.26 = (bf16[2,2,192,256]{3,2,1,0:T(8,128)(2,1)S(1)}, bf16[2,2,192,256]{3,2,1,0:T(8,128)(2,1)S(1)}, u32[]{:S(2)}, u32[]{:S(2)}) collective-permute-start(bf16[2,2,192,256]{3,2,1,0:T(8,128)(2,1)S(1)} %pad_maximum_fusion.2), channel_id=1, source_target_pairs={{0,4},{4,8},{8,12},{12,0},{1,5},{5,9},{9,13},{13,1},{2,6},{6,10},{... | collective-permute-start | bytes 1179656 | tf_op jit(solution)/shard_map/ppermute | solution.py:364
  78.4 40.6 %collective-permute-start.18 = (bf16[8,2,192,256]{3,2,1,0:T(8,128)(2,1)S(1)}, bf16[8,2,192,256]{3,2,1,0:T(8,128)(2,1)}, u32[]{:S(2)}, u32[]{:S(2)}) collective-permute-start(bf16[8,2,192,256]{3,2,1,0:T(8,128)(2,1)S(1)} %constant_dynamic-update-slice_fusion.6.w0.u0), channel_id=1, source_target_pairs={{0,1},{1,0},{2,3},{3,2},{4,5},{5,4},{6,7},{7,6},{8,9},{9,8},{10,11... | collective-permute-start | bytes 4718600 | tf_op jit(solution)/shard_map/ppermute | solution.py:369
  81.6 18.6 %collective-permute-start.2 = (bf16[512,512]{1,0:T(8,128)(2,1)}, bf16[512,512]{1,0:T(8,128)(2,1)}, u32[]{:S(2)}, u32[]{:S(2)}) collective-permute-start(bf16[512,512]{1,0:T(8,128)(2,1)} %slice.73), channel_id=1, source_target_pairs={{0,16},{16,32},{32,48},{48,0},{1,17},{17,33},{33,49},{49,1},{2,18}... | collective-permute-start | bytes 1572872 | tf_op jit(solution)/shard_map/ppermute | solution.py:353
  84.1 18.8 %collective-permute-start.3 = (bf16[512,512]{1,0:T(8,128)(2,1)}, bf16[512,512]{1,0:T(8,128)(2,1)}, u32[]{:S(2)}, u32[]{:S(2)}) collective-permute-start(bf16[512,512]{1,0:T(8,128)(2,1)} %slice.74), channel_id=1, source_target_pairs={{0,48},{16,0},{32,16},{48,32},{1,49},{17,1},{33,17},{49,33},{2,50}... | collective-permute-start | bytes 1572872 | tf_op jit(solution)/shard_map/ppermute | solution.py:354
  89.7 8.6 %collective-permute-start.27 = (bf16[2,2,192,256]{3,2,1,0:T(8,128)(2,1)S(1)}, bf16[2,2,192,256]{3,2,1,0:T(8,128)(2,1)}, u32[]{:S(2)}, u32[]{:S(2)}) collective-permute-start(bf16[2,2,192,256]{3,2,1,0:T(8,128)(2,1)S(1)} %pad_maximum_fusion.2), channel_id=1, source_target_pairs={{0,12},{4,0},{8,4},{12,8},{1,13},{5,1},{9,5},{13,9},{2,14},{6,2},{... | collective-permute-start | bytes 1179656 | tf_op jit(solution)/shard_map/ppermute | solution.py:365
  98.2 14.5 %collective-permute-start.28 = (bf16[1,2,192,256]{3,2,1,0:T(8,128)(2,1)S(1)}, bf16[1,2,192,256]{3,2,1,0:T(8,128)(2,1)S(1)}, u32[]{:S(2)}, u32[]{:S(2)}) collective-permute-start(bf16[1,2,192,256]{3,2,1,0:T(8,128)(2,1)S(1)} %slice.81), channel_id=1, source_target_pairs={{0,4},{4,8},{8,12},{12,0},{1,5},{5,9},{9,13},{13,1},{2,6},{6,10},{... | collective-permute-start | bytes 589832 | tf_op jit(solution)/shard_map/ppermute | solution.py:366
  100.2 14.0 %collective-permute-start.29 = (bf16[1,2,192,256]{3,2,1,0:T(8,128)(2,1)S(1)}, bf16[1,2,192,256]{3,2,1,0:T(8,128)(2,1)S(1)}, u32[]{:S(2)}, u32[]{:S(2)}) collective-permute-start(bf16[1,2,192,256]{3,2,1,0:T(8,128)(2,1)S(1)} %slice.82), channel_id=1, source_target_pairs={{0,12},{4,0},{8,4},{12,8},{1,13},{5,1},{9,5},{13,9},{2,14},{6,2},{... | collective-permute-start | bytes 589832 | tf_op jit(solution)/shard_map/ppermute | solution.py:367
  102.9 24.7 %collective-permute-start.20 = (bf16[1024,512]{1,0:T(8,128)(2,1)}, bf16[1024,512]{1,0:T(8,128)(2,1)S(1)}, u32[]{:S(2)}, u32[]{:S(2)}) collective-permute-start(bf16[1024,512]{1,0:T(8,128)(2,1)} %g0), channel_id=1, source_target_pairs={{0,16},{16,32},{32,48},{48,0},{1,17},{17,33},{33,49},{49,1},{2,18}... | collective-permute-start | bytes 3145736 | tf_op jit(solution)/shard_map/ppermute | solution.py:347
  102.9 24.8 %collective-permute-start.21 = (bf16[1024,512]{1,0:T(8,128)(2,1)}, bf16[1024,512]{1,0:T(8,128)(2,1)S(1)}, u32[]{:S(2)}, u32[]{:S(2)}) collective-permute-start(bf16[1024,512]{1,0:T(8,128)(2,1)} %g0), channel_id=1, source_target_pairs={{0,48},{16,0},{32,16},{48,32},{1,49},{17,1},{33,17},{49,33},{2,50}... | collective-permute-start | bytes 3145736 | tf_op jit(solution)/shard_map/ppermute | solution.py:348
  112.7 30.6 %copy-start.10 = (f32[1024,384]{1,0:T(8,128)}, f32[1024,384]{1,0:T(8,128)S(1)}, u32[]{:S(2)}) copy-start(f32[1024,384]{1,0:T(8,128)S(1)} %get-tuple-element.22.own_g) | copy-start | bytes 4718596
  112.7 14.6 %collective-permute-start.11 = (bf16[1024,384]{1,0:T(8,128)(2,1)S(1)}, bf16[1024,384]{1,0:T(8,128)(2,1)S(1)}, u32[]{:S(2)}, u32[]{:S(2)}) collective-permute-start(bf16[1024,384]{1,0:T(8,128)(2,1)S(1)} %get-tuple-element.23), channel_id=1, source_target_pairs={{0,64},{64,0},{1,65},{65,1},{2,66},{66,2},{3,67},{67,3},{4,68},{68... | collective-permute-start | bytes 2359304 | tf_op jit(solution)/shard_map/ppermute | solution.py:397
  114.2 43.3 %collective-permute-start.30 = (bf16[8,2,192,256]{3,2,1,0:T(8,128)(2,1)S(1)}, bf16[8,2,192,256]{3,2,1,0:T(8,128)(2,1)S(1)}, u32[]{:S(2)}, u32[]{:S(2)}) collective-permute-start(bf16[8,2,192,256]{3,2,1,0:T(8,128)(2,1)S(1)} %constant_dynamic-update-slice_fusion.11.w0), channel_id=1, source_target_pairs={{0,1},{1,0},{2,3},{3,2},{4,5},{5,4},{6,7},{7,6},{8,9},{9,8},{10,11... | collective-permute-start | bytes 4718600 | tf_op jit(solution)/shard_map/ppermute | solution.py:369
  127.3 16.0 %collective-permute-start.19 = (bf16[1024,384]{1,0:T(8,128)(2,1)S(1)}, bf16[1024,384]{1,0:T(8,128)(2,1)S(1)}, u32[]{:S(2)}, u32[]{:S(2)}) collective-permute-start(bf16[1024,384]{1,0:T(8,128)(2,1)S(1)} %get-tuple-element.27), channel_id=1, source_target_pairs={{0,64},{64,0},{1,65},{65,1},{2,66},{66,2},{3,67},{67,3},{4,68},{68... | collective-permute-start | bytes 2359304 | tf_op jit(solution)/shard_map/ppermute | solution.py:399
  127.6 9.3 %collective-permute-start.22 = (bf16[512,512]{1,0:T(8,128)(2,1)S(1)}, bf16[512,512]{1,0:T(8,128)(2,1)S(1)}, u32[]{:S(2)}, u32[]{:S(2)}) collective-permute-start(bf16[512,512]{1,0:T(8,128)(2,1)S(1)} %slice.79), channel_id=1, source_target_pairs={{0,16},{16,32},{32,48},{48,0},{1,17},{17,33},{33,49},{49,1},{2,18}... | collective-permute-start | bytes 1572872 | tf_op jit(solution)/shard_map/ppermute | solution.py:353
  127.8 9.2 %collective-permute-start.23 = (bf16[512,512]{1,0:T(8,128)(2,1)S(1)}, bf16[512,512]{1,0:T(8,128)(2,1)S(1)}, u32[]{:S(2)}, u32[]{:S(2)}) collective-permute-start(bf16[512,512]{1,0:T(8,128)(2,1)S(1)} %slice.80), channel_id=1, source_target_pairs={{0,48},{16,0},{32,16},{48,32},{1,49},{17,1},{33,17},{49,33},{2,50}... | collective-permute-start | bytes 1572872 | tf_op jit(solution)/shard_map/ppermute | solution.py:354
  151.1 31.2 %copy-start.8 = (bf16[1024,512]{1,0:T(8,128)(2,1)S(1)}, bf16[1024,512]{1,0:T(8,128)(2,1)}, u32[]{:S(2)}) copy-start(bf16[1024,512]{1,0:T(8,128)(2,1)} %x0.6) | copy-start | bytes 3145732
  151.1 48.6 %collective-permute-start.41 = (bf16[4,2,1,2,192,256]{5,4,3,2,1,0:T(8,128)(2,1)S(1)}, bf16[4,2,1,2,192,256]{5,4,3,2,1,0:T(8,128)(2,1)}, u32[]{:S(2)}, u32[]{:S(2)}) collective-permute-start(bf16[4,2,1,2,192,256]{5,4,3,2,1,0:T(8,128)(2,1)S(1)} %get-tuple-element.38), channel_id=1, source_target_pairs={{0,1},{1,0},{2,3},{3,2},{4,5},{5,4},{6,7},{7,6},{8,9},{9,8},{10,11... | collective-permute-start | bytes 4718600 | tf_op jit(solution)/shard_map/ppermute | solution.py:373
  163.5 18.8 %collective-permute-start.31 = (bf16[1024,384]{1,0:T(8,128)(2,1)S(1)}, bf16[1024,384]{1,0:T(8,128)(2,1)S(1)}, u32[]{:S(2)}, u32[]{:S(2)}) collective-permute-start(bf16[1024,384]{1,0:T(8,128)(2,1)S(1)} %get-tuple-element.32), channel_id=1, source_target_pairs={{0,64},{64,0},{1,65},{65,1},{2,66},{66,2},{3,67},{67,3},{4,68},{68... | collective-permute-start | bytes 2359304 | tf_op jit(solution)/shard_map/ppermute | solution.py:401
  198.4 6.9 %collective-permute-start.38 = (bf16[4,2,2,2,192,256]{5,4,3,2,1,0:T(8,128)(2,1)}, bf16[4,2,2,2,192,256]{5,4,3,2,1,0:T(8,128)(2,1)}, u32[]{:S(2)}, u32[]{:S(2)}) collective-permute-start(bf16[4,2,2,2,192,256]{5,4,3,2,1,0:T(8,128)(2,1)} %get-tuple-element.36), channel_id=1, source_target_pairs={{0,1},{1,0},{2,3},{3,2},{4,5},{5,4},{6,7},{7,6},{8,9},{9,8},{10,11... | collective-permute-start | bytes 9437192 | tf_op jit(solution)/shard_map/ppermute | solution.py:373
  202.8 80.5 %reduce-scatter.3.cloned.1.call-start = ((), (), s32[]{:S(2)}) async-start(), calls=%async_computation.2 | async-start | bytes 3932160 | tf_op jit(solution)/shard_map/reduce_scatter | solution.py:375
  223.3 61.1 %collective-permute-start.32 = (bf16[1024,512]{1,0:T(8,128)(2,1)}, bf16[1024,512]{1,0:T(8,128)(2,1)S(1)}, u32[]{:S(2)}, u32[]{:S(2)}) collective-permute-start(bf16[1024,512]{1,0:T(8,128)(2,1)} %get-tuple-element.39), channel_id=1, source_target_pairs={{0,16},{16,32},{32,48},{48,0},{1,17},{17,33},{33,49},{49,1},{2,18}... | collective-permute-start | bytes 3145736 | tf_op jit(solution)/shard_map/ppermute | solution.py:411
  223.3 64.1 %collective-permute-start.33 = (bf16[1024,512]{1,0:T(8,128)(2,1)}, bf16[1024,512]{1,0:T(8,128)(2,1)S(1)}, u32[]{:S(2)}, u32[]{:S(2)}) collective-permute-start(bf16[1024,512]{1,0:T(8,128)(2,1)} %get-tuple-element.41), channel_id=1, source_target_pairs={{0,48},{16,0},{32,16},{48,32},{1,49},{17,1},{33,17},{49,33},{2,50}... | collective-permute-start | bytes 3145736 | tf_op jit(solution)/shard_map/ppermute | solution.py:412
  226.0 64.3 %collective-permute-start.34 = (bf16[1024,512]{1,0:T(8,128)(2,1)}, bf16[1024,512]{1,0:T(8,128)(2,1)S(1)}, u32[]{:S(2)}, u32[]{:S(2)}) collective-permute-start(bf16[1024,512]{1,0:T(8,128)(2,1)} %get-tuple-element.40), channel_id=1, source_target_pairs={{0,32},{16,48},{32,0},{48,16},{1,33},{17,49},{33,1},{49,17},{2,34}... | collective-permute-start | bytes 3145736 | tf_op jit(solution)/shard_map/ppermute | solution.py:413
  226.0 2.8 collective-permute-start.35
  228.7 41.7 %collective-permute-start.36 = (f32[8,128]{1,0:T(8,128)S(1)}, f32[8,128]{1,0:T(8,128)S(1)}, u32[]{:S(2)}, u32[]{:S(2)}) collective-permute-start(f32[8,128]{1,0:T(8,128)S(1)} %add.53), channel_id=1, source_target_pairs={{0,16},{16,0},{32,48},{48,32},{1,17},{17,1},{33,49},{49,33},{2,18}... | collective-permute-start | bytes 12296 | tf_op jit(solution)/shard_map/ppermute | solution.py:420
  270.5 4.0 %collective-permute-start.37 = (f32[8,128]{1,0:T(8,128)S(1)}, f32[8,128]{1,0:T(8,128)S(1)}, u32[]{:S(2)}, u32[]{:S(2)}) collective-permute-start(f32[8,128]{1,0:T(8,128)S(1)} %add.54), channel_id=1, source_target_pairs={{0,32},{16,48},{32,0},{48,16},{1,33},{17,49},{33,1},{49,17},{2,34}... | collective-permute-start | bytes 12296 | tf_op jit(solution)/shard_map/ppermute | solution.py:421
  276.8 16.3 %collective-permute-start.42 = (bf16[1,2,192,256]{3,2,1,0:T(8,128)(2,1)}, bf16[1,2,192,256]{3,2,1,0:T(8,128)(2,1)S(1)}, u32[]{:S(2)}, u32[]{:S(2)}) collective-permute-start(bf16[1,2,192,256]{3,2,1,0:T(8,128)(2,1)} %get-tuple-element.46), channel_id=1, source_target_pairs={{0,0},{2,2},{4,4},{6,6},{8,64},{10,66},{12,68},{14,70},{64,8},{66,... | collective-permute-start | bytes 589832 | tf_op jit(solution)/shard_map/ppermute | solution.py:378
  280.3 21.6 %collective-permute-start.43 = (bf16[1,2,192,256]{3,2,1,0:T(8,128)(2,1)S(1)}, bf16[1,2,192,256]{3,2,1,0:T(8,128)(2,1)}, u32[]{:S(2)}, u32[]{:S(2)}) collective-permute-start(bf16[1,2,192,256]{3,2,1,0:T(8,128)(2,1)S(1)} %get-tuple-element.47), channel_id=1, source_target_pairs={{0,2},{2,0},{4,6},{6,4},{8,66},{10,64},{12,70},{14,68},{64,10},{66... | collective-permute-start | bytes 589832 | tf_op jit(solution)/shard_map/ppermute | solution.py:379
  284.5 19.2 %collective-permute-start.39 = (bf16[2,2,192,256]{3,2,1,0:T(8,128)(2,1)S(1)}, bf16[2,2,192,256]{3,2,1,0:T(8,128)(2,1)S(1)}, u32[]{:S(2)}, u32[]{:S(2)}) collective-permute-start(bf16[2,2,192,256]{3,2,1,0:T(8,128)(2,1)S(1)} %get-tuple-element.44), channel_id=1, source_target_pairs={{0,0},{2,2},{4,4},{6,6},{8,64},{10,66},{12,68},{14,70},{64,8},{66,... | collective-permute-start | bytes 1179656 | tf_op jit(solution)/shard_map/ppermute | solution.py:378
  287.4 23.5 %collective-permute-start.40 = (bf16[2,2,192,256]{3,2,1,0:T(8,128)(2,1)S(1)}, bf16[2,2,192,256]{3,2,1,0:T(8,128)(2,1)S(1)}, u32[]{:S(2)}, u32[]{:S(2)}) collective-permute-start(bf16[2,2,192,256]{3,2,1,0:T(8,128)(2,1)S(1)} %get-tuple-element.45), channel_id=1, source_target_pairs={{0,2},{2,0},{4,6},{6,4},{8,66},{10,64},{12,70},{14,68},{64,10},{66... | collective-permute-start | bytes 1179656 | tf_op jit(solution)/shard_map/ppermute | solution.py:379
  (14 other events, 127.5 us)
Sparse Core Ops, SparseCore 0:
  202.9 21.3 reduce-scatter.4
  226.7 38.8 reduce-scatter.2

commit v3 on v2

--- a/solution.py
+++ b/solution.py
@@ -17,11 +17,10 @@
 F32 = jnp.float32
 NT = (((1,), (1,)), ((), ()))
 OFFS = (0, 3, 1, 2)
-SLOTS = ((0, 0), (0, 1), (3, 0), (3, 1), (1, 0), (1, 1), (2, 0), (2, 1))
 ANY = pl.BlockSpec(memory_space=pl.ANY)
 VM = pl.BlockSpec(memory_space=pltpu.VMEM)
 SM = pl.BlockSpec(memory_space=pltpu.SMEM)
-Y, XL, FIRST, LIVE, CORE, Z, XH = range(7)
+Y, XL, FIRST, LIVE, CORE, XH = range(6)
 
 
 def ring(n, k):
@@ -58,29 +57,28 @@
     rows, width = pieces[0].shape
     half = rows // 2
     copies = []
-    for p in range(3):
-        at = aligned(y_of(sc, p), width)
-        copies.append(pltpu.make_async_copy(pieces[p], dst.at[:, at], sem.at[p]))
-    at = aligned(y_of(sc, 3), width)
-    copies.append(pltpu.make_async_copy(pieces[3], dst.at[pl.ds(0, half), at], sem.at[3]))
-    copies.append(pltpu.make_async_copy(pieces[4], dst.at[pl.ds(half, half), at], sem.at[4]))
+    for i, piece in enumerate(pieces):
+        where = aligned(y_of(sc, (i + 1) // 2), width)
+        some = pl.ds(0, rows) if i == 0 else pl.ds((i - 1) % 2 * half, half)
+        copies.append(pltpu.make_async_copy(piece, dst.at[some, where], sem.at[i]))
     return copies
 
 
-def load_weight(sc, pair, row, dst, sem, at_sem):
+def load_weight(sc, pair, w, row, dst, sem, at_sem):
     copies = []
     for c, ref in enumerate(pair):
         core = sc[CORE] if c == 0 else 1 - sc[CORE]
-        for i, (step, flip) in enumerate(SLOTS):
-            slot = lax.rem(sc[Z] + step, 4)
-            xh = 1 - sc[XH] if flip else sc[XH]
-            cb = lax.rem(slot, 2) * 4 + xh * 2 + core
-            rows = pl.ds(pl.multiple_of(row + lax.div(slot, 2) * HID, 64), HID)
-            copies.append(
-                pltpu.make_async_copy(
-                    ref.at[i], dst.at[:, rows, aligned(cb, COLS)], sem.at[at_sem + c * 8 + i]
+        for slot in range(4):
+            for flip in range(2):
+                xh = 1 - sc[XH] if flip else sc[XH]
+                cb = slot % 2 * 4 + xh * 2 + core
+                copies.append(
+                    pltpu.make_async_copy(
+                        ref.at[slot, flip, w],
+                        dst.at[:, pl.ds(row + slot // 2 * HID, HID), aligned(cb, COLS)],
+                        sem.at[at_sem + c * 8 + slot * 2 + flip],
+                    )
                 )
-            )
     return copies
 
 
@@ -113,10 +111,10 @@
         c.wait()
 
 
-def pre_kernel(sc, x0, x1, x2, x3, x4, w0, w1, own, send, xv, wv, xsem, wsem):
+def pre_kernel(w, sc, x0, x1, x2, x3, x4, x5, x6, w0, w1, own, send, xv, wv, xsem, wsem):
     wait_all(
         start_all(
-            load_weight(sc, (w0, w1), 0, wv, wsem, 0) + load_rows(sc, (x0, x1, x2, x3, x4), xv, xsem)
+            load_weight(sc, (w0, w1), w, 0, wv, wsem, 0) + load_rows(sc, (x0, x1, x2, x3, x4, x5, x6), xv, xsem)
         )
     )
 
@@ -131,18 +129,18 @@
         by_tile(sc, t, work)
 
 
-def pre_part(sc, pieces, weight):
+def pre_part(sc, pieces, weight, w):
     rows, width = pieces[0].shape
     wide, n = 4 * width, 2 * HID
     return pl.pallas_call(
-        pre_kernel,
+        functools.partial(pre_kernel, w),
         out_shape=(jax.ShapeDtypeStruct((rows, n), F32), jax.ShapeDtypeStruct((rows, n), BF)),
-        in_specs=[SM] + [ANY] * 7,
+        in_specs=[SM] + [ANY] * 9,
         out_specs=(VM, VM),
         scratch_shapes=[
             pltpu.VMEM((rows, wide), BF),
             pltpu.VMEM((EXP, n, wide), BF),
-            pltpu.SemaphoreType.DMA((5,)),
+            pltpu.SemaphoreType.DMA((7,)),
             pltpu.SemaphoreType.DMA((16,)),
         ],
         compiler_params=pltpu.CompilerParams(vmem_limit_bytes=32 << 20),
@@ -181,10 +179,10 @@
 
 
 def down_kernel(
-    sc, scores, own_g, got_g, own_u, got_u, g0, g1, g2, g3, g4, keep, away, gv, st, dd, gsem, dsem
+    sc, scores, own_g, got_g, own_u, got_u, g0, g1, g2, g3, g4, g5, g6, keep, away, gv, st, dd, gsem, dsem
 ):
     rows, width = g0.shape
-    gload = start_all(load_rows(sc, (g0, g1, g2, g3, g4), gv, gsem))
+    gload = start_all(load_rows(sc, (g0, g1, g2, g3, g4, g5, g6), gv, gsem))
 
     @pl.loop(0, rows // BLOCK)
     def _(b):
@@ -212,13 +210,13 @@
     return pl.pallas_call(
         down_kernel,
         out_shape=(out, out),
-        in_specs=[SM] + [VM] * 5 + [ANY] * 5,
+        in_specs=[SM] + [VM] * 5 + [ANY] * 7,
         out_specs=(ANY, ANY),
         scratch_shapes=[
             pltpu.VMEM((rows, 4 * width), BF),
             pltpu.VMEM((EXP, 2 * HID, rows), BF),
             pltpu.VMEM((EXP, 2 * HID, 4 * width), BF),
-            pltpu.SemaphoreType.DMA((5,)),
+            pltpu.SemaphoreType.DMA((7,)),
             pltpu.SemaphoreType.DMA((32,)),
         ],
         compiler_params=pltpu.CompilerParams(vmem_limit_bytes=40 << 20),
@@ -229,12 +227,12 @@
 
 
 def gate_up_kernel(
-    sc, scores, own_g, got_g, own_u, got_u, own_b, got_b, x0, x1, x2, x3, x4,
+    sc, scores, own_g, got_g, own_u, got_u, own_b, got_b, x0, x1, x2, x3, x4, x5, x6,
     sgrad, gu, keep, away, xv, gut, dgu, xsem, dsem,
 ):
     rows, width = x0.shape
     n = 2 * HID
-    xload = start_all(load_rows(sc, (x0, x1, x2, x3, x4), xv, xsem))
+    xload = start_all(load_rows(sc, (x0, x1, x2, x3, x4, x5, x6), xv, xsem))
 
     @pl.loop(0, rows // BLOCK)
     def _(b):
@@ -279,13 +277,13 @@
             out,
             out,
         ),
-        in_specs=[SM] + [VM] * 7 + [ANY] * 5,
+        in_specs=[SM] + [VM] * 7 + [ANY] * 7,
         out_specs=(VM, VM, ANY, ANY),
         scratch_shapes=[
             pltpu.VMEM((rows, 4 * width), BF),
             pltpu.VMEM((EXP, 4 * HID, rows), BF),
             pltpu.VMEM((EXP, 4 * HID, 4 * width), BF),
-            pltpu.SemaphoreType.DMA((5,)),
+            pltpu.SemaphoreType.DMA((7,)),
             pltpu.SemaphoreType.DMA((64,)),
         ],
         compiler_params=pltpu.CompilerParams(vmem_limit_bytes=48 << 20),
@@ -295,12 +293,12 @@
     )(sc, scores, own_g, got_g, own_u, got_u, own_b, got_b, *feats)
 
 
-def rows_kernel(sc, gu, g0, g1, u0, u1, dx, wv, dxv, wsem, osem):
+def rows_kernel(sc, gu, w0, w1, d0, d1, d2, d3, wv, dxv, wsem, osem):
     rows, wide = dxv.shape
     width = wide // 4
     wait_all(
         start_all(
-            load_weight(sc, (g0, g1), 0, wv, wsem, 0) + load_weight(sc, (u0, u1), 2 * HID, wv, wsem, 16)
+            load_weight(sc, (w0, w1), 0, 0, wv, wsem, 0) + load_weight(sc, (w0, w1), 1, 2 * HID, wv, wsem, 16)
         )
     )
 
@@ -315,20 +313,20 @@
     wait_all(
         start_all(
             [
-                pltpu.make_async_copy(dxv.at[:, aligned(y_of(sc, p), width)], dx.at[p], osem.at[p])
-                for p in range(4)
+                pltpu.make_async_copy(dxv.at[:, aligned(y_of(sc, p), width)], d, osem.at[p])
+                for p, d in enumerate((d0, d1, d2, d3))
             ]
         )
     )
 
 
-def rows_part(sc, gu, w_gate, w_up):
+def rows_part(sc, gu, weight):
     rows, width = gu.shape[0], 512
     return pl.pallas_call(
         rows_kernel,
-        out_shape=jax.ShapeDtypeStruct((4, rows, width), BF),
-        in_specs=[SM, VM] + [ANY] * 4,
-        out_specs=ANY,
+        out_shape=(jax.ShapeDtypeStruct((rows, width), BF),) * 4,
+        in_specs=[SM, VM] + [ANY] * 2,
+        out_specs=(ANY,) * 4,
         scratch_shapes=[
             pltpu.VMEM((EXP, 4 * HID, 4 * width), BF),
             pltpu.VMEM((rows, 4 * width), BF),
@@ -339,40 +337,37 @@
         cost_estimate=pl.CostEstimate(
             flops=8 * rows * HID * 4 * width, bytes_accessed=14 << 20, transcendentals=0
         ),
-    )(sc, gu, *w_gate, *w_up)
-
-
-def spread_rows(x):
+    )(sc, gu, *weight)
+
+
+def halves_over(x):
     half = x.shape[0] // 2
-    below = lax.ppermute(x, "y", ring(4, 1))
-    above = lax.ppermute(x, "y", ring(4, 3))
-    return (
-        x,
-        below,
-        above,
-        lax.ppermute(below[:half], "y", ring(4, 1)),
-        lax.ppermute(above[half:], "y", ring(4, 3)),
-    )
-
-
-def spread_weight(w, *before):
+    near = [lax.ppermute(x[:half], "y", ring(4, k)) for k in (1, 3)]
+    rest = [lax.ppermute(x[half:], "y", ring(4, k)) for k in (1, 3)]
+    return x, near[0], rest[0], near[1], rest[1]
+
+
+def opposite_over(pieces):
+    return lax.ppermute(pieces[1], "y", ring(4, 1)), lax.ppermute(pieces[4], "y", ring(4, 3))
+
+
+def plane_pair(w):
     straight = lax.ppermute(w, ("xl", "z", "xh"), swap_pairs(0))
     crossed = lax.ppermute(w, ("xl", "z", "xh"), swap_pairs(1))
-    pair = jnp.stack([straight, crossed])
-    if before:
-        pair = after(pair, *before)
-    below = lax.ppermute(pair, "z", ring(4, 1))
-    above = lax.ppermute(pair, "z", ring(4, 3))
-    far0 = lax.ppermute(below[:1], "z", ring(4, 1))
-    far1 = lax.ppermute(above[1:], "z", ring(4, 3))
-    here = jnp.concatenate([pair, below, above, far0, far1])
-    return (here, lax.ppermute(here, "core", ring(2, 1))), below
-
-
-def sum_weights(keep, away, xh):
+    return jnp.stack([straight, crossed])
+
+
+def spread_pair(pair, *before):
+    here = after(lax.all_gather(pair, "z", axis=0, tiled=False), *before)
+    return here, lax.ppermute(here, "core", ring(2, 1))
+
+
+def over_cores(keep, away):
     got = lax.ppermute(away, "core", ring(2, 1))
-    both = (keep.astype(F32) + got.astype(F32)).astype(BF)
-    part = lax.psum_scatter(both, "z", scatter_dimension=0, tiled=False)
+    return (keep.astype(F32) + got.astype(F32)).astype(BF)
+
+
+def over_chips(part, xh):
     straight = lax.dynamic_index_in_dim(part, xh, 0, False)
     crossed = lax.dynamic_index_in_dim(part, 1 - xh, 0, False)
     straight = lax.ppermute(straight, ("xl", "z", "xh"), swap_pairs(0))
@@ -380,34 +375,47 @@
     return straight.astype(F32) + crossed.astype(F32)
 
 
+def scatter_z(both):
+    return lax.psum_scatter(both, "z", scatter_dimension=0, tiled=False)
+
+
 def on_device(features, grad_out, scores, counts, w_gate, w_up, w_down):
     rows = features.shape[0]
-    xh = lax.axis_index("xh")
-    y, xl, core, z = (lax.axis_index(a) for a in ("y", "xl", "core", "z"))
-    sc = jnp.stack([y, xl, counts[0, 0], counts[0, 0] + counts[0, 1], core, z, xh]).astype(jnp.int32)
+    y, xl, core, xh = (lax.axis_index(a) for a in ("y", "xl", "core", "xh"))
+    sc = jnp.stack([y, xl, counts[0, 0], counts[0, 0] + counts[0, 1], core, xh]).astype(jnp.int32)
     scores = scores.reshape(rows // BLOCK, BLOCK)
 
-    feats = spread_rows(features)
-    gate_all, gate_step = spread_weight(w_gate)
-    up_all, up_step = spread_weight(w_up, gate_step)
-    down_all, _ = spread_weight(w_down, up_step)
-    grads = spread_rows(after(grad_out, feats[3], feats[4]))
-
-    own_g, send_g = pre_part(sc, feats, gate_all)
+    feats = halves_over(features)
+    feats += opposite_over(feats)
+    pair_gu = after(plane_pair(jnp.stack([w_gate, w_up])), feats[1], feats[3])
+    pair_d = plane_pair(after(w_down, pair_gu)[None])
+    grads = halves_over(after(grad_out, feats[5], feats[6]))
+    w_gu = spread_pair(pair_gu, feats[2], feats[4], pair_d, grads[1], grads[3])
+    w_d = spread_pair(pair_d)
+
+    own_g, send_g = pre_part(sc, feats, w_gu, 0)
     got_g = lax.ppermute(send_g, "xl", ring(2, 1))
-    own_u, send_u = pre_part(sc, feats, up_all)
+    own_u, send_u = pre_part(after(sc, send_g, grads[2], grads[4]), feats, w_gu, 1)
     got_u = lax.ppermute(after(send_u, got_g), "xl", ring(2, 1))
-    own_b, send_b = pre_part(sc, grads, down_all)
+    grads += opposite_over(after(grads, send_g))
+    own_b, send_b = pre_part(sc, grads, w_d, 0)
     got_b = lax.ppermute(after(send_b, got_u), "xl", ring(2, 1))
 
-    down = down_part(sc, scores, own_g, got_g, own_u, got_u, grads)
-    grad_down = sum_weights(*down, xh)
-    sgrad, gu, keep, away = gate_up_part(
-        sc, scores, own_g, got_g, own_u, got_u, own_b, got_b, feats
-    )
-    grad_gate_up = sum_weights(keep, away, xh)
-
-    dx = rows_part(sc, gu, gate_all, up_all)
+    both_d = over_cores(
+        *down_part(after(sc, send_b), scores, own_g, got_g, own_u, got_u, grads)
+    )
+    part_d = scatter_z(both_d)
+    total, gu, keep, away = gate_up_part(
+        sc, scores, own_g, got_g, own_u, got_u, own_b, after(got_b, both_d), feats
+    )
+    both_gu = over_cores(keep, away)
+    part_gu = scatter_z(both_gu)
+    total = total + lax.ppermute(total, "y", [(i, i ^ 1) for i in range(4)])
+
+    dx = rows_part(sc, after(gu, total, both_gu), w_gu)
+    total = total + lax.ppermute(total, "y", [(i, i ^ 2) for i in range(4)])
+    dx, _ = lax.optimization_barrier((dx, total))
+    total = total + lax.ppermute(total, "xl", ring(2, 1))
     from_below = lax.ppermute(dx[2], "y", ring(4, 1))
     from_above = lax.ppermute(dx[1], "y", ring(4, 3))
     opposite = lax.ppermute(dx[3], "y", ring(4, 2))
@@ -415,11 +423,9 @@
         (dx[0].astype(F32) + from_below.astype(F32)) + (from_above.astype(F32) + opposite.astype(F32))
     ).astype(BF)
 
-    total = sgrad
-    total = total + lax.ppermute(total, "xl", ring(2, 1))
-    total = total + lax.ppermute(total, "y", [(i, i ^ 1) for i in range(4)])
-    total = total + lax.ppermute(total, "y", [(i, i ^ 2) for i in range(4)])
-    return grad_features, total.reshape(rows), grad_gate_up[0], grad_gate_up[1], grad_down[0]
+    grad_down = over_chips(part_d, xh)
+    grad_gu = over_chips(after(part_gu, grad_down, total), xh)
+    return grad_features, total.reshape(rows), grad_gu[0], grad_gu[1], grad_down[0]
 
 
 def solution(mesh):

time: 320 us -> 319 us (level)
  starting transfers between devices: 80.6 us -> 57.1 us
  waiting for transfers between devices: 139 us -> 153 us
  local copies, waits for them, and re-layouts: 21.1 us -> 25.8 us
    ppermute x1, waiting for transfers between devices: 41.2 us -> 1.68 us  [on_device(): total = total + lax.ppermute(total, 'y', [(i, i ^ 1) for i in range(4)])]
    reduce_scatter x2, waiting for transfers between devices: 0.01 us -> 30.5 us  [scatter_z(): return lax.psum_scatter(both, 'z', scatter_dimension=0, tiled=False)]
    ppermute x35 -> x24, starting transfers between devices: 74.6 us -> 46.9 us  [the longest x2 8.22 us: plane_pair(): straight = lax.ppermute(w, ('xl', 'z', 'xh'), swap_pairs(0))]
    all_gather x0 -> x2, waiting for transfers between devices: none -> 24.7 us  [spread_pair(): here = after(lax.all_gather(pair, 'z', axis=0, tiled=False), *before)]
    ppermute x1, waiting for transfers between devices: 2.44 us -> 9.44 us  [on_device(): got_g = lax.ppermute(send_g, 'xl', ring(2, 1))]
    unnamed x45 -> x48, local copies, waits for them, and re-layouts: 10.3 us -> 17.2 us
    ppermute x35 -> x24, waiting for transfers between devices: 65.8 us -> 60.3 us  [the longest x2 19.5 us: plane_pair(): crossed = lax.ppermute(w, ('xl', 'z', 'xh'), swap_pairs(1))]
    ppermute x1, waiting for transfers between devices: 18.8 us -> 14.6 us  [on_device(): got_b = lax.ppermute(after(send_b, got_u), 'xl', ring(2, 1))]
  transfers between devices with their start and end apart: 46 -> 37, of which waited for: 18 -> 17; matrix products, arithmetic and copies ran while one was open for 8% -> 7% of each run, Pallas kernels for 15% -> 9%
where the time goes in v3:
time: 319 us; the launch traced here: 318 us
  waiting for transfers between devices  153 us (48%)
  starting transfers between devices  57.1 us (18%)
  Pallas kernels  51 us (16%)
  local copies, waits for them, and re-layouts  25.8 us (8%)
  other arithmetic  16.2 us (5%)
  between operations  15.3 us (5%)
    reduce_scatter x2, waiting for transfers between devices, scatter_z(): return lax.psum_scatter(both, 'z', scatter_dimension=0, tiled=False)  30.5 us
    all_gather x2, waiting for transfers between devices, spread_pair(): here = after(lax.all_gather(pair, 'z', axis=0, tiled=False), *before)  24.7 us
    ppermute x2, waiting for transfers between devices, plane_pair(): crossed = lax.ppermute(w, ('xl', 'z', 'xh'), swap_pairs(1))  19.5 us
    pallas_call x3, Pallas kernels, pre_part(): pl.pallas_call(functools.partial(pre_kernel, w), out_shape=(jax.ShapeDtyp...  18.9 us
    unnamed x48, local copies, waits for them, and re-layouts  17.2 us
    pallas_call x1, Pallas kernels, gate_up_part(): pl.pallas_call(gate_up_kernel, out_shape=(jax.ShapeDtypeStruct((rows // B...  16.2 us
    ppermute x1, waiting for transfers between devices, on_device(): got_b = lax.ppermute(after(send_b, got_u), 'xl', ring(2, 1))  14.6 us
    ppermute x4, waiting for transfers between devices, halves_over(): rest = [lax.ppermute(x[half:], 'y', ring(4, k)) for k in (1, 3)]  10.3 us
  transfers between devices with their start and end apart: 37, of which 17 were waited for; matrix products, arithmetic and copies ran while one was open for 7% of the time, Pallas kernels for 9%

profile of v3, /device:TPU:3, one launch (start us, length us, event | category | flops | bytes accessed | tf_op | source)
XLA Modules:
  0.0 318.1 jit_solution(13680314402607816164)
XLA Ops:
  8.3 4.6 %collective-permute-start.7 = (bf16[2,2,192,256]{3,2,1,0:T(8,128)(2,1)S(1)}, bf16[2,2,192,256]{3,2,1,0:T(8,128)(2,1)S(1)}, u32[]{:S(2)}, u32[]{:S(2)}) collective-permute-start(bf16[2,2,192,256]{3,2,1,0:T(8,128)(2,1)S(1)} %pad_maximum_fusion.1), channel_id=1, source_target_pairs={{0,2},{2,0},{4,6},{6,4},{8,66},{10,64},{12,70},{14,68},{64,10},{66... | collective-permute-start | bytes 1179656 | tf_op jit(solution)/shard_map/ppermute | solution.py:356
  12.9 2.5 collective-permute-start.6
  15.4 2.3 fusion.2
  19.0 1.4 collective-permute-start.2
  20.4 13.6 %collective-permute-done.7 = bf16[2,2,192,256]{3,2,1,0:T(8,128)(2,1)S(1)} collective-permute-done((bf16[2,2,192,256]{3,2,1,0:T(8,128)(2,1)S(1)}, bf16[2,2,192,256]{3,2,1,0:T(8,128)(2,1)S(1)}, u32[]{:S(2)}, u32[]{:S(2)}) %collective-permute-start.7) | collective-permute-done | bytes 393248 | tf_op jit(solution)/shard_map/ppermute | solution.py:356
  35.0 2.8 collective-permute-start.3
  37.8 10.2 %collective-permute-done.3.x4 = bf16[512,512]{1,0:T(8,128)(2,1)S(1)} collective-permute-done((bf16[512,512]{1,0:T(8,128)(2,1)}, bf16[512,512]{1,0:T(8,128)(2,1)S(1)}, u32[]{:S(2)}, u32[]{:S(2)}) %collective-permute-start.3) | collective-permute-done | bytes 524320 | tf_op jit(solution)/shard_map/ppermute | solution.py:346
  48.1 3.3 %collective-permute-start.5 = (bf16[512,512]{1,0:T(8,128)(2,1)S(1)}, bf16[512,512]{1,0:T(8,128)(2,1)S(1)}, u32[]{:S(2)}, u32[]{:S(2)}) collective-permute-start(bf16[512,512]{1,0:T(8,128)(2,1)S(1)} %collective-permute-done.3.x4), channel_id=1, source_target_pairs={{0,48},{16,0},{32,16},{48,32},{1,49},{17,1},{33,17},{49,33},{2,50}... | collective-permute-start | bytes 1572872 | tf_op jit(solution)/shard_map/ppermute | solution.py:351
  53.0 7.4 %collective-permute-done.5.x6 = bf16[512,512]{1,0:T(8,128)(2,1)S(1)} collective-permute-done((bf16[512,512]{1,0:T(8,128)(2,1)S(1)}, bf16[512,512]{1,0:T(8,128)(2,1)S(1)}, u32[]{:S(2)}, u32[]{:S(2)}) %collective-permute-start.5) | collective-permute-done | bytes 524320 | tf_op jit(solution)/shard_map/ppermute | solution.py:351
  62.3 3.5 %collective-permute-start.11 = (bf16[512,512]{1,0:T(8,128)(2,1)}, bf16[512,512]{1,0:T(8,128)(2,1)}, u32[]{:S(2)}, u32[]{:S(2)}) collective-permute-start(bf16[512,512]{1,0:T(8,128)(2,1)} %get-tuple-element.72), channel_id=1, source_target_pairs={{0,48},{16,0},{32,16},{48,32},{1,49},{17,1},{33,17},{49,33},{2,50}... | collective-permute-start | bytes 1572872 | tf_op jit(solution)/shard_map/ppermute | solution.py:345
  65.8 5.7 %collective-permute-start.8 = (bf16[1,2,192,256]{3,2,1,0:T(8,128)(2,1)}, bf16[1,2,192,256]{3,2,1,0:T(8,128)(2,1)S(1)}, u32[]{:S(2)}, u32[]{:S(2)}) collective-permute-start(bf16[1,2,192,256]{3,2,1,0:T(8,128)(2,1)} %bitcast.48), channel_id=1, source_target_pairs={{0,0},{2,2},{4,4},{6,6},{8,64},{10,66},{12,68},{14,70},{64,8},{66,... | collective-permute-start | bytes 589832 | tf_op jit(solution)/shard_map/ppermute | solution.py:355
  72.0 3.0 collective-permute-done.8
  75.0 5.9 %collective-permute-done.9 = bf16[1,2,192,256]{3,2,1,0:T(8,128)(2,1)S(1)} collective-permute-done((bf16[1,2,192,256]{3,2,1,0:T(8,128)(2,1)}, bf16[1,2,192,256]{3,2,1,0:T(8,128)(2,1)S(1)}, u32[]{:S(2)}, u32[]{:S(2)}) %collective-permute-start.9) | collective-permute-done | bytes 196640 | tf_op jit(solution)/shard_map/ppermute | solution.py:356
  81.7 2.1 all-gather.5.cloned.1.call-done
  88.4 1.6 collective-permute-start.15
  90.0 22.6 %all-gather.7.cloned.1.call-done = bf16[8,1,2,192,256]{4,3,2,1,0:T(8,128)(2,1)} async-done(((bf16[2,1,2,192,256]{4,3,2,1,0:T(8,128)(2,1)}), bf16[8,1,2,192,256]{4,3,2,1,0:T(8,128)(2,1)}) %all-gather.7.cloned.1.call-update) | async-done | bytes 1572880 | tf_op jit(solution)/shard_map/all_gather | solution.py:361
  113.2 1.9 copy-done.2
  118.2 5.9 %shard_map.110 = (f32[1024,384]{1,0:T(8,128)S(1)}, bf16[1024,384]{1,0:T(8,128)(2,1)S(1)}) custom-call(s32[6]{0:T(128)S(1)} %stack.50.sc, bf16[1024,512]{1,0:T(8,128)(2,1)S(1)} %copy-done.1, bf16[512,512]{1,0:T(8,128)(2,1)S(1)} %collective-permute-done.x1, bf16[512,512]{1,0:T(8,128)(2,1)} %collective-permute-done.1.x2, ...), custom_call_target="tpu_custom_call" | custom-call | flops 3221225472 | bytes 10485760 | tf_op jit(solution)/shard_map/pallas_call | solution.py:135
  125.8 1.5 collective-permute-start.18
  128.3 5.9 %shard_map.111 = (f32[1024,384]{1,0:T(8,128)S(1)}, bf16[1024,384]{1,0:T(8,128)(2,1)S(1)}) custom-call(s32[6]{0:T(128)S(1)} %stack.50.sc, bf16[1024,512]{1,0:T(8,128)(2,1)S(1)} %copy-done.1, bf16[512,512]{1,0:T(8,128)(2,1)S(1)} %collective-permute-done.x1, bf16[512,512]{1,0:T(8,128)(2,1)} %collective-permute-done.1.x2, bf16[512,512]{1,0:T(8,128)(2,1)S(1)} %copy-done.6, ...), custom_call_target="tpu_custom_call" | custom-call | flops 3221225472 | bytes 10485760 | tf_op jit(solution)/shard_map/pallas_call | solution.py:135
  134.3 9.4 %collective-permute-done.13.got_g = bf16[1024,384]{1,0:T(8,128)(2,1)S(1)} collective-permute-done((bf16[1024,384]{1,0:T(8,128)(2,1)S(1)}, bf16[1024,384]{1,0:T(8,128)(2,1)S(1)}, u32[]{:S(2)}, u32[]{:S(2)}) %collective-permute-start.13) | collective-permute-done | bytes 786464 | tf_op jit(solution)/shard_map/ppermute | solution.py:397
  144.0 7.0 %shard_map.112 = (f32[1024,384]{1,0:T(8,128)S(1)}, bf16[1024,384]{1,0:T(8,128)(2,1)}) custom-call(s32[6]{0:T(128)S(1)} %stack.50.sc, bf16[1024,512]{1,0:T(8,128)(2,1)S(1)} %copy-done, bf16[512,512]{1,0:T(8,128)(2,1)} %collective-permute-done.10.x1.g1, bf16[512,512]{1,0:T(8,128)(2,1)} %collective-permute-done.14.x2.g2, ...), custom_call_target="tpu_custom_call" | custom-call | flops 3221225472 | bytes 10485760 | tf_op jit(solution)/shard_map/pallas_call | solution.py:135
  152.2 10.1 %collective-permute-done.16.got_u = bf16[1024,384]{1,0:T(8,128)(2,1)S(1)} collective-permute-done((bf16[1024,384]{1,0:T(8,128)(2,1)S(1)}, bf16[1024,384]{1,0:T(8,128)(2,1)S(1)}, u32[]{:S(2)}, u32[]{:S(2)}) %collective-permute-start.16) | collective-permute-done | bytes 786464 | tf_op jit(solution)/shard_map/ppermute | solution.py:399
  162.3 7.5 %shard_map.113 = (bf16[4,2,1,2,192,256]{5,4,3,2,1,0:T(8,128)(2,1)S(1)}, bf16[4,2,1,2,192,256]{5,4,3,2,1,0:T(8,128)(2,1)S(1)}) custom-call(s32[6]{0:T(128)S(1)} %stack.50.sc, f32[8,128]{1,0:T(8,128)S(1)} %bitcast.38, f32[1024,384]{1,0:T(8,128)S(1)} %get-tuple-element.42.own_g, bf16[1024,384]{1,0:T(8,128)(2,1)S(1)} %collective-permute-done.13.got_g, ...), custom_call_target="tpu_custom_call" | custom-call | flops 3221225472 | bytes 14680064 | tf_op jit(solution)/shard_map/pallas_call | solution.py:210
  169.8 1.5 collective-permute-start.21
  171.6 2.7 collective-permute-done.21
  174.4 1.6 add_convert_fusion.1
  176.0 14.6 %collective-permute-done.20.got_b = bf16[1024,384]{1,0:T(8,128)(2,1)S(1)} collective-permute-done((bf16[1024,384]{1,0:T(8,128)(2,1)}, bf16[1024,384]{1,0:T(8,128)(2,1)S(1)}, u32[]{:S(2)}, u32[]{:S(2)}) %collective-permute-start.20) | collective-permute-done | bytes 786464 | tf_op jit(solution)/shard_map/ppermute | solution.py:402
  194.8 16.2 %shard_map.114 = (f32[8,128]{1,0:T(8,128)S(1)}, bf16[1024,768]{1,0:T(8,128)(2,1)}, bf16[4,2,2,2,192,256]{5,4,3,2,1,0:T(8,128)(2,1)}, bf16[4,2,2,2,192,256]{5,4,3,2,1,0:T(8,128)(2,1)}) custom-call(s32[6]{0:T(128)S(1)} %stack.50.sc, f32[8,128]{1,0:T(8,128)S(1)} %bitcast.39, f32[1024,384]{1,0:T(8,128)} %copy-done.19, ...), custom_call_target="tpu_custom_call" | custom-call | flops 6442450944 | bytes 20971520 | tf_op jit(solution)/shard_map/pallas_call | solution.py:272
  212.3 5.3 %collective-permute-done.23 = bf16[4,2,2,2,192,256]{5,4,3,2,1,0:T(8,128)(2,1)} collective-permute-done((bf16[4,2,2,2,192,256]{5,4,3,2,1,0:T(8,128)(2,1)}, bf16[4,2,2,2,192,256]{5,4,3,2,1,0:T(8,128)(2,1)}, u32[]{:S(2)}, u32[]{:S(2)}) %collective-permute-start.23) | collective-permute-done | bytes 3145760 | tf_op jit(solution)/shard_map/ppermute | solution.py:366
  217.6 5.9 %add_convert_fusion = bf16[4,2,2,2,192,256]{5,4,3,2,1,0:T(8,128)(2,1)} fusion(bf16[4,2,2,2,192,256]{5,4,3,2,1,0:T(8,128)(2,1)} %collective-permute-done.23, bf16[4,2,2,2,192,256]{5,4,3,2,1,0:T(8,128)(2,1)} %get-tuple-element.59), kind=kLoop, calls=%fused_computation | loop fusion | flops 6291456 | bytes 9437184 | tf_op jit(solution)/shard_map/convert_element_type | solution.py:367
  224.8 1.7 collective-permute-done.22
  226.5 2.7 collective-permute-start.24
  230.5 1.9 copy-done.3
  232.4 1.4 copy-done.21
  233.8 8.4 %shard_map.115 = (bf16[1024,512]{1,0:T(8,128)(2,1)S(1)}, bf16[1024,512]{1,0:T(8,128)(2,1)S(1)}, bf16[1024,512]{1,0:T(8,128)(2,1)}, bf16[1024,512]{1,0:T(8,128)(2,1)S(1)}) custom-call(s32[6]{0:T(128)S(1)} %stack.50.sc, bf16[1024,768]{1,0:T(8,128)(2,1)S(1)} %copy-done.21, bf16[4,2,2,2,192,256]{5,4,3,2,1,0:T(8,128)(2,1)S(1)} %bitcast.35, ...), custom_call_target="tpu_custom_call" | custom-call | flops 3221225472 | bytes 14680064 | tf_op jit(solution)/shard_map/pallas_call | solution.py:325
  242.2 1.6 collective-permute-start.25
  244.9 1.9 collective-permute-start.27
  247.1 1.9 dynamic-slice_bitcast_fusion.3
  249.0 2.7 collective-permute-start.29
  251.7 2.8 collective-permute-start.30
  255.1 30.5 %reduce-scatter.3.cloned.1.call-done = bf16[1,2,2,2,192,256]{5,4,3,2,1,0:T(8,128)(2,1)} async-done(((bf16[4,2,2,2,192,256]{5,4,3,2,1,0:T(8,128)(2,1)}), bf16[1,2,2,2,192,256]{5,4,3,2,1,0:T(8,128)(2,1)}) %reduce-scatter.3.cloned.1.call-update) | async-done | bytes 786448 | tf_op jit(solution)/shard_map/reduce_scatter | solution.py:379
  286.8 2.3 collective-permute-start.31
  289.2 4.2 %collective-permute-start.32 = (bf16[2,2,192,256]{3,2,1,0:T(8,128)(2,1)S(1)}, bf16[2,2,192,256]{3,2,1,0:T(8,128)(2,1)S(1)}, u32[]{:S(2)}, u32[]{:S(2)}) collective-permute-start(bf16[2,2,192,256]{3,2,1,0:T(8,128)(2,1)S(1)} %get-tuple-element.78), channel_id=1, source_target_pairs={{0,2},{2,0},{4,6},{6,4},{8,66},{10,64},{12,70},{14,68},{64,10},{66... | collective-permute-start | bytes 1179656 | tf_op jit(solution)/shard_map/ppermute | solution.py:374
  293.3 1.7 fusion
  295.1 3.4 %add_convert_fusion.2 = bf16[1024,512]{1,0:T(8,128)(2,1)} fusion(bf16[1024,512]{1,0:T(8,128)(2,1)} %collective-permute-done.27, bf16[1024,512]{1,0:T(8,128)(2,1)} %collective-permute-done.26, bf16[1024,512]{1,0:T(8,128)(2,1)} %collective-permute-done.25, bf16[1024,512]{1,0:T(8,128)(2,1)S(1)} %get-tuple-element.66), kind=kLoop, calls=%fused_computation.2 | loop fusion | flops 4194304 | bytes 5242880 | tf_op jit(solution)/shard_map/convert_element_type | solution.py:424
  298.5 2.8 collective-permute-done.31
  301.2 9.3 %collective-permute-done.32 = bf16[2,2,192,256]{3,2,1,0:T(8,128)(2,1)S(1)} collective-permute-done((bf16[2,2,192,256]{3,2,1,0:T(8,128)(2,1)S(1)}, bf16[2,2,192,256]{3,2,1,0:T(8,128)(2,1)S(1)}, u32[]{:S(2)}, u32[]{:S(2)}) %collective-permute-start.32) | collective-permute-done | bytes 393248 | tf_op jit(solution)/shard_map/ppermute | solution.py:374
  (102 shorter events, 31.8 us)
Async XLA Ops:
  7.2 76.6 %all-gather.5.cloned.1.call-start = ((), (), s32[]{:S(2)}) async-start(), calls=%async_computation.4 | async-start | bytes 3932160 | tf_op jit(solution)/shard_map/all_gather | solution.py:361
  8.3 53.0 %copy-start = (bf16[1024,512]{1,0:T(8,128)(2,1)S(1)}, bf16[1024,512]{1,0:T(8,128)(2,1)}, u32[]{:S(2)}) copy-start(bf16[1024,512]{1,0:T(8,128)(2,1)} %g0) | copy-start | bytes 3145732
  8.3 25.7 %collective-permute-start.7 = (bf16[2,2,192,256]{3,2,1,0:T(8,128)(2,1)S(1)}, bf16[2,2,192,256]{3,2,1,0:T(8,128)(2,1)S(1)}, u32[]{:S(2)}, u32[]{:S(2)}) collective-permute-start(bf16[2,2,192,256]{3,2,1,0:T(8,128)(2,1)S(1)} %pad_maximum_fusion.1), channel_id=1, source_target_pairs={{0,2},{2,0},{4,6},{6,4},{8,66},{10,64},{12,70},{14,68},{64,10},{66... | collective-permute-start | bytes 1179656 | tf_op jit(solution)/shard_map/ppermute | solution.py:356
  12.9 21.1 %collective-permute-start.6 = (bf16[2,2,192,256]{3,2,1,0:T(8,128)(2,1)S(1)}, bf16[2,2,192,256]{3,2,1,0:T(8,128)(2,1)S(1)}, u32[]{:S(2)}, u32[]{:S(2)}) collective-permute-start(bf16[2,2,192,256]{3,2,1,0:T(8,128)(2,1)S(1)} %pad_maximum_fusion.1), channel_id=1, source_target_pairs={{0,0},{2,2},{4,4},{6,6},{8,64},{10,66},{12,68},{14,70},{64,8},{66,... | collective-permute-start | bytes 1179656 | tf_op jit(solution)/shard_map/ppermute | solution.py:355
  17.7 17.3 %collective-permute-start = (bf16[512,512]{1,0:T(8,128)(2,1)}, bf16[512,512]{1,0:T(8,128)(2,1)S(1)}, u32[]{:S(2)}, u32[]{:S(2)}) collective-permute-start(bf16[512,512]{1,0:T(8,128)(2,1)} %get-tuple-element.74), channel_id=1, source_target_pairs={{0,16},{16,32},{32,48},{48,0},{1,17},{17,33},{33,49},{49,1},{2,18}... | collective-permute-start | bytes 1572872 | tf_op jit(solution)/shard_map/ppermute | solution.py:345
  19.0 16.0 %collective-permute-start.2 = (bf16[512,512]{1,0:T(8,128)(2,1)}, bf16[512,512]{1,0:T(8,128)(2,1)S(1)}, u32[]{:S(2)}, u32[]{:S(2)}) collective-permute-start(bf16[512,512]{1,0:T(8,128)(2,1)} %get-tuple-element.74), channel_id=1, source_target_pairs={{0,48},{16,0},{32,16},{48,32},{1,49},{17,1},{33,17},{49,33},{2,50}... | collective-permute-start | bytes 1572872 | tf_op jit(solution)/shard_map/ppermute | solution.py:345
  34.9 49.7 %copy-start.23 = (s32[1,2]{1,0:T(1,128)S(1)}, s32[1,2]{1,0:T(1,128)}, u32[]{:S(2)}) copy-start(s32[1,2]{1,0:T(1,128)} %param.10) | copy-start | bytes 28
  34.9 78.3 %copy-start.1 = (bf16[1024,512]{1,0:T(8,128)(2,1)S(1)}, bf16[1024,512]{1,0:T(8,128)(2,1)}, u32[]{:S(2)}) copy-start(bf16[1024,512]{1,0:T(8,128)(2,1)} %x0.6) | copy-start | bytes 3145732
  35.0 89.2 %copy-start.5 = (bf16[512,512]{1,0:T(8,128)(2,1)}, bf16[512,512]{1,0:T(8,128)(2,1)S(1)}, u32[]{:S(2)}) copy-start(bf16[512,512]{1,0:T(8,128)(2,1)S(1)} %collective-permute-done.2.x3) | copy-start | bytes 1572868
  35.0 77.6 %all-gather.7.cloned.1.call-start = ((), (), s32[]{:S(2)}) async-start(), calls=%async_computation.5 | async-start | bytes 1966080 | tf_op jit(solution)/shard_map/all_gather | solution.py:361
  35.0 13.1 %collective-permute-start.3 = (bf16[512,512]{1,0:T(8,128)(2,1)}, bf16[512,512]{1,0:T(8,128)(2,1)S(1)}, u32[]{:S(2)}, u32[]{:S(2)}) collective-permute-start(bf16[512,512]{1,0:T(8,128)(2,1)} %get-tuple-element.73), channel_id=1, source_target_pairs={{0,48},{16,0},{32,16},{48,32},{1,49},{17,1},{33,17},{49,33},{2,50}... | collective-permute-start | bytes 1572872 | tf_op jit(solution)/shard_map/ppermute | solution.py:346
  37.8 14.4 %collective-permute-start.4 = (bf16[512,512]{1,0:T(8,128)(2,1)S(1)}, bf16[512,512]{1,0:T(8,128)(2,1)S(1)}, u32[]{:S(2)}, u32[]{:S(2)}) collective-permute-start(bf16[512,512]{1,0:T(8,128)(2,1)S(1)} %collective-permute-done.x1), channel_id=1, source_target_pairs={{0,16},{16,32},{32,48},{48,0},{1,17},{17,33},{33,49},{49,1},{2,18}... | collective-permute-start | bytes 1572872 | tf_op jit(solution)/shard_map/ppermute | solution.py:351
  48.1 12.3 %collective-permute-start.5 = (bf16[512,512]{1,0:T(8,128)(2,1)S(1)}, bf16[512,512]{1,0:T(8,128)(2,1)S(1)}, u32[]{:S(2)}, u32[]{:S(2)}) collective-permute-start(bf16[512,512]{1,0:T(8,128)(2,1)S(1)} %collective-permute-done.3.x4), channel_id=1, source_target_pairs={{0,48},{16,0},{32,16},{48,32},{1,49},{17,1},{33,17},{49,33},{2,50}... | collective-permute-start | bytes 1572872 | tf_op jit(solution)/shard_map/ppermute | solution.py:351
  52.2 29.5 %collective-permute-start.1 = (bf16[512,512]{1,0:T(8,128)(2,1)}, bf16[512,512]{1,0:T(8,128)(2,1)}, u32[]{:S(2)}, u32[]{:S(2)}) collective-permute-start(bf16[512,512]{1,0:T(8,128)(2,1)} %get-tuple-element.73), channel_id=1, source_target_pairs={{0,16},{16,32},{32,48},{48,0},{1,17},{17,33},{33,49},{49,1},{2,18}... | collective-permute-start | bytes 1572872 | tf_op jit(solution)/shard_map/ppermute | solution.py:346
  62.3 19.4 %collective-permute-start.10 = (bf16[512,512]{1,0:T(8,128)(2,1)}, bf16[512,512]{1,0:T(8,128)(2,1)}, u32[]{:S(2)}, u32[]{:S(2)}) collective-permute-start(bf16[512,512]{1,0:T(8,128)(2,1)} %get-tuple-element.72), channel_id=1, source_target_pairs={{0,16},{16,32},{32,48},{48,0},{1,17},{17,33},{33,49},{49,1},{2,18}... | collective-permute-start | bytes 1572872 | tf_op jit(solution)/shard_map/ppermute | solution.py:345
  62.3 19.4 %collective-permute-start.11 = (bf16[512,512]{1,0:T(8,128)(2,1)}, bf16[512,512]{1,0:T(8,128)(2,1)}, u32[]{:S(2)}, u32[]{:S(2)}) collective-permute-start(bf16[512,512]{1,0:T(8,128)(2,1)} %get-tuple-element.72), channel_id=1, source_target_pairs={{0,48},{16,0},{32,16},{48,32},{1,49},{17,1},{33,17},{49,33},{2,50}... | collective-permute-start | bytes 1572872 | tf_op jit(solution)/shard_map/ppermute | solution.py:345
  65.8 9.2 %collective-permute-start.8 = (bf16[1,2,192,256]{3,2,1,0:T(8,128)(2,1)}, bf16[1,2,192,256]{3,2,1,0:T(8,128)(2,1)S(1)}, u32[]{:S(2)}, u32[]{:S(2)}) collective-permute-start(bf16[1,2,192,256]{3,2,1,0:T(8,128)(2,1)} %bitcast.48), channel_id=1, source_target_pairs={{0,0},{2,2},{4,4},{6,6},{8,64},{10,66},{12,68},{14,70},{64,8},{66,... | collective-permute-start | bytes 589832 | tf_op jit(solution)/shard_map/ppermute | solution.py:355
  71.5 9.3 %collective-permute-start.9 = (bf16[1,2,192,256]{3,2,1,0:T(8,128)(2,1)}, bf16[1,2,192,256]{3,2,1,0:T(8,128)(2,1)S(1)}, u32[]{:S(2)}, u32[]{:S(2)}) collective-permute-start(bf16[1,2,192,256]{3,2,1,0:T(8,128)(2,1)} %bitcast.49), channel_id=1, source_target_pairs={{0,2},{2,0},{4,6},{6,4},{8,66},{10,64},{12,70},{14,68},{64,10},{66... | collective-permute-start | bytes 589832 | tf_op jit(solution)/shard_map/ppermute | solution.py:356
  83.8 29.4 %collective-permute-start.12 = (bf16[4,2,2,2,192,256]{5,4,3,2,1,0:T(8,128)(2,1)}, bf16[4,2,2,2,192,256]{5,4,3,2,1,0:T(8,128)(2,1)}, u32[]{:S(2)}, u32[]{:S(2)}) collective-permute-start(bf16[4,2,2,2,192,256]{5,4,3,2,1,0:T(8,128)(2,1)} %bitcast.32), channel_id=1, source_target_pairs={{0,1},{1,0},{2,3},{3,2},{4,5},{5,4},{6,7},{7,6},{8,9},{9,8},{10,11... | collective-permute-start | bytes 9437192 | tf_op jit(solution)/shard_map/ppermute | solution.py:362
  84.6 162.5 %reduce-scatter.5.cloned.1.call-start = ((), (), s32[]{:S(2)}) async-start(), calls=%async_computation.3 | async-start | bytes 1966080 | tf_op jit(solution)/shard_map/reduce_scatter | solution.py:379
  87.3 37.3 %collective-permute-start.14 = (bf16[512,512]{1,0:T(8,128)(2,1)}, bf16[512,512]{1,0:T(8,128)(2,1)}, u32[]{:S(2)}, u32[]{:S(2)}) collective-permute-start(bf16[512,512]{1,0:T(8,128)(2,1)} %get-tuple-element.71), channel_id=1, source_target_pairs={{0,16},{16,32},{32,48},{48,0},{1,17},{17,33},{33,49},{49,1},{2,18}... | collective-permute-start | bytes 1572872 | tf_op jit(solution)/shard_map/ppermute | solution.py:346
  88.4 36.2 %collective-permute-start.15 = (bf16[512,512]{1,0:T(8,128)(2,1)}, bf16[512,512]{1,0:T(8,128)(2,1)}, u32[]{:S(2)}, u32[]{:S(2)}) collective-permute-start(bf16[512,512]{1,0:T(8,128)(2,1)} %get-tuple-element.71), channel_id=1, source_target_pairs={{0,48},{16,0},{32,16},{48,32},{1,49},{17,1},{33,17},{49,33},{2,50}... | collective-permute-start | bytes 1572872 | tf_op jit(solution)/shard_map/ppermute | solution.py:346
  112.5 31.5 %collective-permute-start.19 = (bf16[4,2,1,2,192,256]{5,4,3,2,1,0:T(8,128)(2,1)}, bf16[4,2,1,2,192,256]{5,4,3,2,1,0:T(8,128)(2,1)S(1)}, u32[]{:S(2)}, u32[]{:S(2)}) collective-permute-start(bf16[4,2,1,2,192,256]{5,4,3,2,1,0:T(8,128)(2,1)} %bitcast.36), channel_id=1, source_target_pairs={{0,1},{1,0},{2,3},{3,2},{4,5},{5,4},{6,7},{7,6},{8,9},{9,8},{10,11... | collective-permute-start | bytes 4718600 | tf_op jit(solution)/shard_map/ppermute | solution.py:362
  113.2 1.9 copy-start.2
  118.2 9.0 %copy-start.10 = (bf16[512,512]{1,0:T(8,128)(2,1)S(1)}, bf16[512,512]{1,0:T(8,128)(2,1)}, u32[]{:S(2)}) copy-start(bf16[512,512]{1,0:T(8,128)(2,1)} %copy-done.8) | copy-start | bytes 1572868
  124.2 38.1 %copy-start.19 = (f32[1024,384]{1,0:T(8,128)}, f32[1024,384]{1,0:T(8,128)S(1)}, u32[]{:S(2)}) copy-start(f32[1024,384]{1,0:T(8,128)S(1)} %get-tuple-element.42.own_g) | copy-start | bytes 4718596
  124.2 19.8 %copy-start.4 = (bf16[8,1,2,192,256]{4,3,2,1,0:T(8,128)(2,1)S(1)}, bf16[8,1,2,192,256]{4,3,2,1,0:T(8,128)(2,1)}, u32[]{:S(2)}) copy-start(bf16[8,1,2,192,256]{4,3,2,1,0:T(8,128)(2,1)} %all-gather.7.cloned.1.call-done) | copy-start | bytes 4718596
  124.2 19.5 %collective-permute-start.13 = (bf16[1024,384]{1,0:T(8,128)(2,1)S(1)}, bf16[1024,384]{1,0:T(8,128)(2,1)S(1)}, u32[]{:S(2)}, u32[]{:S(2)}) collective-permute-start(bf16[1024,384]{1,0:T(8,128)(2,1)S(1)} %get-tuple-element.43), channel_id=1, source_target_pairs={{0,64},{64,0},{1,65},{65,1},{2,66},{66,2},{3,67},{67,3},{4,68},{68... | collective-permute-start | bytes 2359304 | tf_op jit(solution)/shard_map/ppermute | solution.py:397
  124.6 19.4 %collective-permute-start.17 = (bf16[512,512]{1,0:T(8,128)(2,1)}, bf16[512,512]{1,0:T(8,128)(2,1)S(1)}, u32[]{:S(2)}, u32[]{:S(2)}) collective-permute-start(bf16[512,512]{1,0:T(8,128)(2,1)} %collective-permute-done.10.x1.g1), channel_id=1, source_target_pairs={{0,16},{16,32},{32,48},{48,0},{1,17},{17,33},{33,49},{49,1},{2,18}... | collective-permute-start | bytes 1572872 | tf_op jit(solution)/shard_map/ppermute | solution.py:351
  125.8 18.2 %collective-permute-start.18 = (bf16[512,512]{1,0:T(8,128)(2,1)}, bf16[512,512]{1,0:T(8,128)(2,1)S(1)}, u32[]{:S(2)}, u32[]{:S(2)}) collective-permute-start(bf16[512,512]{1,0:T(8,128)(2,1)} %collective-permute-done.15.x4.g4), channel_id=1, source_target_pairs={{0,48},{16,0},{32,16},{48,32},{1,49},{17,1},{33,17},{49,33},{2,50}... | collective-permute-start | bytes 1572872 | tf_op jit(solution)/shard_map/ppermute | solution.py:351
  134.3 28.0 %copy-start.20 = (f32[1024,384]{1,0:T(8,128)}, f32[1024,384]{1,0:T(8,128)S(1)}, u32[]{:S(2)}) copy-start(f32[1024,384]{1,0:T(8,128)S(1)} %get-tuple-element.45.own_u) | copy-start | bytes 4718596
  143.7 18.6 %copy-start.18 = (f32[1024]{0:T(1024)S(1)}, f32[1024]{0:T(1024)}, u32[]{:S(2)}) copy-start(f32[1024]{0:T(1024)} %param.9) | copy-start | bytes 12292
  143.7 18.6 %collective-permute-start.16 = (bf16[1024,384]{1,0:T(8,128)(2,1)S(1)}, bf16[1024,384]{1,0:T(8,128)(2,1)S(1)}, u32[]{:S(2)}, u32[]{:S(2)}) collective-permute-start(bf16[1024,384]{1,0:T(8,128)(2,1)S(1)} %get-tuple-element.47), channel_id=1, source_target_pairs={{0,64},{64,0},{1,65},{65,1},{2,66},{66,2},{3,67},{67,3},{4,68},{68... | collective-permute-start | bytes 2359304 | tf_op jit(solution)/shard_map/ppermute | solution.py:399
  169.8 4.5 %collective-permute-start.21 = (bf16[4,2,1,2,192,256]{5,4,3,2,1,0:T(8,128)(2,1)S(1)}, bf16[4,2,1,2,192,256]{5,4,3,2,1,0:T(8,128)(2,1)S(1)}, u32[]{:S(2)}, u32[]{:S(2)}) collective-permute-start(bf16[4,2,1,2,192,256]{5,4,3,2,1,0:T(8,128)(2,1)S(1)} %get-tuple-element.55), channel_id=1, source_target_pairs={{0,1},{1,0},{2,3},{3,2},{4,5},{5,4},{6,7},{7,6},{8,9},{9,8},{10,11... | collective-permute-start | bytes 4718600 | tf_op jit(solution)/shard_map/ppermute | solution.py:366
  171.3 19.3 %collective-permute-start.20 = (bf16[1024,384]{1,0:T(8,128)(2,1)}, bf16[1024,384]{1,0:T(8,128)(2,1)S(1)}, u32[]{:S(2)}, u32[]{:S(2)}) collective-permute-start(bf16[1024,384]{1,0:T(8,128)(2,1)} %get-tuple-element.52), channel_id=1, source_target_pairs={{0,64},{64,0},{1,65},{65,1},{2,66},{66,2},{3,67},{67,3},{4,68},{68... | collective-permute-start | bytes 2359304 | tf_op jit(solution)/shard_map/ppermute | solution.py:402
  211.0 6.6 %collective-permute-start.23 = (bf16[4,2,2,2,192,256]{5,4,3,2,1,0:T(8,128)(2,1)}, bf16[4,2,2,2,192,256]{5,4,3,2,1,0:T(8,128)(2,1)}, u32[]{:S(2)}, u32[]{:S(2)}) collective-permute-start(bf16[4,2,2,2,192,256]{5,4,3,2,1,0:T(8,128)(2,1)} %get-tuple-element.60), channel_id=1, source_target_pairs={{0,1},{1,0},{2,3},{3,2},{4,5},{5,4},{6,7},{7,6},{8,9},{9,8},{10,11... | collective-permute-start | bytes 9437192 | tf_op jit(solution)/shard_map/ppermute | solution.py:366
  212.0 73.7 %reduce-scatter.3.cloned.1.call-start = ((), (), s32[]{:S(2)}) async-start(), calls=%async_computation.2 | async-start | bytes 3932160 | tf_op jit(solution)/shard_map/reduce_scatter | solution.py:379
  223.5 2.9 collective-permute-start.22
  226.5 4.0 %collective-permute-start.24 = (f32[8,128]{1,0:T(8,128)S(1)}, f32[8,128]{1,0:T(8,128)S(1)}, u32[]{:S(2)}, u32[]{:S(2)}) collective-permute-start(f32[8,128]{1,0:T(8,128)S(1)} %add.51), channel_id=1, source_target_pairs={{0,32},{16,48},{32,0},{48,16},{1,33},{17,49},{33,1},{49,17},{2,34}... | collective-permute-start | bytes 12296 | tf_op jit(solution)/shard_map/ppermute | solution.py:416
  230.5 1.9 copy-start.3
  242.2 52.9 %collective-permute-start.25 = (bf16[1024,512]{1,0:T(8,128)(2,1)}, bf16[1024,512]{1,0:T(8,128)(2,1)}, u32[]{:S(2)}, u32[]{:S(2)}) collective-permute-start(bf16[1024,512]{1,0:T(8,128)(2,1)} %get-tuple-element.67), channel_id=1, source_target_pairs={{0,16},{16,32},{32,48},{48,0},{1,17},{17,33},{33,49},{49,1},{2,18}... | collective-permute-start | bytes 3145736 | tf_op jit(solution)/shard_map/ppermute | solution.py:419
  243.8 51.2 %collective-permute-start.26 = (bf16[1024,512]{1,0:T(8,128)(2,1)S(1)}, bf16[1024,512]{1,0:T(8,128)(2,1)}, u32[]{:S(2)}, u32[]{:S(2)}) collective-permute-start(bf16[1024,512]{1,0:T(8,128)(2,1)S(1)} %get-tuple-element.68), channel_id=1, source_target_pairs={{0,48},{16,0},{32,16},{48,32},{1,49},{17,1},{33,17},{49,33},{2,50}... | collective-permute-start | bytes 3145736 | tf_op jit(solution)/shard_map/ppermute | solution.py:420
  244.9 50.1 %collective-permute-start.27 = (bf16[1024,512]{1,0:T(8,128)(2,1)S(1)}, bf16[1024,512]{1,0:T(8,128)(2,1)}, u32[]{:S(2)}, u32[]{:S(2)}) collective-permute-start(bf16[1024,512]{1,0:T(8,128)(2,1)S(1)} %get-tuple-element.69), channel_id=1, source_target_pairs={{0,32},{16,48},{32,0},{48,16},{1,33},{17,49},{33,1},{49,17},{2,34}... | collective-permute-start | bytes 3145736 | tf_op jit(solution)/shard_map/ppermute | solution.py:421
  246.8 4.9 %collective-permute-start.28 = (f32[8,128]{1,0:T(8,128)S(1)}, f32[8,128]{1,0:T(8,128)S(1)}, u32[]{:S(2)}, u32[]{:S(2)}) collective-permute-start(f32[8,128]{1,0:T(8,128)S(1)} %add.53), channel_id=1, source_target_pairs={{0,64},{64,0},{1,65},{65,1},{2,66},{66,2},{3,67},{67,3},{4,68},{68... | collective-permute-start | bytes 12296 | tf_op jit(solution)/shard_map/ppermute | solution.py:418
  249.0 37.8 %collective-permute-start.29 = (bf16[1,2,192,256]{3,2,1,0:T(8,128)(2,1)}, bf16[1,2,192,256]{3,2,1,0:T(8,128)(2,1)S(1)}, u32[]{:S(2)}, u32[]{:S(2)}) collective-permute-start(bf16[1,2,192,256]{3,2,1,0:T(8,128)(2,1)} %get-tuple-element.79), channel_id=1, source_target_pairs={{0,0},{2,2},{4,4},{6,6},{8,64},{10,66},{12,68},{14,70},{64,8},{66,... | collective-permute-start | bytes 589832 | tf_op jit(solution)/shard_map/ppermute | solution.py:373
  251.7 37.5 %collective-permute-start.30 = (bf16[1,2,192,256]{3,2,1,0:T(8,128)(2,1)S(1)}, bf16[1,2,192,256]{3,2,1,0:T(8,128)(2,1)}, u32[]{:S(2)}, u32[]{:S(2)}) collective-permute-start(bf16[1,2,192,256]{3,2,1,0:T(8,128)(2,1)S(1)} %get-tuple-element.80), channel_id=1, source_target_pairs={{0,2},{2,0},{4,6},{6,4},{8,66},{10,64},{12,70},{14,68},{64,10},{66... | collective-permute-start | bytes 589832 | tf_op jit(solution)/shard_map/ppermute | solution.py:374
  286.8 14.4 %collective-permute-start.31 = (bf16[2,2,192,256]{3,2,1,0:T(8,128)(2,1)S(1)}, bf16[2,2,192,256]{3,2,1,0:T(8,128)(2,1)S(1)}, u32[]{:S(2)}, u32[]{:S(2)}) collective-permute-start(bf16[2,2,192,256]{3,2,1,0:T(8,128)(2,1)S(1)} %get-tuple-element.77), channel_id=1, source_target_pairs={{0,0},{2,2},{4,4},{6,6},{8,64},{10,66},{12,68},{14,70},{64,8},{66,... | collective-permute-start | bytes 1179656 | tf_op jit(solution)/shard_map/ppermute | solution.py:373
  289.2 21.4 %collective-permute-start.32 = (bf16[2,2,192,256]{3,2,1,0:T(8,128)(2,1)S(1)}, bf16[2,2,192,256]{3,2,1,0:T(8,128)(2,1)S(1)}, u32[]{:S(2)}, u32[]{:S(2)}) collective-permute-start(bf16[2,2,192,256]{3,2,1,0:T(8,128)(2,1)S(1)} %get-tuple-element.78), channel_id=1, source_target_pairs={{0,2},{2,0},{4,6},{6,4},{8,66},{10,64},{12,70},{14,68},{64,10},{66... | collective-permute-start | bytes 1179656 | tf_op jit(solution)/shard_map/ppermute | solution.py:374
  (13 other events, 13.4 us)
Sparse Core Ops, SparseCore 0:
  35.1 48.6 all-gather.4
  86.0 26.4 all-gather.6
  212.1 23.9 reduce-scatter.4
  238.4 47.2 reduce-scatter.2

commit v4 on v3

--- a/solution.py
+++ b/solution.py
@@ -1,5 +1,3 @@
-import functools
-
 import jax
 import jax.numpy as jnp
 from jax import lax
@@ -12,6 +10,7 @@
 BLOCK = 128
 TILE = 256
 HID = 192
+VMEM = 28 << 20
 COLS = 256
 BF = jnp.bfloat16
 F32 = jnp.float32
@@ -64,7 +63,7 @@
     return copies
 
 
-def load_weight(sc, pair, w, row, dst, sem, at_sem):
+def load_weight(sc, pair, row, dst, sem, at_sem):
     copies = []
     for c, ref in enumerate(pair):
         core = sc[CORE] if c == 0 else 1 - sc[CORE]
@@ -74,7 +73,7 @@
                 cb = slot % 2 * 4 + xh * 2 + core
                 copies.append(
                     pltpu.make_async_copy(
-                        ref.at[slot, flip, w],
+                        ref.at[slot, flip],
                         dst.at[:, pl.ds(row + slot // 2 * HID, HID), aligned(cb, COLS)],
                         sem.at[at_sem + c * 8 + slot * 2 + flip],
                     )
@@ -111,10 +110,10 @@
         c.wait()
 
 
-def pre_kernel(w, sc, x0, x1, x2, x3, x4, x5, x6, w0, w1, own, send, xv, wv, xsem, wsem):
+def pre_kernel(sc, x0, x1, x2, x3, x4, x5, x6, w0, w1, own, send, xv, wv, xsem, wsem):
     wait_all(
         start_all(
-            load_weight(sc, (w0, w1), w, 0, wv, wsem, 0) + load_rows(sc, (x0, x1, x2, x3, x4, x5, x6), xv, xsem)
+            load_weight(sc, (w0, w1), 0, wv, wsem, 0) + load_rows(sc, (x0, x1, x2, x3, x4, x5, x6), xv, xsem)
         )
     )
 
@@ -129,11 +128,11 @@
         by_tile(sc, t, work)
 
 
-def pre_part(sc, pieces, weight, w):
+def pre_part(sc, pieces, weight):
     rows, width = pieces[0].shape
     wide, n = 4 * width, 2 * HID
     return pl.pallas_call(
-        functools.partial(pre_kernel, w),
+        pre_kernel,
         out_shape=(jax.ShapeDtypeStruct((rows, n), F32), jax.ShapeDtypeStruct((rows, n), BF)),
         in_specs=[SM] + [ANY] * 9,
         out_specs=(VM, VM),
@@ -143,7 +142,7 @@
             pltpu.SemaphoreType.DMA((7,)),
             pltpu.SemaphoreType.DMA((16,)),
         ],
-        compiler_params=pltpu.CompilerParams(vmem_limit_bytes=32 << 20),
+        compiler_params=pltpu.CompilerParams(vmem_limit_bytes=VMEM),
         cost_estimate=pl.CostEstimate(
             flops=4 * rows * n * wide, bytes_accessed=10 << 20, transcendentals=0
         ),
@@ -219,7 +218,7 @@
             pltpu.SemaphoreType.DMA((7,)),
             pltpu.SemaphoreType.DMA((32,)),
         ],
-        compiler_params=pltpu.CompilerParams(vmem_limit_bytes=40 << 20),
+        compiler_params=pltpu.CompilerParams(vmem_limit_bytes=VMEM),
         cost_estimate=pl.CostEstimate(
             flops=8 * rows * HID * 4 * width, bytes_accessed=14 << 20, transcendentals=rows * 384
         ),
@@ -286,19 +285,19 @@
             pltpu.SemaphoreType.DMA((7,)),
             pltpu.SemaphoreType.DMA((64,)),
         ],
-        compiler_params=pltpu.CompilerParams(vmem_limit_bytes=48 << 20),
+        compiler_params=pltpu.CompilerParams(vmem_limit_bytes=VMEM),
         cost_estimate=pl.CostEstimate(
             flops=16 * rows * HID * 4 * width, bytes_accessed=20 << 20, transcendentals=rows * 384
         ),
     )(sc, scores, own_g, got_g, own_u, got_u, own_b, got_b, *feats)
 
 
-def rows_kernel(sc, gu, w0, w1, d0, d1, d2, d3, wv, dxv, wsem, osem):
+def rows_kernel(sc, gu, g0, g1, u0, u1, d0, d1, d2, d3, wv, dxv, wsem, osem):
     rows, wide = dxv.shape
     width = wide // 4
     wait_all(
         start_all(
-            load_weight(sc, (w0, w1), 0, 0, wv, wsem, 0) + load_weight(sc, (w0, w1), 1, 2 * HID, wv, wsem, 16)
+            load_weight(sc, (g0, g1), 0, wv, wsem, 0) + load_weight(sc, (u0, u1), 2 * HID, wv, wsem, 16)
         )
     )
 
@@ -320,12 +319,12 @@
     )
 
 
-def rows_part(sc, gu, weight):
+def rows_part(sc, gu, w_gate, w_up):
     rows, width = gu.shape[0], 512
     return pl.pallas_call(
         rows_kernel,
         out_shape=(jax.ShapeDtypeStruct((rows, width), BF),) * 4,
-        in_specs=[SM, VM] + [ANY] * 2,
+        in_specs=[SM, VM] + [ANY] * 4,
         out_specs=(ANY,) * 4,
         scratch_shapes=[
             pltpu.VMEM((EXP, 4 * HID, 4 * width), BF),
@@ -333,11 +332,11 @@
             pltpu.SemaphoreType.DMA((32,)),
             pltpu.SemaphoreType.DMA((4,)),
         ],
-        compiler_params=pltpu.CompilerParams(vmem_limit_bytes=32 << 20),
+        compiler_params=pltpu.CompilerParams(vmem_limit_bytes=VMEM),
         cost_estimate=pl.CostEstimate(
             flops=8 * rows * HID * 4 * width, bytes_accessed=14 << 20, transcendentals=0
         ),
-    )(sc, gu, *weight)
+    )(sc, gu, *w_gate, *w_up)
 
 
 def halves_over(x):
@@ -351,10 +350,11 @@
     return lax.ppermute(pieces[1], "y", ring(4, 1)), lax.ppermute(pieces[4], "y", ring(4, 3))
 
 
-def plane_pair(w):
-    straight = lax.ppermute(w, ("xl", "z", "xh"), swap_pairs(0))
-    crossed = lax.ppermute(w, ("xl", "z", "xh"), swap_pairs(1))
-    return jnp.stack([straight, crossed])
+def to_plane(w):
+    return (
+        lax.ppermute(w, ("xl", "z", "xh"), swap_pairs(0)),
+        lax.ppermute(w, ("xl", "z", "xh"), swap_pairs(1)),
+    )
 
 
 def spread_pair(pair, *before):
@@ -362,8 +362,7 @@
     return here, lax.ppermute(here, "core", ring(2, 1))
 
 
-def over_cores(keep, away):
-    got = lax.ppermute(away, "core", ring(2, 1))
+def over_cores(keep, got):
     return (keep.astype(F32) + got.astype(F32)).astype(BF)
 
 
@@ -387,32 +386,33 @@
 
     feats = halves_over(features)
     feats += opposite_over(feats)
-    pair_gu = after(plane_pair(jnp.stack([w_gate, w_up])), feats[1], feats[3])
-    pair_d = plane_pair(after(w_down, pair_gu)[None])
+    pair_g = after(jnp.stack(to_plane(w_gate)), feats[1], feats[3])
+    straight, crossed = to_plane(after(jnp.stack([w_up, w_down]), pair_g))
+    pair_u, pair_d = (jnp.stack([straight[i], crossed[i]]) for i in range(2))
     grads = halves_over(after(grad_out, feats[5], feats[6]))
-    w_gu = spread_pair(pair_gu, feats[2], feats[4], pair_d, grads[1], grads[3])
-    w_d = spread_pair(pair_d)
-
-    own_g, send_g = pre_part(sc, feats, w_gu, 0)
+    gate_all = spread_pair(pair_g, *feats[1:], pair_u, pair_d)
+
+    own_g, send_g = pre_part(sc, feats, gate_all)
     got_g = lax.ppermute(send_g, "xl", ring(2, 1))
-    own_u, send_u = pre_part(after(sc, send_g, grads[2], grads[4]), feats, w_gu, 1)
-    got_u = lax.ppermute(after(send_u, got_g), "xl", ring(2, 1))
+    up_all = spread_pair(pair_u, send_g, *grads[1:])
+    own_u, send_u = pre_part(after(sc, got_g), feats, up_all)
+    got_u = lax.ppermute(send_u, "xl", ring(2, 1))
     grads += opposite_over(after(grads, send_g))
-    own_b, send_b = pre_part(sc, grads, w_d, 0)
-    got_b = lax.ppermute(after(send_b, got_u), "xl", ring(2, 1))
-
-    both_d = over_cores(
-        *down_part(after(sc, send_b), scores, own_g, got_g, own_u, got_u, grads)
-    )
+    own_b, send_b = pre_part(sc, grads, spread_pair(pair_d, send_u))
+    got_b = lax.ppermute(send_b, "xl", ring(2, 1))
+
+    keep, away = down_part(after(sc, send_b), scores, own_g, got_g, own_u, got_u, grads)
+    both_d = over_cores(keep, lax.ppermute(away, "core", ring(2, 1)))
     part_d = scatter_z(both_d)
     total, gu, keep, away = gate_up_part(
         sc, scores, own_g, got_g, own_u, got_u, own_b, after(got_b, both_d), feats
     )
-    both_gu = over_cores(keep, away)
+    got = lax.ppermute(after(away, part_d), "core", ring(2, 1))
+    total = total + lax.ppermute(total, "y", [(i, i ^ 1) for i in range(4)])
+    both_gu = over_cores(after(keep, total), got)
     part_gu = scatter_z(both_gu)
-    total = total + lax.ppermute(total, "y", [(i, i ^ 1) for i in range(4)])
-
-    dx = rows_part(sc, after(gu, total, both_gu), w_gu)
+
+    dx = rows_part(sc, after(gu, both_gu), gate_all, up_all)
     total = total + lax.ppermute(total, "y", [(i, i ^ 2) for i in range(4)])
     dx, _ = lax.optimization_barrier((dx, total))
     total = total + lax.ppermute(total, "xl", ring(2, 1))

time: 319 us -> 331 us (1.038)
  local copies, waits for them, and re-layouts: 25.8 us -> 40.4 us
  waiting for transfers between devices: 153 us -> 164 us
  starting transfers between devices: 57.1 us -> 47.8 us
    all_gather x2 -> x3, waiting for transfers between devices: 24.7 us -> 0.02 us  [spread_pair(): here = after(lax.all_gather(pair, 'z', axis=0, tiled=False), *before)]
    ppermute x2, waiting for transfers between devices: 0.01 us -> 23.5 us  [opposite_over(): lax.ppermute(pieces[1], 'y', ring(4, 1))]
    unnamed x48 -> x80, local copies, waits for them, and re-layouts: 17.2 us -> 31.9 us
    ppermute x4, waiting for transfers between devices: 10.3 us -> 20.6 us  [halves_over(): rest = [lax.ppermute(x[half:], 'y', ring(4, k)) for k in (1, 3)]]
    ppermute x1, waiting for transfers between devices: 9.44 us -> 19.3 us  [on_device(): got_g = lax.ppermute(send_g, 'xl', ring(2, 1))]
    ppermute x2, waiting for transfers between devices: 7.41 us -> 0.01 us  [opposite_over(): lax.ppermute(pieces[4], 'y', ring(4, 3))]
    ppermute x8, waiting for transfers between devices: 55.2 us -> 47.9 us  [the longest x2 14.8 us: to_plane(): lax.ppermute(w, ('xl', 'z', 'xh'), swap_pairs(0))]
    reduce_scatter x2, waiting for transfers between devices: 30.5 us -> 36 us  [scatter_z(): return lax.psum_scatter(both, 'z', scatter_dimension=0, tiled=False)]
  transfers between devices with their start and end apart: 37 -> 39, of which waited for: 17 -> 17; matrix products, arithmetic and copies ran while one was open for 7% -> 6% of each run, Pallas kernels for 9% -> 8%
where the time goes in v4:
time: 331 us; the launch traced here: 330 us
  waiting for transfers between devices  164 us (50%)
  starting transfers between devices  47.8 us (14%)
  Pallas kernels  47.8 us (14%)
  local copies, waits for them, and re-layouts  40.4 us (12%)
  between operations  15.5 us (5%)
  other arithmetic  14 us (4%)
    reduce_scatter x2, waiting for transfers between devices, scatter_z(): return lax.psum_scatter(both, 'z', scatter_dimension=0, tiled=False)  36 us
    unnamed x80, local copies, waits for them, and re-layouts  31.9 us
    ppermute x2, waiting for transfers between devices, opposite_over(): lax.ppermute(pieces[1], 'y', ring(4, 1))  23.5 us
    ppermute x4, waiting for transfers between devices, halves_over(): rest = [lax.ppermute(x[half:], 'y', ring(4, k)) for k in (1, 3)]  20.6 us
    ppermute x1, waiting for transfers between devices, on_device(): got_g = lax.ppermute(send_g, 'xl', ring(2, 1))  19.3 us
    pallas_call x3, Pallas kernels, pre_part(): pl.pallas_call(pre_kernel, out_shape=(jax.ShapeDtypeStruct((rows, n), F32...  18.7 us
    ppermute x2, waiting for transfers between devices, to_plane(): lax.ppermute(w, ('xl', 'z', 'xh'), swap_pairs(0))  14.8 us
    ppermute x1, waiting for transfers between devices, on_device(): got_b = lax.ppermute(send_b, 'xl', ring(2, 1))  14.6 us
  transfers between devices with their start and end apart: 39, of which 17 were waited for; matrix products, arithmetic and copies ran while one was open for 6% of the time, Pallas kernels for 8%

profile of v4, /device:TPU:3, one launch (start us, length us, event | category | flops | bytes accessed | tf_op | source)
XLA Modules:
  0.0 329.7 jit_solution(1753876968707108581)
XLA Ops:
  7.2 2.2 fusion.2
  10.7 1.4 collective-permute-start.2
  12.2 5.5 %collective-permute-start.6 = (bf16[2,192,256]{2,1,0:T(8,128)(2,1)S(1)}, bf16[2,192,256]{2,1,0:T(8,128)(2,1)S(1)}, u32[]{:S(2)}, u32[]{:S(2)}) collective-permute-start(bf16[2,192,256]{2,1,0:T(8,128)(2,1)S(1)} %copy-done.39), channel_id=1, source_target_pairs={{0,0},{2,2},{4,4},{6,6},{8,64},{10,66},{12,68},{14,70},{64,8},{66,... | collective-permute-start | bytes 589832 | tf_op jit(solution)/shard_map/ppermute | solution.py:355
  18.7 3.0 collective-permute-done.6
  21.7 7.1 %collective-permute-done.7 = bf16[2,192,256]{2,1,0:T(8,128)(2,1)S(1)} collective-permute-done((bf16[2,192,256]{2,1,0:T(8,128)(2,1)S(1)}, bf16[2,192,256]{2,1,0:T(8,128)(2,1)S(1)}, u32[]{:S(2)}, u32[]{:S(2)}) %collective-permute-start.7) | collective-permute-done | bytes 196640 | tf_op jit(solution)/shard_map/ppermute | solution.py:356
  29.7 2.1 collective-permute-start.8
  31.8 3.0 collective-permute-start.9
  36.2 11.8 %collective-permute-done.8 = bf16[2,2,192,256]{3,2,1,0:T(8,128)(2,1)S(1)} collective-permute-done((bf16[2,2,192,256]{3,2,1,0:T(8,128)(2,1)S(1)}, bf16[2,2,192,256]{3,2,1,0:T(8,128)(2,1)S(1)}, u32[]{:S(2)}, u32[]{:S(2)}) %collective-permute-start.8) | collective-permute-done | bytes 393248 | tf_op jit(solution)/shard_map/ppermute | solution.py:355
  48.0 5.6 %collective-permute-done.9 = bf16[2,2,192,256]{3,2,1,0:T(8,128)(2,1)S(1)} collective-permute-done((bf16[2,2,192,256]{3,2,1,0:T(8,128)(2,1)S(1)}, bf16[2,2,192,256]{3,2,1,0:T(8,128)(2,1)S(1)}, u32[]{:S(2)}, u32[]{:S(2)}) %collective-permute-start.9) | collective-permute-done | bytes 393248 | tf_op jit(solution)/shard_map/ppermute | solution.py:356
  55.9 1.5 collective-permute-start.5
  58.2 10.8 %collective-permute-done.1.x2 = bf16[512,512]{1,0:T(8,128)(2,1)} collective-permute-done((bf16[512,512]{1,0:T(8,128)(2,1)}, bf16[512,512]{1,0:T(8,128)(2,1)}, u32[]{:S(2)}, u32[]{:S(2)}) %collective-permute-start.1) | collective-permute-done | bytes 524320 | tf_op jit(solution)/shard_map/ppermute | solution.py:345
  69.0 11.2 %collective-permute-done.4.x5 = bf16[512,512]{1,0:T(8,128)(2,1)} collective-permute-done((bf16[512,512]{1,0:T(8,128)(2,1)S(1)}, bf16[512,512]{1,0:T(8,128)(2,1)}, u32[]{:S(2)}, u32[]{:S(2)}) %collective-permute-start.4) | collective-permute-done | bytes 524320 | tf_op jit(solution)/shard_map/ppermute | solution.py:350
  80.3 1.5 collective-permute-start.10
  82.8 2.7 collective-permute-start.14
  85.5 1.4 collective-permute-start.15
  91.2 6.1 %shard_map.110 = (f32[1024,384]{1,0:T(8,128)S(1)}, bf16[1024,384]{1,0:T(8,128)(2,1)S(1)}) custom-call(s32[6]{0:T(128)S(1)} %stack.47.sc, bf16[1024,512]{1,0:T(8,128)(2,1)S(1)} %copy-done.1, bf16[512,512]{1,0:T(8,128)(2,1)S(1)} %collective-permute-done.x1, bf16[512,512]{1,0:T(8,128)(2,1)} %collective-permute-done.1.x2, ...), custom_call_target="tpu_custom_call" | custom-call | flops 3221225472 | bytes 10485760 | tf_op jit(solution)/shard_map/pallas_call | solution.py:134
  99.3 9.8 %collective-permute-done.13.x2.g2 = bf16[512,512]{1,0:T(8,128)(2,1)} collective-permute-done((bf16[512,512]{1,0:T(8,128)(2,1)}, bf16[512,512]{1,0:T(8,128)(2,1)}, u32[]{:S(2)}, u32[]{:S(2)}) %collective-permute-start.13) | collective-permute-done | bytes 524320 | tf_op jit(solution)/shard_map/ppermute | solution.py:345
  110.0 19.3 %collective-permute-done.11.got_g = bf16[1024,384]{1,0:T(8,128)(2,1)S(1)} collective-permute-done((bf16[1024,384]{1,0:T(8,128)(2,1)}, bf16[1024,384]{1,0:T(8,128)(2,1)S(1)}, u32[]{:S(2)}, u32[]{:S(2)}) %collective-permute-start.11) | collective-permute-done | bytes 786464 | tf_op jit(solution)/shard_map/ppermute | solution.py:396
  129.3 1.7 copy-done.5
  133.1 5.9 %shard_map.111 = (f32[1024,384]{1,0:T(8,128)S(1)}, bf16[1024,384]{1,0:T(8,128)(2,1)S(1)}) custom-call(s32[6]{0:T(128)S(1)} %stack.47.sc, bf16[1024,512]{1,0:T(8,128)(2,1)S(1)} %copy-done.1, bf16[512,512]{1,0:T(8,128)(2,1)S(1)} %copy-done.20, bf16[512,512]{1,0:T(8,128)(2,1)} %collective-permute-done.1.x2, bf16[512,512]{1,0:T(8,128)(2,1)S(1)} %copy-done.23, ...), custom_call_target="tpu_custom_call" | custom-call | flops 3221225472 | bytes 10485760 | tf_op jit(solution)/shard_map/pallas_call | solution.py:134
  144.2 1.9 collective-permute-start.19
  146.1 12.3 %collective-permute-done.18.x5.g5 = bf16[512,512]{1,0:T(8,128)(2,1)S(1)} collective-permute-done((bf16[512,512]{1,0:T(8,128)(2,1)}, bf16[512,512]{1,0:T(8,128)(2,1)S(1)}, u32[]{:S(2)}, u32[]{:S(2)}) %collective-permute-start.18) | collective-permute-done | bytes 524320 | tf_op jit(solution)/shard_map/ppermute | solution.py:350
  159.8 6.7 %shard_map.112 = (f32[1024,384]{1,0:T(8,128)S(1)}, bf16[1024,384]{1,0:T(8,128)(2,1)}) custom-call(s32[6]{0:T(128)S(1)} %stack.47.sc, bf16[1024,512]{1,0:T(8,128)(2,1)S(1)} %copy-done, bf16[512,512]{1,0:T(8,128)(2,1)} %collective-permute-done.12.x1.g1, bf16[512,512]{1,0:T(8,128)(2,1)} %collective-permute-done.13.x2.g2, ...), custom_call_target="tpu_custom_call" | custom-call | flops 3221225472 | bytes 10485760 | tf_op jit(solution)/shard_map/pallas_call | solution.py:134
  167.7 1.7 copy-done.27
  169.4 7.5 %shard_map.113 = (bf16[4,2,1,2,192,256]{5,4,3,2,1,0:T(8,128)(2,1)S(1)}, bf16[4,2,1,2,192,256]{5,4,3,2,1,0:T(8,128)(2,1)S(1)}) custom-call(s32[6]{0:T(128)S(1)} %stack.47.sc, f32[8,128]{1,0:T(8,128)S(1)} %bitcast.38, f32[1024,384]{1,0:T(8,128)S(1)} %copy-done.27, bf16[1024,384]{1,0:T(8,128)(2,1)S(1)} %copy-done.11, f32[1024,384]{1,0:T(8,128)S(1)} %copy-done.30, ...), custom_call_target="tpu_custom_call" | custom-call | flops 3221225472 | bytes 14680064 | tf_op jit(solution)/shard_map/pallas_call | solution.py:209
  178.2 3.0 collective-permute-done.22
  181.2 1.7 add_convert_fusion.1
  182.9 14.6 %collective-permute-done.21.got_b = bf16[1024,384]{1,0:T(8,128)(2,1)S(1)} collective-permute-done((bf16[1024,384]{1,0:T(8,128)(2,1)}, bf16[1024,384]{1,0:T(8,128)(2,1)S(1)}, u32[]{:S(2)}, u32[]{:S(2)}) %collective-permute-start.21) | collective-permute-done | bytes 786464 | tf_op jit(solution)/shard_map/ppermute | solution.py:402
  209.3 13.2 %shard_map.114 = (f32[8,128]{1,0:T(8,128)S(1)}, bf16[1024,768]{1,0:T(8,128)(2,1)S(1)}, bf16[4,2,2,2,192,256]{5,4,3,2,1,0:T(8,128)(2,1)S(1)}, bf16[4,2,2,2,192,256]{5,4,3,2,1,0:T(8,128)(2,1)}) custom-call(s32[6]{0:T(128)S(1)} %stack.47.sc, f32[8,128]{1,0:T(8,128)S(1)} %bitcast.39, f32[1024,384]{1,0:T(8,128)S(1)} %copy-done.28, ...), custom_call_target="tpu_custom_call" | custom-call | flops 6442450944 | bytes 20971520 | tf_op jit(solution)/shard_map/pallas_call | solution.py:271
  225.8 1.5 collective-permute-done.23
  227.3 2.8 collective-permute-done.24
  230.1 4.7 %add_convert_fusion = bf16[4,2,2,2,192,256]{5,4,3,2,1,0:T(8,128)(2,1)} fusion(bf16[4,2,2,2,192,256]{5,4,3,2,1,0:T(8,128)(2,1)} %collective-permute-done.24, bf16[4,2,2,2,192,256]{5,4,3,2,1,0:T(8,128)(2,1)S(1)} %get-tuple-element.61), kind=kLoop, calls=%fused_computation | loop fusion | flops 6291456 | bytes 9437184 | tf_op jit(solution)/shard_map/convert_element_type | solution.py:366
  234.9 2.5 collective-permute-start.25
  237.4 1.5 collective-permute-done.25
  239.0 1.4 copy-done.6
  240.4 1.4 copy-done.8
  241.8 1.4 copy-done.33
  243.2 8.4 %shard_map.115 = (bf16[1024,512]{1,0:T(8,128)(2,1)S(1)}, bf16[1024,512]{1,0:T(8,128)(2,1)}, bf16[1024,512]{1,0:T(8,128)(2,1)}, bf16[1024,512]{1,0:T(8,128)(2,1)}) custom-call(s32[6]{0:T(128)S(1)} %stack.47.sc, bf16[1024,768]{1,0:T(8,128)(2,1)S(1)} %copy-done.33, bf16[4,2,2,192,256]{4,3,2,1,0:T(8,128)(2,1)S(1)} %bitcast.32, ...), custom_call_target="tpu_custom_call" | custom-call | flops 3221225472 | bytes 14680064 | tf_op jit(solution)/shard_map/pallas_call | solution.py:324
  253.0 1.6 collective-permute-start.27
  256.0 1.7 dynamic-slice_bitcast_fusion.3
  257.7 1.9 collective-permute-start.30
  261.2 36.0 %reduce-scatter.3.cloned.1.call-done = bf16[1,2,2,2,192,256]{5,4,3,2,1,0:T(8,128)(2,1)} async-done(((bf16[4,2,2,2,192,256]{5,4,3,2,1,0:T(8,128)(2,1)}), bf16[1,2,2,2,192,256]{5,4,3,2,1,0:T(8,128)(2,1)}) %reduce-scatter.3.cloned.1.call-update) | async-done | bytes 786448 | tf_op jit(solution)/shard_map/reduce_scatter | solution.py:378
  298.5 2.3 collective-permute-start.32
  300.8 3.2 collective-permute-start.33
  304.0 1.7 fusion
  305.7 2.8 add_convert_fusion.2
  308.5 4.4 %collective-permute-done.32 = bf16[2,2,192,256]{3,2,1,0:T(8,128)(2,1)S(1)} collective-permute-done((bf16[2,2,192,256]{3,2,1,0:T(8,128)(2,1)S(1)}, bf16[2,2,192,256]{3,2,1,0:T(8,128)(2,1)S(1)}, u32[]{:S(2)}, u32[]{:S(2)}) %collective-permute-start.32) | collective-permute-done | bytes 393248 | tf_op jit(solution)/shard_map/ppermute | solution.py:372
  312.9 9.3 %collective-permute-done.33 = bf16[2,2,192,256]{3,2,1,0:T(8,128)(2,1)S(1)} collective-permute-done((bf16[2,2,192,256]{3,2,1,0:T(8,128)(2,1)S(1)}, bf16[2,2,192,256]{3,2,1,0:T(8,128)(2,1)S(1)}, u32[]{:S(2)}, u32[]{:S(2)}) %collective-permute-start.33) | collective-permute-done | bytes 393248 | tf_op jit(solution)/shard_map/ppermute | solution.py:373
  (142 shorter events, 47.3 us)
Async XLA Ops:
  7.2 22.5 %copy-start.37 = (bf16[2,192,256]{2,1,0:T(8,128)(2,1)S(1)}, bf16[2,192,256]{2,1,0:T(8,128)(2,1)}, u32[]{:S(2)}) copy-start(bf16[2,192,256]{2,1,0:T(8,128)(2,1)} %param.12) | copy-start | bytes 589828
  7.2 22.5 %copy-start.36 = (bf16[2,192,256]{2,1,0:T(8,128)(2,1)S(1)}, bf16[2,192,256]{2,1,0:T(8,128)(2,1)}, u32[]{:S(2)}) copy-start(bf16[2,192,256]{2,1,0:T(8,128)(2,1)} %param.13) | copy-start | bytes 589828
  7.2 73.1 %all-gather.7.cloned.1.call-start = ((), (), s32[]{:S(2)}) async-start(), calls=%async_computation.4 | async-start | bytes 1966080 | tf_op jit(solution)/shard_map/all_gather | solution.py:361
  9.4 20.1 %collective-permute-start = (bf16[512,512]{1,0:T(8,128)(2,1)S(1)}, bf16[512,512]{1,0:T(8,128)(2,1)S(1)}, u32[]{:S(2)}, u32[]{:S(2)}) collective-permute-start(bf16[512,512]{1,0:T(8,128)(2,1)S(1)} %get-tuple-element.76), channel_id=1, source_target_pairs={{0,16},{16,32},{32,48},{48,0},{1,17},{17,33},{33,49},{49,1},{2,18}... | collective-permute-start | bytes 1572872 | tf_op jit(solution)/shard_map/ppermute | solution.py:344
  10.7 18.8 %collective-permute-start.2 = (bf16[512,512]{1,0:T(8,128)(2,1)S(1)}, bf16[512,512]{1,0:T(8,128)(2,1)S(1)}, u32[]{:S(2)}, u32[]{:S(2)}) collective-permute-start(bf16[512,512]{1,0:T(8,128)(2,1)S(1)} %get-tuple-element.76), channel_id=1, source_target_pairs={{0,48},{16,0},{32,16},{48,32},{1,49},{17,1},{33,17},{49,33},{2,50}... | collective-permute-start | bytes 1572872 | tf_op jit(solution)/shard_map/ppermute | solution.py:344
  12.2 9.5 %collective-permute-start.6 = (bf16[2,192,256]{2,1,0:T(8,128)(2,1)S(1)}, bf16[2,192,256]{2,1,0:T(8,128)(2,1)S(1)}, u32[]{:S(2)}, u32[]{:S(2)}) collective-permute-start(bf16[2,192,256]{2,1,0:T(8,128)(2,1)S(1)} %copy-done.39), channel_id=1, source_target_pairs={{0,0},{2,2},{4,4},{6,6},{8,64},{10,66},{12,68},{14,70},{64,8},{66,... | collective-permute-start | bytes 589832 | tf_op jit(solution)/shard_map/ppermute | solution.py:355
  17.6 11.1 %collective-permute-start.7 = (bf16[2,192,256]{2,1,0:T(8,128)(2,1)S(1)}, bf16[2,192,256]{2,1,0:T(8,128)(2,1)S(1)}, u32[]{:S(2)}, u32[]{:S(2)}) collective-permute-start(bf16[2,192,256]{2,1,0:T(8,128)(2,1)S(1)} %copy-done.39), channel_id=1, source_target_pairs={{0,2},{2,0},{4,6},{6,4},{8,66},{10,64},{12,70},{14,68},{64,10},{66... | collective-permute-start | bytes 589832 | tf_op jit(solution)/shard_map/ppermute | solution.py:356
  29.5 60.2 %copy-start.19 = (bf16[512,512]{1,0:T(8,128)(2,1)}, bf16[512,512]{1,0:T(8,128)(2,1)S(1)}, u32[]{:S(2)}) copy-start(bf16[512,512]{1,0:T(8,128)(2,1)S(1)} %collective-permute-done.x1) | copy-start | bytes 1572868
  29.5 60.2 %copy-start.22 = (bf16[512,512]{1,0:T(8,128)(2,1)}, bf16[512,512]{1,0:T(8,128)(2,1)S(1)}, u32[]{:S(2)}) copy-start(bf16[512,512]{1,0:T(8,128)(2,1)S(1)} %collective-permute-done.2.x3) | copy-start | bytes 1572868
  29.6 79.5 %all-gather.9.cloned.1.call-start = ((), (), s32[]{:S(2)}) async-start(), calls=%async_computation.5 | async-start | bytes 1966080 | tf_op jit(solution)/shard_map/all_gather | solution.py:361
  29.7 52.1 %copy-start = (bf16[1024,512]{1,0:T(8,128)(2,1)S(1)}, bf16[1024,512]{1,0:T(8,128)(2,1)}, u32[]{:S(2)}) copy-start(bf16[1024,512]{1,0:T(8,128)(2,1)} %g0) | copy-start | bytes 3145732
  29.7 18.3 %collective-permute-start.8 = (bf16[2,2,192,256]{3,2,1,0:T(8,128)(2,1)S(1)}, bf16[2,2,192,256]{3,2,1,0:T(8,128)(2,1)S(1)}, u32[]{:S(2)}, u32[]{:S(2)}) collective-permute-start(bf16[2,2,192,256]{3,2,1,0:T(8,128)(2,1)S(1)} %pad_maximum_fusion.1), channel_id=1, source_target_pairs={{0,0},{2,2},{4,4},{6,6},{8,64},{10,66},{12,68},{14,70},{64,8},{66,... | collective-permute-start | bytes 1179656 | tf_op jit(solution)/shard_map/ppermute | solution.py:355
  31.8 21.9 %collective-permute-start.9 = (bf16[2,2,192,256]{3,2,1,0:T(8,128)(2,1)S(1)}, bf16[2,2,192,256]{3,2,1,0:T(8,128)(2,1)S(1)}, u32[]{:S(2)}, u32[]{:S(2)}) collective-permute-start(bf16[2,2,192,256]{3,2,1,0:T(8,128)(2,1)S(1)} %pad_maximum_fusion.1), channel_id=1, source_target_pairs={{0,2},{2,0},{4,6},{6,4},{8,66},{10,64},{12,70},{14,68},{64,10},{66... | collective-permute-start | bytes 1179656 | tf_op jit(solution)/shard_map/ppermute | solution.py:356
  34.8 21.1 %collective-permute-start.3 = (bf16[512,512]{1,0:T(8,128)(2,1)}, bf16[512,512]{1,0:T(8,128)(2,1)}, u32[]{:S(2)}, u32[]{:S(2)}) collective-permute-start(bf16[512,512]{1,0:T(8,128)(2,1)} %get-tuple-element.75), channel_id=1, source_target_pairs={{0,48},{16,0},{32,16},{48,32},{1,49},{17,1},{33,17},{49,33},{2,50}... | collective-permute-start | bytes 1572872 | tf_op jit(solution)/shard_map/ppermute | solution.py:345
  53.7 33.3 %copy-start.38 = (s32[1,2]{1,0:T(1,128)S(1)}, s32[1,2]{1,0:T(1,128)}, u32[]{:S(2)}) copy-start(s32[1,2]{1,0:T(1,128)} %param.10) | copy-start | bytes 28
  53.7 36.1 %copy-start.1 = (bf16[1024,512]{1,0:T(8,128)(2,1)S(1)}, bf16[1024,512]{1,0:T(8,128)(2,1)}, u32[]{:S(2)}) copy-start(bf16[1024,512]{1,0:T(8,128)(2,1)} %x0.6) | copy-start | bytes 3145732
  54.5 87.7 %all-gather.11.cloned.1.call-start = ((), (), s32[]{:S(2)}) async-start(), calls=%async_computation.6 | async-start | bytes 1966080 | tf_op jit(solution)/shard_map/all_gather | solution.py:361
  54.6 14.5 %collective-permute-start.1 = (bf16[512,512]{1,0:T(8,128)(2,1)}, bf16[512,512]{1,0:T(8,128)(2,1)}, u32[]{:S(2)}, u32[]{:S(2)}) collective-permute-start(bf16[512,512]{1,0:T(8,128)(2,1)} %get-tuple-element.75), channel_id=1, source_target_pairs={{0,16},{16,32},{32,48},{48,0},{1,17},{17,33},{33,49},{49,1},{2,18}... | collective-permute-start | bytes 1572872 | tf_op jit(solution)/shard_map/ppermute | solution.py:345
  54.6 25.6 %collective-permute-start.4 = (bf16[512,512]{1,0:T(8,128)(2,1)S(1)}, bf16[512,512]{1,0:T(8,128)(2,1)}, u32[]{:S(2)}, u32[]{:S(2)}) collective-permute-start(bf16[512,512]{1,0:T(8,128)(2,1)S(1)} %collective-permute-done.x1), channel_id=1, source_target_pairs={{0,16},{16,32},{32,48},{48,0},{1,17},{17,33},{33,49},{49,1},{2,18}... | collective-permute-start | bytes 1572872 | tf_op jit(solution)/shard_map/ppermute | solution.py:350
  55.9 24.4 %collective-permute-start.5 = (bf16[512,512]{1,0:T(8,128)(2,1)}, bf16[512,512]{1,0:T(8,128)(2,1)}, u32[]{:S(2)}, u32[]{:S(2)}) collective-permute-start(bf16[512,512]{1,0:T(8,128)(2,1)} %collective-permute-done.3.x4), channel_id=1, source_target_pairs={{0,48},{16,0},{32,16},{48,32},{1,49},{17,1},{33,17},{49,33},{2,50}... | collective-permute-start | bytes 1572872 | tf_op jit(solution)/shard_map/ppermute | solution.py:350
  80.3 9.5 %collective-permute-start.10 = (bf16[4,2,2,192,256]{4,3,2,1,0:T(8,128)(2,1)}, bf16[4,2,2,192,256]{4,3,2,1,0:T(8,128)(2,1)}, u32[]{:S(2)}, u32[]{:S(2)}) collective-permute-start(bf16[4,2,2,192,256]{4,3,2,1,0:T(8,128)(2,1)} %bitcast.30), channel_id=1, source_target_pairs={{0,1},{1,0},{2,3},{3,2},{4,5},{5,4},{6,7},{7,6},{8,9},{9,8},{10,11... | collective-permute-start | bytes 4718600 | tf_op jit(solution)/shard_map/ppermute | solution.py:362
  82.8 16.5 %collective-permute-start.12 = (bf16[512,512]{1,0:T(8,128)(2,1)}, bf16[512,512]{1,0:T(8,128)(2,1)}, u32[]{:S(2)}, u32[]{:S(2)}) collective-permute-start(bf16[512,512]{1,0:T(8,128)(2,1)} %get-tuple-element.74), channel_id=1, source_target_pairs={{0,16},{16,32},{32,48},{48,0},{1,17},{17,33},{33,49},{49,1},{2,18}... | collective-permute-start | bytes 1572872 | tf_op jit(solution)/shard_map/ppermute | solution.py:344
  82.8 26.3 %collective-permute-start.13 = (bf16[512,512]{1,0:T(8,128)(2,1)}, bf16[512,512]{1,0:T(8,128)(2,1)}, u32[]{:S(2)}, u32[]{:S(2)}) collective-permute-start(bf16[512,512]{1,0:T(8,128)(2,1)} %get-tuple-element.73), channel_id=1, source_target_pairs={{0,16},{16,32},{32,48},{48,0},{1,17},{17,33},{33,49},{49,1},{2,18}... | collective-permute-start | bytes 1572872 | tf_op jit(solution)/shard_map/ppermute | solution.py:345
  82.8 26.3 %collective-permute-start.14 = (bf16[512,512]{1,0:T(8,128)(2,1)}, bf16[512,512]{1,0:T(8,128)(2,1)}, u32[]{:S(2)}, u32[]{:S(2)}) collective-permute-start(bf16[512,512]{1,0:T(8,128)(2,1)} %get-tuple-element.74), channel_id=1, source_target_pairs={{0,48},{16,0},{32,16},{48,32},{1,49},{17,1},{33,17},{49,33},{2,50}... | collective-permute-start | bytes 1572872 | tf_op jit(solution)/shard_map/ppermute | solution.py:344
  85.5 23.6 %collective-permute-start.15 = (bf16[512,512]{1,0:T(8,128)(2,1)}, bf16[512,512]{1,0:T(8,128)(2,1)}, u32[]{:S(2)}, u32[]{:S(2)}) collective-permute-start(bf16[512,512]{1,0:T(8,128)(2,1)} %get-tuple-element.73), channel_id=1, source_target_pairs={{0,48},{16,0},{32,16},{48,32},{1,49},{17,1},{33,17},{49,33},{2,50}... | collective-permute-start | bytes 1572872 | tf_op jit(solution)/shard_map/ppermute | solution.py:345
  87.0 169.1 %reduce-scatter.5.cloned.1.call-start = ((), (), s32[]{:S(2)}) async-start(), calls=%async_computation.3 | async-start | bytes 1966080 | tf_op jit(solution)/shard_map/reduce_scatter | solution.py:378
  109.1 20.2 %collective-permute-start.16 = (bf16[4,2,2,192,256]{4,3,2,1,0:T(8,128)(2,1)}, bf16[4,2,2,192,256]{4,3,2,1,0:T(8,128)(2,1)S(1)}, u32[]{:S(2)}, u32[]{:S(2)}) collective-permute-start(bf16[4,2,2,192,256]{4,3,2,1,0:T(8,128)(2,1)} %bitcast.33), channel_id=1, source_target_pairs={{0,1},{1,0},{2,3},{3,2},{4,5},{5,4},{6,7},{7,6},{8,9},{9,8},{10,11... | collective-permute-start | bytes 4718600 | tf_op jit(solution)/shard_map/ppermute | solution.py:362
  110.0 19.3 %collective-permute-start.11 = (bf16[1024,384]{1,0:T(8,128)(2,1)}, bf16[1024,384]{1,0:T(8,128)(2,1)S(1)}, u32[]{:S(2)}, u32[]{:S(2)}) collective-permute-start(bf16[1024,384]{1,0:T(8,128)(2,1)} %copy-done.18), channel_id=1, source_target_pairs={{0,64},{64,0},{1,65},{65,1},{2,66},{66,2},{3,67},{67,3},{4,68},{68... | collective-permute-start | bytes 2359304 | tf_op jit(solution)/shard_map/ppermute | solution.py:396
  129.3 9.7 %copy-start.10 = (bf16[1024,384]{1,0:T(8,128)(2,1)}, bf16[1024,384]{1,0:T(8,128)(2,1)S(1)}, u32[]{:S(2)}) copy-start(bf16[1024,384]{1,0:T(8,128)(2,1)S(1)} %collective-permute-done.11.got_g) | copy-start | bytes 2359300
  133.1 34.6 %copy-start.25 = (f32[1024]{0:T(1024)S(1)}, f32[1024]{0:T(1024)}, u32[]{:S(2)}) copy-start(f32[1024]{0:T(1024)} %param.9) | copy-start | bytes 12292
  142.2 16.2 %collective-permute-start.20 = (bf16[4,2,2,192,256]{4,3,2,1,0:T(8,128)(2,1)}, bf16[4,2,2,192,256]{4,3,2,1,0:T(8,128)(2,1)S(1)}, u32[]{:S(2)}, u32[]{:S(2)}) collective-permute-start(bf16[4,2,2,192,256]{4,3,2,1,0:T(8,128)(2,1)} %bitcast.36), channel_id=1, source_target_pairs={{0,1},{1,0},{2,3},{3,2},{4,5},{5,4},{6,7},{7,6},{8,9},{9,8},{10,11... | collective-permute-start | bytes 4718600 | tf_op jit(solution)/shard_map/ppermute | solution.py:362
  143.4 15.0 %collective-permute-start.18 = (bf16[512,512]{1,0:T(8,128)(2,1)}, bf16[512,512]{1,0:T(8,128)(2,1)S(1)}, u32[]{:S(2)}, u32[]{:S(2)}) collective-permute-start(bf16[512,512]{1,0:T(8,128)(2,1)} %collective-permute-done.12.x1.g1), channel_id=1, source_target_pairs={{0,16},{16,32},{32,48},{48,0},{1,17},{17,33},{33,49},{49,1},{2,18}... | collective-permute-start | bytes 1572872 | tf_op jit(solution)/shard_map/ppermute | solution.py:350
  144.2 14.2 %collective-permute-start.19 = (bf16[512,512]{1,0:T(8,128)(2,1)}, bf16[512,512]{1,0:T(8,128)(2,1)S(1)}, u32[]{:S(2)}, u32[]{:S(2)}) collective-permute-start(bf16[512,512]{1,0:T(8,128)(2,1)} %collective-permute-done.15.x4.g4), channel_id=1, source_target_pairs={{0,48},{16,0},{32,16},{48,32},{1,49},{17,1},{33,17},{49,33},{2,50}... | collective-permute-start | bytes 1572872 | tf_op jit(solution)/shard_map/ppermute | solution.py:350
  146.1 21.6 %collective-permute-start.17 = (bf16[1024,384]{1,0:T(8,128)(2,1)}, bf16[1024,384]{1,0:T(8,128)(2,1)S(1)}, u32[]{:S(2)}, u32[]{:S(2)}) collective-permute-start(bf16[1024,384]{1,0:T(8,128)(2,1)} %copy-done.15), channel_id=1, source_target_pairs={{0,64},{64,0},{1,65},{65,1},{2,66},{66,2},{3,67},{67,3},{4,68},{68... | collective-permute-start | bytes 2359304 | tf_op jit(solution)/shard_map/ppermute | solution.py:399
  177.0 4.2 %collective-permute-start.22 = (bf16[4,2,1,2,192,256]{5,4,3,2,1,0:T(8,128)(2,1)S(1)}, bf16[4,2,1,2,192,256]{5,4,3,2,1,0:T(8,128)(2,1)S(1)}, u32[]{:S(2)}, u32[]{:S(2)}) collective-permute-start(bf16[4,2,1,2,192,256]{5,4,3,2,1,0:T(8,128)(2,1)S(1)} %get-tuple-element.56), channel_id=1, source_target_pairs={{0,1},{1,0},{2,3},{3,2},{4,5},{5,4},{6,7},{7,6},{8,9},{9,8},{10,11... | collective-permute-start | bytes 4718600 | tf_op jit(solution)/shard_map/ppermute | solution.py:405
  178.2 19.3 %collective-permute-start.21 = (bf16[1024,384]{1,0:T(8,128)(2,1)}, bf16[1024,384]{1,0:T(8,128)(2,1)S(1)}, u32[]{:S(2)}, u32[]{:S(2)}) collective-permute-start(bf16[1024,384]{1,0:T(8,128)(2,1)} %get-tuple-element.53), channel_id=1, source_target_pairs={{0,64},{64,0},{1,65},{65,1},{2,66},{66,2},{3,67},{67,3},{4,68},{68... | collective-permute-start | bytes 2359304 | tf_op jit(solution)/shard_map/ppermute | solution.py:402
  223.6 6.5 %collective-permute-start.24 = (bf16[4,2,2,2,192,256]{5,4,3,2,1,0:T(8,128)(2,1)}, bf16[4,2,2,2,192,256]{5,4,3,2,1,0:T(8,128)(2,1)}, u32[]{:S(2)}, u32[]{:S(2)}) collective-permute-start(bf16[4,2,2,2,192,256]{5,4,3,2,1,0:T(8,128)(2,1)} %get-tuple-element.62), channel_id=1, source_target_pairs={{0,1},{1,0},{2,3},{3,2},{4,5},{5,4},{6,7},{7,6},{8,9},{9,8},{10,11... | collective-permute-start | bytes 9437192 | tf_op jit(solution)/shard_map/ppermute | solution.py:410
  224.5 72.8 %reduce-scatter.3.cloned.1.call-start = ((), (), s32[]{:S(2)}) async-start(), calls=%async_computation.2 | async-start | bytes 3932160 | tf_op jit(solution)/shard_map/reduce_scatter | solution.py:378
  224.5 2.8 collective-permute-start.23
  234.9 4.1 %collective-permute-start.25 = (f32[8,128]{1,0:T(8,128)S(1)}, f32[8,128]{1,0:T(8,128)S(1)}, u32[]{:S(2)}, u32[]{:S(2)}) collective-permute-start(f32[8,128]{1,0:T(8,128)S(1)} %add.51), channel_id=1, source_target_pairs={{0,32},{16,48},{32,0},{48,16},{1,33},{17,49},{33,1},{49,17},{2,34}... | collective-permute-start | bytes 12296 | tf_op jit(solution)/shard_map/ppermute | solution.py:416
  251.7 54.0 %collective-permute-start.26 = (bf16[1024,512]{1,0:T(8,128)(2,1)}, bf16[1024,512]{1,0:T(8,128)(2,1)S(1)}, u32[]{:S(2)}, u32[]{:S(2)}) collective-permute-start(bf16[1024,512]{1,0:T(8,128)(2,1)} %get-tuple-element.69), channel_id=1, source_target_pairs={{0,16},{16,32},{32,48},{48,0},{1,17},{17,33},{33,49},{49,1},{2,18}... | collective-permute-start | bytes 3145736 | tf_op jit(solution)/shard_map/ppermute | solution.py:419
  253.0 52.7 %collective-permute-start.27 = (bf16[1024,512]{1,0:T(8,128)(2,1)}, bf16[1024,512]{1,0:T(8,128)(2,1)S(1)}, u32[]{:S(2)}, u32[]{:S(2)}) collective-permute-start(bf16[1024,512]{1,0:T(8,128)(2,1)} %get-tuple-element.70), channel_id=1, source_target_pairs={{0,48},{16,0},{32,16},{48,32},{1,49},{17,1},{33,17},{49,33},{2,50}... | collective-permute-start | bytes 3145736 | tf_op jit(solution)/shard_map/ppermute | solution.py:420
  254.6 51.1 %collective-permute-start.28 = (bf16[1024,512]{1,0:T(8,128)(2,1)}, bf16[1024,512]{1,0:T(8,128)(2,1)}, u32[]{:S(2)}, u32[]{:S(2)}) collective-permute-start(bf16[1024,512]{1,0:T(8,128)(2,1)} %get-tuple-element.71), channel_id=1, source_target_pairs={{0,32},{16,48},{32,0},{48,16},{1,33},{17,49},{33,1},{49,17},{2,34}... | collective-permute-start | bytes 3145736 | tf_op jit(solution)/shard_map/ppermute | solution.py:421
  256.0 3.6 %collective-permute-start.29 = (f32[8,128]{1,0:T(8,128)S(1)}, f32[8,128]{1,0:T(8,128)S(1)}, u32[]{:S(2)}, u32[]{:S(2)}) collective-permute-start(f32[8,128]{1,0:T(8,128)S(1)} %add.53), channel_id=1, source_target_pairs={{0,64},{64,0},{1,65},{65,1},{2,66},{66,2},{3,67},{67,3},{4,68},{68... | collective-permute-start | bytes 12296 | tf_op jit(solution)/shard_map/ppermute | solution.py:418
  257.7 40.7 %collective-permute-start.30 = (bf16[1,2,192,256]{3,2,1,0:T(8,128)(2,1)}, bf16[1,2,192,256]{3,2,1,0:T(8,128)(2,1)S(1)}, u32[]{:S(2)}, u32[]{:S(2)}) collective-permute-start(bf16[1,2,192,256]{3,2,1,0:T(8,128)(2,1)} %get-tuple-element.81), channel_id=1, source_target_pairs={{0,0},{2,2},{4,4},{6,6},{8,64},{10,66},{12,68},{14,70},{64,8},{66,... | collective-permute-start | bytes 589832 | tf_op jit(solution)/shard_map/ppermute | solution.py:372
  259.7 41.1 %collective-permute-start.31 = (bf16[1,2,192,256]{3,2,1,0:T(8,128)(2,1)S(1)}, bf16[1,2,192,256]{3,2,1,0:T(8,128)(2,1)}, u32[]{:S(2)}, u32[]{:S(2)}) collective-permute-start(bf16[1,2,192,256]{3,2,1,0:T(8,128)(2,1)S(1)} %get-tuple-element.82), channel_id=1, source_target_pairs={{0,2},{2,0},{4,6},{6,4},{8,66},{10,64},{12,70},{14,68},{64,10},{66... | collective-permute-start | bytes 589832 | tf_op jit(solution)/shard_map/ppermute | solution.py:373
  298.5 14.4 %collective-permute-start.32 = (bf16[2,2,192,256]{3,2,1,0:T(8,128)(2,1)S(1)}, bf16[2,2,192,256]{3,2,1,0:T(8,128)(2,1)S(1)}, u32[]{:S(2)}, u32[]{:S(2)}) collective-permute-start(bf16[2,2,192,256]{3,2,1,0:T(8,128)(2,1)S(1)} %get-tuple-element.79), channel_id=1, source_target_pairs={{0,0},{2,2},{4,4},{6,6},{8,64},{10,66},{12,68},{14,70},{64,8},{66,... | collective-permute-start | bytes 1179656 | tf_op jit(solution)/shard_map/ppermute | solution.py:372
  300.8 21.4 %collective-permute-start.33 = (bf16[2,2,192,256]{3,2,1,0:T(8,128)(2,1)S(1)}, bf16[2,2,192,256]{3,2,1,0:T(8,128)(2,1)S(1)}, u32[]{:S(2)}, u32[]{:S(2)}) collective-permute-start(bf16[2,2,192,256]{3,2,1,0:T(8,128)(2,1)S(1)} %get-tuple-element.80), channel_id=1, source_target_pairs={{0,2},{2,0},{4,6},{6,4},{8,66},{10,64},{12,70},{14,68},{64,10},{66... | collective-permute-start | bytes 1179656 | tf_op jit(solution)/shard_map/ppermute | solution.py:373
  (31 other events, 66.1 us)
Sparse Core Ops, SparseCore 0:
  29.7 36.9 all-gather.6
  68.9 25.4 all-gather.8
  96.7 26.6 all-gather.10
  224.6 23.0 reduce-scatter.4
  250.0 47.2 reduce-scatter.2

commit v5 on v4

--- a/solution.py
+++ b/solution.py
@@ -10,7 +10,7 @@
 BLOCK = 128
 TILE = 256
 HID = 192
-VMEM = 28 << 20
+VMEM = 60 << 20
 COLS = 256
 BF = jnp.bfloat16
 F32 = jnp.float32
@@ -374,10 +374,6 @@
     return straight.astype(F32) + crossed.astype(F32)
 
 
-def scatter_z(both):
-    return lax.psum_scatter(both, "z", scatter_dimension=0, tiled=False)
-
-
 def on_device(features, grad_out, scores, counts, w_gate, w_up, w_down):
     rows = features.shape[0]
     y, xl, core, xh = (lax.axis_index(a) for a in ("y", "xl", "core", "xh"))
@@ -387,14 +383,14 @@
     feats = halves_over(features)
     feats += opposite_over(feats)
     pair_g = after(jnp.stack(to_plane(w_gate)), feats[1], feats[3])
-    straight, crossed = to_plane(after(jnp.stack([w_up, w_down]), pair_g))
+    straight, crossed = to_plane(after(jnp.stack([w_up, w_down]), feats[2], feats[4]))
     pair_u, pair_d = (jnp.stack([straight[i], crossed[i]]) for i in range(2))
     grads = halves_over(after(grad_out, feats[5], feats[6]))
     gate_all = spread_pair(pair_g, *feats[1:], pair_u, pair_d)
 
     own_g, send_g = pre_part(sc, feats, gate_all)
     got_g = lax.ppermute(send_g, "xl", ring(2, 1))
-    up_all = spread_pair(pair_u, send_g, *grads[1:])
+    up_all = spread_pair(pair_u, got_g, *grads[1:])
     own_u, send_u = pre_part(after(sc, got_g), feats, up_all)
     got_u = lax.ppermute(send_u, "xl", ring(2, 1))
     grads += opposite_over(after(grads, send_g))
@@ -403,16 +399,15 @@
 
     keep, away = down_part(after(sc, send_b), scores, own_g, got_g, own_u, got_u, grads)
     both_d = over_cores(keep, lax.ppermute(away, "core", ring(2, 1)))
-    part_d = scatter_z(both_d)
     total, gu, keep, away = gate_up_part(
         sc, scores, own_g, got_g, own_u, got_u, own_b, after(got_b, both_d), feats
     )
-    got = lax.ppermute(after(away, part_d), "core", ring(2, 1))
+    got = lax.ppermute(away, "core", ring(2, 1))
     total = total + lax.ppermute(total, "y", [(i, i ^ 1) for i in range(4)])
-    both_gu = over_cores(after(keep, total), got)
-    part_gu = scatter_z(both_gu)
-
-    dx = rows_part(sc, after(gu, both_gu), gate_all, up_all)
+    both = jnp.concatenate([over_cores(after(keep, total), got), both_d], axis=2)
+    part = lax.psum_scatter(both, "z", scatter_dimension=0, tiled=False)
+
+    dx = rows_part(sc, after(gu, both), gate_all, up_all)
     total = total + lax.ppermute(total, "y", [(i, i ^ 2) for i in range(4)])
     dx, _ = lax.optimization_barrier((dx, total))
     total = total + lax.ppermute(total, "xl", ring(2, 1))
@@ -423,9 +418,8 @@
         (dx[0].astype(F32) + from_below.astype(F32)) + (from_above.astype(F32) + opposite.astype(F32))
     ).astype(BF)
 
-    grad_down = over_chips(part_d, xh)
-    grad_gu = over_chips(after(part_gu, grad_down, total), xh)
-    return grad_features, total.reshape(rows), grad_gu[0], grad_gu[1], grad_down[0]
+    weights = over_chips(part, xh)
+    return grad_features, total.reshape(rows), weights[0], weights[1], weights[2]
 
 
 def solution(mesh):

time: 331 us -> 309 us (0.934)
  local copies, waits for them, and re-layouts: 40.4 us -> 11.7 us
  Pallas kernels: 47.8 us -> 62.8 us
  starting transfers between devices: 47.8 us -> 42.6 us
    unnamed x80 -> x44, local copies, waits for them, and re-layouts: 31.9 us -> 5.87 us
    ppermute x1, waiting for transfers between devices: 19.3 us -> 0.01 us  [on_device(): got_g = lax.ppermute(send_g, 'xl', ring(2, 1))]
    ppermute x2, waiting for transfers between devices: 23.5 us -> 11.8 us  [opposite_over(): lax.ppermute(pieces[1], 'y', ring(4, 1))]
    ppermute x4, waiting for transfers between devices: 0.01 us -> 10 us  [halves_over(): near = [lax.ppermute(x[:half], 'y', ring(4, k)) for k in (1, 3)]]
    pallas_call x3, Pallas kernels: 18.7 us -> 25.6 us  [pre_part(): pl.pallas_call(pre_kernel, out_shape=(jax.ShapeDtypeStruct((rows, n), F32...]
    all_gather x3, waiting for transfers between devices: 0.02 us -> 6.16 us  [spread_pair(): here = after(lax.all_gather(pair, 'z', axis=0, tiled=False), *before)]
    ppermute x4, waiting for transfers between devices: 20.6 us -> 25.6 us  [halves_over(): rest = [lax.ppermute(x[half:], 'y', ring(4, k)) for k in (1, 3)]]
    reduce_scatter x2 -> x1, waiting for transfers between devices: 36 us -> 31.6 us  [on_device(): part = lax.psum_scatter(both, 'z', scatter_dimension=0, tiled=False)]
  transfers between devices with their start and end apart: 39 -> 36, of which waited for: 17 -> 23; matrix products, arithmetic and copies ran while one was open for 6% -> 4% of each run, Pallas kernels for 8% -> 12%
where the time goes in v5:
time: 309 us
  waiting for transfers between devices  162 us (52%)
  Pallas kernels  62.8 us (20%)
  starting transfers between devices  42.6 us (14%)
  between operations  15.4 us (5%)
  other arithmetic  14.1 us (5%)
  local copies, waits for them, and re-layouts  11.7 us (4%)
    reduce_scatter x1, waiting for transfers between devices, on_device(): part = lax.psum_scatter(both, 'z', scatter_dimension=0, tiled=False)  31.6 us
    ppermute x4, waiting for transfers between devices, halves_over(): rest = [lax.ppermute(x[half:], 'y', ring(4, k)) for k in (1, 3)]  25.6 us
    pallas_call x3, Pallas kernels, pre_part(): pl.pallas_call(pre_kernel, out_shape=(jax.ShapeDtypeStruct((rows, n), F32...  25.6 us
    pallas_call x1, Pallas kernels, gate_up_part(): pl.pallas_call(gate_up_kernel, out_shape=(jax.ShapeDtypeStruct((rows // B...  16.5 us
    ppermute x2, waiting for transfers between devices, to_plane(): lax.ppermute(w, ('xl', 'z', 'xh'), swap_pairs(1))  14.5 us
    ppermute x1, waiting for transfers between devices, on_device(): got_b = lax.ppermute(send_b, 'xl', ring(2, 1))  13.9 us
    ppermute x1, waiting for transfers between devices, over_chips(): crossed = lax.ppermute(crossed, ('xl', 'z', 'xh'), swap_pairs(1))  13.5 us
    ppermute x2, waiting for transfers between devices, to_plane(): lax.ppermute(w, ('xl', 'z', 'xh'), swap_pairs(0))  13.4 us
  transfers between devices with their start and end apart: 36, of which 23 were waited for; matrix products, arithmetic and copies ran while one was open for 4% of the time, Pallas kernels for 12%

profile of v5, /device:TPU:3, one launch (start us, length us, event | category | flops | bytes accessed | tf_op | source)
XLA Modules:
  0.0 308.5 jit_solution(9608986648604327610)
XLA Ops:
  7.2 1.4 fusion.1
  8.6 1.4 collective-permute-start
  10.0 1.5 collective-permute-start.2
  11.5 5.5 %collective-permute-start.6 = (bf16[2,192,256]{2,1,0:T(8,128)(2,1)S(1)}, bf16[2,192,256]{2,1,0:T(8,128)(2,1)S(1)}, u32[]{:S(2)}, u32[]{:S(2)}) collective-permute-start(bf16[2,192,256]{2,1,0:T(8,128)(2,1)S(1)} %copy-done.21), channel_id=1, source_target_pairs={{0,0},{2,2},{4,4},{6,6},{8,64},{10,66},{12,68},{14,70},{64,8},{66,... | collective-permute-start | bytes 589832 | tf_op jit(solution)/shard_map/ppermute | solution.py:355
  18.0 3.1 collective-permute-done.6
  21.1 7.0 %collective-permute-done.7 = bf16[2,192,256]{2,1,0:T(8,128)(2,1)S(1)} collective-permute-done((bf16[2,192,256]{2,1,0:T(8,128)(2,1)S(1)}, bf16[2,192,256]{2,1,0:T(8,128)(2,1)S(1)}, u32[]{:S(2)}, u32[]{:S(2)}) %collective-permute-start.7) | collective-permute-done | bytes 196640 | tf_op jit(solution)/shard_map/ppermute | solution.py:356
  29.0 1.4 collective-permute-start.3
  30.6 11.6 %collective-permute-done.3.x4 = bf16[512,512]{1,0:T(8,128)(2,1)S(1)} collective-permute-done((bf16[512,512]{1,0:T(8,128)(2,1)S(1)}, bf16[512,512]{1,0:T(8,128)(2,1)S(1)}, u32[]{:S(2)}, u32[]{:S(2)}) %collective-permute-start.3) | collective-permute-done | bytes 524320 | tf_op jit(solution)/shard_map/ppermute | solution.py:345
  42.2 2.2 collective-permute-done.1.x2
  44.3 1.9 collective-permute-start.8
  46.2 1.3 collective-permute-start.9
  47.6 2.7 collective-permute-start.5
  50.2 10.4 %collective-permute-done.8 = bf16[2,2,192,256]{3,2,1,0:T(8,128)(2,1)S(1)} collective-permute-done((bf16[2,2,192,256]{3,2,1,0:T(8,128)(2,1)S(1)}, bf16[2,2,192,256]{3,2,1,0:T(8,128)(2,1)S(1)}, u32[]{:S(2)}, u32[]{:S(2)}) %collective-permute-start.8) | collective-permute-done | bytes 393248 | tf_op jit(solution)/shard_map/ppermute | solution.py:355
  60.7 7.5 %collective-permute-done.9 = bf16[2,2,192,256]{3,2,1,0:T(8,128)(2,1)S(1)} collective-permute-done((bf16[2,2,192,256]{3,2,1,0:T(8,128)(2,1)S(1)}, bf16[2,2,192,256]{3,2,1,0:T(8,128)(2,1)S(1)}, u32[]{:S(2)}, u32[]{:S(2)}) %collective-permute-start.9) | collective-permute-done | bytes 393248 | tf_op jit(solution)/shard_map/ppermute | solution.py:356
  69.8 2.4 all-gather.7.cloned.1.call-done
  74.8 1.4 stack.47.sc
  76.3 8.6 %shard_map.110 = (f32[1024,384]{1,0:T(8,128)}, bf16[1024,384]{1,0:T(8,128)(2,1)}) custom-call(s32[6]{0:T(128)} %stack.47.sc, bf16[1024,512]{1,0:T(8,128)(2,1)} %x0.6, bf16[512,512]{1,0:T(8,128)(2,1)} %copy-done.11, bf16[512,512]{1,0:T(8,128)(2,1)} %copy-done.14, bf16[512,512]{1,0:T(8,128)(2,1)} %copy-done.12, bf16[512,512]{1,0:T(8,128)(2,1)} %copy-done.13, ...), custom_call_target="tpu_custom_call" | custom-call | flops 3221225472 | bytes 10485760 | tf_op jit(solution)/shard_map/pallas_call | solution.py:134
  87.5 1.5 collective-permute-start.14
  89.3 10.0 %collective-permute-done.12.x1.g1 = bf16[512,512]{1,0:T(8,128)(2,1)S(1)} collective-permute-done((bf16[512,512]{1,0:T(8,128)(2,1)S(1)}, bf16[512,512]{1,0:T(8,128)(2,1)S(1)}, u32[]{:S(2)}, u32[]{:S(2)}) %collective-permute-start.12) | collective-permute-done | bytes 524320 | tf_op jit(solution)/shard_map/ppermute | solution.py:344
  99.3 11.1 %collective-permute-done.13.x2.g2 = bf16[512,512]{1,0:T(8,128)(2,1)S(1)} collective-permute-done((bf16[512,512]{1,0:T(8,128)(2,1)S(1)}, bf16[512,512]{1,0:T(8,128)(2,1)S(1)}, u32[]{:S(2)}, u32[]{:S(2)}) %collective-permute-start.13) | collective-permute-done | bytes 524320 | tf_op jit(solution)/shard_map/ppermute | solution.py:345
  111.2 2.1 collective-permute-start.16
  113.3 3.2 %collective-permute-done.16.w1.u1 = bf16[4,2,2,192,256]{4,3,2,1,0:T(8,128)(2,1)S(1)} collective-permute-done((bf16[4,2,2,192,256]{4,3,2,1,0:T(8,128)(2,1)}, bf16[4,2,2,192,256]{4,3,2,1,0:T(8,128)(2,1)S(1)}, u32[]{:S(2)}, u32[]{:S(2)}) %collective-permute-start.16) | collective-permute-done | bytes 1572896 | tf_op jit(solution)/shard_map/ppermute | solution.py:362
  117.8 8.5 %shard_map.111 = (f32[1024,384]{1,0:T(8,128)}, bf16[1024,384]{1,0:T(8,128)(2,1)}) custom-call(s32[6]{0:T(128)} %stack.47.sc, bf16[1024,512]{1,0:T(8,128)(2,1)} %x0.6, bf16[512,512]{1,0:T(8,128)(2,1)} %copy-done.11, bf16[512,512]{1,0:T(8,128)(2,1)} %copy-done.14, bf16[512,512]{1,0:T(8,128)(2,1)} %copy-done.12, bf16[512,512]{1,0:T(8,128)(2,1)} %copy-done.13, ...), custom_call_target="tpu_custom_call" | custom-call | flops 3221225472 | bytes 10485760 | tf_op jit(solution)/shard_map/pallas_call | solution.py:134
  126.3 3.7 %all-gather.11.cloned.1.call-done = bf16[8,2,192,256]{3,2,1,0:T(8,128)(2,1)} async-done(((bf16[2,2,192,256]{3,2,1,0:T(8,128)(2,1)}), bf16[8,2,192,256]{3,2,1,0:T(8,128)(2,1)}) %all-gather.11.cloned.1.call-update) | async-done | bytes 1572880 | tf_op jit(solution)/shard_map/all_gather | solution.py:361
  132.0 1.5 collective-permute-start.19
  133.7 11.8 %collective-permute-done.18.x5.g5 = bf16[512,512]{1,0:T(8,128)(2,1)S(1)} collective-permute-done((bf16[512,512]{1,0:T(8,128)(2,1)S(1)}, bf16[512,512]{1,0:T(8,128)(2,1)S(1)}, u32[]{:S(2)}, u32[]{:S(2)}) %collective-permute-start.18) | collective-permute-done | bytes 524320 | tf_op jit(solution)/shard_map/ppermute | solution.py:350
  148.3 8.5 %shard_map.112 = (f32[1024,384]{1,0:T(8,128)}, bf16[1024,384]{1,0:T(8,128)(2,1)}) custom-call(s32[6]{0:T(128)} %stack.47.sc, bf16[1024,512]{1,0:T(8,128)(2,1)} %g0, bf16[512,512]{1,0:T(8,128)(2,1)} %copy-done.16, bf16[512,512]{1,0:T(8,128)(2,1)} %copy-done.17, bf16[512,512]{1,0:T(8,128)(2,1)} %copy-done.18, bf16[512,512]{1,0:T(8,128)(2,1)} %collective-permute-done.15.x4.g4, ...), custom_call_target="tpu_custom_call" | custom-call | flops 3221225472 | bytes 10485760 | tf_op jit(solution)/shard_map/pallas_call | solution.py:134
  157.7 9.6 %shard_map.113 = (bf16[4,2,1,2,192,256]{5,4,3,2,1,0:T(8,128)(2,1)}, bf16[4,2,1,2,192,256]{5,4,3,2,1,0:T(8,128)(2,1)}) custom-call(s32[6]{0:T(128)} %stack.47.sc, f32[8,128]{1,0:T(8,128)} %bitcast.38, f32[1024,384]{1,0:T(8,128)} %get-tuple-element.41.own_g, bf16[1024,384]{1,0:T(8,128)(2,1)} %copy-done.7, f32[1024,384]{1,0:T(8,128)} %get-tuple-element.46.own_u, ...), custom_call_target="tpu_custom_call" | custom-call | flops 3221225472 | bytes 14680064 | tf_op jit(solution)/shard_map/pallas_call | solution.py:209
  168.8 3.0 collective-permute-done.22
  171.8 1.9 add_convert_fusion.1
  173.7 13.9 %collective-permute-done.21.got_b = bf16[1024,384]{1,0:T(8,128)(2,1)S(1)} collective-permute-done((bf16[1024,384]{1,0:T(8,128)(2,1)S(1)}, bf16[1024,384]{1,0:T(8,128)(2,1)S(1)}, u32[]{:S(2)}, u32[]{:S(2)}) %collective-permute-start.21) | collective-permute-done | bytes 786464 | tf_op jit(solution)/shard_map/ppermute | solution.py:398
  188.5 16.5 %shard_map.114 = (f32[8,128]{1,0:T(8,128)}, bf16[1024,768]{1,0:T(8,128)(2,1)}, bf16[4,2,2,2,192,256]{5,4,3,2,1,0:T(8,128)(2,1)}, bf16[4,2,2,2,192,256]{5,4,3,2,1,0:T(8,128)(2,1)}) custom-call(s32[6]{0:T(128)} %stack.47.sc, f32[8,128]{1,0:T(8,128)} %bitcast.39, f32[1024,384]{1,0:T(8,128)} %get-tuple-element.41.own_g, bf16[1024,384]{1,0:T(8,128)(2,1)} %copy-done.7, ...), custom_call_target="tpu_custom_call" | custom-call | flops 6442450944 | bytes 20971520 | tf_op jit(solution)/shard_map/pallas_call | solution.py:271
  206.5 2.1 collective-permute-done.23
  209.3 2.1 collective-permute-done.24
  211.4 3.0 add_convert_fusion
  214.4 2.6 pad_maximum_fusion
  217.0 2.1 collective-permute-start.25
  219.2 2.1 collective-permute-done.25
  221.3 11.1 %shard_map.115 = (bf16[1024,512]{1,0:T(8,128)(2,1)}, bf16[1024,512]{1,0:T(8,128)(2,1)}, bf16[1024,512]{1,0:T(8,128)(2,1)}, bf16[1024,512]{1,0:T(8,128)(2,1)}) custom-call(s32[6]{0:T(128)} %stack.47.sc, bf16[1024,768]{1,0:T(8,128)(2,1)} %get-tuple-element.62.gu, bf16[4,2,2,192,256]{4,3,2,1,0:T(8,128)(2,1)} %bitcast.32, ...), custom_call_target="tpu_custom_call" | custom-call | flops 3221225472 | bytes 14680064 | tf_op jit(solution)/shard_map/pallas_call | solution.py:324
  232.6 2.6 collective-permute-start.27
  235.7 31.6 %reduce-scatter.2.cloned.1.call-done = bf16[1,2,3,2,192,256]{5,4,3,2,1,0:T(8,128)(2,1)} async-done(((bf16[4,2,3,2,192,256]{5,4,3,2,1,0:T(8,128)(2,1)}), bf16[1,2,3,2,192,256]{5,4,3,2,1,0:T(8,128)(2,1)}) %reduce-scatter.2.cloned.1.call-update) | async-done | bytes 1179664 | tf_op jit(solution)/shard_map/reduce_scatter | solution.py:408
  267.3 1.3 dynamic-slice_bitcast_fusion.1
  268.7 3.1 %collective-permute-start.30 = (bf16[3,2,192,256]{3,2,1,0:T(8,128)(2,1)S(1)}, bf16[3,2,192,256]{3,2,1,0:T(8,128)(2,1)S(1)}, u32[]{:S(2)}, u32[]{:S(2)}) collective-permute-start(bf16[3,2,192,256]{3,2,1,0:T(8,128)(2,1)S(1)} %get-tuple-element.74), channel_id=1, source_target_pairs={{0,0},{2,2},{4,4},{6,6},{8,64},{10,66},{12,68},{14,70},{64,8},{66,... | collective-permute-start | bytes 1769480 | tf_op jit(solution)/shard_map/ppermute | solution.py:372
  271.8 3.4 %collective-permute-start.31 = (bf16[3,2,192,256]{3,2,1,0:T(8,128)(2,1)S(1)}, bf16[3,2,192,256]{3,2,1,0:T(8,128)(2,1)S(1)}, u32[]{:S(2)}, u32[]{:S(2)}) collective-permute-start(bf16[3,2,192,256]{3,2,1,0:T(8,128)(2,1)S(1)} %get-tuple-element.75), channel_id=1, source_target_pairs={{0,2},{2,0},{4,6},{6,4},{8,66},{10,64},{12,70},{14,68},{64,10},{66... | collective-permute-start | bytes 1769480 | tf_op jit(solution)/shard_map/ppermute | solution.py:373
  275.8 3.3 %collective-permute-done.28 = bf16[1024,512]{1,0:T(8,128)(2,1)} collective-permute-done((bf16[1024,512]{1,0:T(8,128)(2,1)}, bf16[1024,512]{1,0:T(8,128)(2,1)}, u32[]{:S(2)}, u32[]{:S(2)}) %collective-permute-start.28) | collective-permute-done | bytes 1048608 | tf_op jit(solution)/shard_map/ppermute | solution.py:416
  279.1 2.8 add_convert_fusion.2
  281.8 5.4 %collective-permute-done.30 = bf16[3,2,192,256]{3,2,1,0:T(8,128)(2,1)S(1)} collective-permute-done((bf16[3,2,192,256]{3,2,1,0:T(8,128)(2,1)S(1)}, bf16[3,2,192,256]{3,2,1,0:T(8,128)(2,1)S(1)}, u32[]{:S(2)}, u32[]{:S(2)}) %collective-permute-start.30) | collective-permute-done | bytes 589856 | tf_op jit(solution)/shard_map/ppermute | solution.py:372
  287.3 13.5 %collective-permute-done.31 = bf16[3,2,192,256]{3,2,1,0:T(8,128)(2,1)S(1)} collective-permute-done((bf16[3,2,192,256]{3,2,1,0:T(8,128)(2,1)S(1)}, bf16[3,2,192,256]{3,2,1,0:T(8,128)(2,1)S(1)}, u32[]{:S(2)}, u32[]{:S(2)}) %collective-permute-start.31) | collective-permute-done | bytes 589856 | tf_op jit(solution)/shard_map/ppermute | solution.py:373
  (98 shorter events, 23.0 us)
Async XLA Ops:
  7.2 23.4 %copy-start.3 = (bf16[2,192,256]{2,1,0:T(8,128)(2,1)S(1)}, bf16[2,192,256]{2,1,0:T(8,128)(2,1)}, u32[]{:S(2)}) copy-start(bf16[2,192,256]{2,1,0:T(8,128)(2,1)} %param.12) | copy-start | bytes 589828
  7.2 23.3 %copy-start.2 = (bf16[2,192,256]{2,1,0:T(8,128)(2,1)S(1)}, bf16[2,192,256]{2,1,0:T(8,128)(2,1)}, u32[]{:S(2)}) copy-start(bf16[2,192,256]{2,1,0:T(8,128)(2,1)} %param.13) | copy-start | bytes 589828
  7.2 65.0 %all-gather.7.cloned.1.call-start = ((), (), s32[]{:S(2)}) async-start(), calls=%async_computation.2 | async-start | bytes 1966080 | tf_op jit(solution)/shard_map/all_gather | solution.py:361
  8.6 20.3 %collective-permute-start = (bf16[512,512]{1,0:T(8,128)(2,1)S(1)}, bf16[512,512]{1,0:T(8,128)(2,1)S(1)}, u32[]{:S(2)}, u32[]{:S(2)}) collective-permute-start(bf16[512,512]{1,0:T(8,128)(2,1)S(1)} %get-tuple-element.79), channel_id=1, source_target_pairs={{0,16},{16,32},{32,48},{48,0},{1,17},{17,33},{33,49},{49,1},{2,18}... | collective-permute-start | bytes 1572872 | tf_op jit(solution)/shard_map/ppermute | solution.py:344
  10.0 18.9 %collective-permute-start.2 = (bf16[512,512]{1,0:T(8,128)(2,1)S(1)}, bf16[512,512]{1,0:T(8,128)(2,1)S(1)}, u32[]{:S(2)}, u32[]{:S(2)}) collective-permute-start(bf16[512,512]{1,0:T(8,128)(2,1)S(1)} %get-tuple-element.79), channel_id=1, source_target_pairs={{0,48},{16,0},{32,16},{48,32},{1,49},{17,1},{33,17},{49,33},{2,50}... | collective-permute-start | bytes 1572872 | tf_op jit(solution)/shard_map/ppermute | solution.py:344
  11.5 9.6 %collective-permute-start.6 = (bf16[2,192,256]{2,1,0:T(8,128)(2,1)S(1)}, bf16[2,192,256]{2,1,0:T(8,128)(2,1)S(1)}, u32[]{:S(2)}, u32[]{:S(2)}) collective-permute-start(bf16[2,192,256]{2,1,0:T(8,128)(2,1)S(1)} %copy-done.21), channel_id=1, source_target_pairs={{0,0},{2,2},{4,4},{6,6},{8,64},{10,66},{12,68},{14,70},{64,8},{66,... | collective-permute-start | bytes 589832 | tf_op jit(solution)/shard_map/ppermute | solution.py:355
  17.0 11.1 %collective-permute-start.7 = (bf16[2,192,256]{2,1,0:T(8,128)(2,1)S(1)}, bf16[2,192,256]{2,1,0:T(8,128)(2,1)S(1)}, u32[]{:S(2)}, u32[]{:S(2)}) collective-permute-start(bf16[2,192,256]{2,1,0:T(8,128)(2,1)S(1)} %copy-done.21), channel_id=1, source_target_pairs={{0,2},{2,0},{4,6},{6,4},{8,66},{10,64},{12,70},{14,68},{64,10},{66... | collective-permute-start | bytes 589832 | tf_op jit(solution)/shard_map/ppermute | solution.py:356
  28.9 40.9 %copy-start.11 = (bf16[512,512]{1,0:T(8,128)(2,1)}, bf16[512,512]{1,0:T(8,128)(2,1)S(1)}, u32[]{:S(2)}) copy-start(bf16[512,512]{1,0:T(8,128)(2,1)S(1)} %collective-permute-done.x1) | copy-start | bytes 1572868
  28.9 40.9 %copy-start.12 = (bf16[512,512]{1,0:T(8,128)(2,1)}, bf16[512,512]{1,0:T(8,128)(2,1)S(1)}, u32[]{:S(2)}) copy-start(bf16[512,512]{1,0:T(8,128)(2,1)S(1)} %collective-permute-done.2.x3) | copy-start | bytes 1572868
  28.9 82.2 %all-gather.9.cloned.1.call-start = ((), (), s32[]{:S(2)}) async-start(), calls=%async_computation.3 | async-start | bytes 1966080 | tf_op jit(solution)/shard_map/all_gather | solution.py:361
  29.0 13.2 %collective-permute-start.3 = (bf16[512,512]{1,0:T(8,128)(2,1)S(1)}, bf16[512,512]{1,0:T(8,128)(2,1)S(1)}, u32[]{:S(2)}, u32[]{:S(2)}) collective-permute-start(bf16[512,512]{1,0:T(8,128)(2,1)S(1)} %get-tuple-element.78), channel_id=1, source_target_pairs={{0,48},{16,0},{32,16},{48,32},{1,49},{17,1},{33,17},{49,33},{2,50}... | collective-permute-start | bytes 1572872 | tf_op jit(solution)/shard_map/ppermute | solution.py:345
  30.4 13.9 %collective-permute-start.1 = (bf16[512,512]{1,0:T(8,128)(2,1)S(1)}, bf16[512,512]{1,0:T(8,128)(2,1)S(1)}, u32[]{:S(2)}, u32[]{:S(2)}) collective-permute-start(bf16[512,512]{1,0:T(8,128)(2,1)S(1)} %get-tuple-element.78), channel_id=1, source_target_pairs={{0,16},{16,32},{32,48},{48,0},{1,17},{17,33},{33,49},{49,1},{2,18}... | collective-permute-start | bytes 1572872 | tf_op jit(solution)/shard_map/ppermute | solution.py:345
  30.5 42.3 %copy-start.4 = (s32[1,2]{1,0:T(1,128)S(1)}, s32[1,2]{1,0:T(1,128)}, u32[]{:S(2)}) copy-start(s32[1,2]{1,0:T(1,128)} %param.10) | copy-start | bytes 28
  42.2 32.6 %copy-start.13 = (bf16[512,512]{1,0:T(8,128)(2,1)}, bf16[512,512]{1,0:T(8,128)(2,1)S(1)}, u32[]{:S(2)}) copy-start(bf16[512,512]{1,0:T(8,128)(2,1)S(1)} %collective-permute-done.3.x4) | copy-start | bytes 1572868
  44.3 30.5 %copy-start.14 = (bf16[512,512]{1,0:T(8,128)(2,1)}, bf16[512,512]{1,0:T(8,128)(2,1)S(1)}, u32[]{:S(2)}) copy-start(bf16[512,512]{1,0:T(8,128)(2,1)S(1)} %collective-permute-done.1.x2) | copy-start | bytes 1572868
  44.3 16.3 %collective-permute-start.8 = (bf16[2,2,192,256]{3,2,1,0:T(8,128)(2,1)S(1)}, bf16[2,2,192,256]{3,2,1,0:T(8,128)(2,1)S(1)}, u32[]{:S(2)}, u32[]{:S(2)}) collective-permute-start(bf16[2,2,192,256]{3,2,1,0:T(8,128)(2,1)S(1)} %pad_maximum_fusion.2), channel_id=1, source_target_pairs={{0,0},{2,2},{4,4},{6,6},{8,64},{10,66},{12,68},{14,70},{64,8},{66,... | collective-permute-start | bytes 1179656 | tf_op jit(solution)/shard_map/ppermute | solution.py:355
  46.2 21.9 %collective-permute-start.9 = (bf16[2,2,192,256]{3,2,1,0:T(8,128)(2,1)S(1)}, bf16[2,2,192,256]{3,2,1,0:T(8,128)(2,1)S(1)}, u32[]{:S(2)}, u32[]{:S(2)}) collective-permute-start(bf16[2,2,192,256]{3,2,1,0:T(8,128)(2,1)S(1)} %pad_maximum_fusion.2), channel_id=1, source_target_pairs={{0,2},{2,0},{4,6},{6,4},{8,66},{10,64},{12,70},{14,68},{64,10},{66... | collective-permute-start | bytes 1179656 | tf_op jit(solution)/shard_map/ppermute | solution.py:356
  47.6 22.2 %collective-permute-start.4 = (bf16[512,512]{1,0:T(8,128)(2,1)S(1)}, bf16[512,512]{1,0:T(8,128)(2,1)S(1)}, u32[]{:S(2)}, u32[]{:S(2)}) collective-permute-start(bf16[512,512]{1,0:T(8,128)(2,1)S(1)} %collective-permute-done.x1), channel_id=1, source_target_pairs={{0,16},{16,32},{32,48},{48,0},{1,17},{17,33},{33,49},{49,1},{2,18}... | collective-permute-start | bytes 1572872 | tf_op jit(solution)/shard_map/ppermute | solution.py:350
  47.6 22.2 %collective-permute-start.5 = (bf16[512,512]{1,0:T(8,128)(2,1)S(1)}, bf16[512,512]{1,0:T(8,128)(2,1)}, u32[]{:S(2)}, u32[]{:S(2)}) collective-permute-start(bf16[512,512]{1,0:T(8,128)(2,1)S(1)} %collective-permute-done.3.x4), channel_id=1, source_target_pairs={{0,48},{16,0},{32,16},{48,32},{1,49},{17,1},{33,17},{49,33},{2,50}... | collective-permute-start | bytes 1572872 | tf_op jit(solution)/shard_map/ppermute | solution.py:350
  69.0 61.1 %all-gather.11.cloned.1.call-start = ((), (), s32[]{:S(2)}) async-start(), calls=%async_computation.4 | async-start | bytes 1966080 | tf_op jit(solution)/shard_map/all_gather | solution.py:361
  72.2 4.0 %collective-permute-start.10 = (bf16[4,2,2,192,256]{4,3,2,1,0:T(8,128)(2,1)}, bf16[4,2,2,192,256]{4,3,2,1,0:T(8,128)(2,1)}, u32[]{:S(2)}, u32[]{:S(2)}) collective-permute-start(bf16[4,2,2,192,256]{4,3,2,1,0:T(8,128)(2,1)} %bitcast.30), channel_id=1, source_target_pairs={{0,1},{1,0},{2,3},{3,2},{4,5},{5,4},{6,7},{7,6},{8,9},{9,8},{10,11... | collective-permute-start | bytes 4718600 | tf_op jit(solution)/shard_map/ppermute | solution.py:362
  84.8 26.3 %collective-permute-start.11 = (bf16[1024,384]{1,0:T(8,128)(2,1)}, bf16[1024,384]{1,0:T(8,128)(2,1)S(1)}, u32[]{:S(2)}, u32[]{:S(2)}) collective-permute-start(bf16[1024,384]{1,0:T(8,128)(2,1)} %get-tuple-element.42), channel_id=1, source_target_pairs={{0,64},{64,0},{1,65},{65,1},{2,66},{66,2},{3,67},{67,3},{4,68},{68... | collective-permute-start | bytes 2359304 | tf_op jit(solution)/shard_map/ppermute | solution.py:392
  85.0 14.3 %collective-permute-start.12 = (bf16[512,512]{1,0:T(8,128)(2,1)S(1)}, bf16[512,512]{1,0:T(8,128)(2,1)S(1)}, u32[]{:S(2)}, u32[]{:S(2)}) collective-permute-start(bf16[512,512]{1,0:T(8,128)(2,1)S(1)} %get-tuple-element.77), channel_id=1, source_target_pairs={{0,16},{16,32},{32,48},{48,0},{1,17},{17,33},{33,49},{49,1},{2,18}... | collective-permute-start | bytes 1572872 | tf_op jit(solution)/shard_map/ppermute | solution.py:344
  86.3 24.1 %collective-permute-start.13 = (bf16[512,512]{1,0:T(8,128)(2,1)S(1)}, bf16[512,512]{1,0:T(8,128)(2,1)S(1)}, u32[]{:S(2)}, u32[]{:S(2)}) collective-permute-start(bf16[512,512]{1,0:T(8,128)(2,1)S(1)} %get-tuple-element.76), channel_id=1, source_target_pairs={{0,16},{16,32},{32,48},{48,0},{1,17},{17,33},{33,49},{49,1},{2,18}... | collective-permute-start | bytes 1572872 | tf_op jit(solution)/shard_map/ppermute | solution.py:345
  87.5 22.9 %collective-permute-start.14 = (bf16[512,512]{1,0:T(8,128)(2,1)S(1)}, bf16[512,512]{1,0:T(8,128)(2,1)S(1)}, u32[]{:S(2)}, u32[]{:S(2)}) collective-permute-start(bf16[512,512]{1,0:T(8,128)(2,1)S(1)} %get-tuple-element.77), channel_id=1, source_target_pairs={{0,48},{16,0},{32,16},{48,32},{1,49},{17,1},{33,17},{49,33},{2,50}... | collective-permute-start | bytes 1572872 | tf_op jit(solution)/shard_map/ppermute | solution.py:344
  89.0 22.2 %collective-permute-start.15 = (bf16[512,512]{1,0:T(8,128)(2,1)S(1)}, bf16[512,512]{1,0:T(8,128)(2,1)}, u32[]{:S(2)}, u32[]{:S(2)}) collective-permute-start(bf16[512,512]{1,0:T(8,128)(2,1)S(1)} %get-tuple-element.76), channel_id=1, source_target_pairs={{0,48},{16,0},{32,16},{48,32},{1,49},{17,1},{33,17},{49,33},{2,50}... | collective-permute-start | bytes 1572872 | tf_op jit(solution)/shard_map/ppermute | solution.py:345
  89.3 178.1 %reduce-scatter.2.cloned.1.call-start = ((), (), s32[]{:S(2)}) async-start(), calls=%async_computation.1 | async-start | bytes 5898240 | tf_op jit(solution)/shard_map/reduce_scatter | solution.py:408
  99.3 47.8 %copy-start.16 = (bf16[512,512]{1,0:T(8,128)(2,1)}, bf16[512,512]{1,0:T(8,128)(2,1)S(1)}, u32[]{:S(2)}) copy-start(bf16[512,512]{1,0:T(8,128)(2,1)S(1)} %collective-permute-done.12.x1.g1) | copy-start | bytes 1572868
  110.4 21.5 %copy-start.17 = (bf16[512,512]{1,0:T(8,128)(2,1)}, bf16[512,512]{1,0:T(8,128)(2,1)S(1)}, u32[]{:S(2)}) copy-start(bf16[512,512]{1,0:T(8,128)(2,1)S(1)} %collective-permute-done.13.x2.g2) | copy-start | bytes 1572868
  110.5 21.5 %copy-start.18 = (bf16[512,512]{1,0:T(8,128)(2,1)}, bf16[512,512]{1,0:T(8,128)(2,1)S(1)}, u32[]{:S(2)}) copy-start(bf16[512,512]{1,0:T(8,128)(2,1)S(1)} %collective-permute-done.14.x3.g3) | copy-start | bytes 1572868
  111.2 45.6 %copy-start.7 = (bf16[1024,384]{1,0:T(8,128)(2,1)}, bf16[1024,384]{1,0:T(8,128)(2,1)S(1)}, u32[]{:S(2)}) copy-start(bf16[1024,384]{1,0:T(8,128)(2,1)S(1)} %collective-permute-done.11.got_g) | copy-start | bytes 2359300
  111.2 5.4 %collective-permute-start.16 = (bf16[4,2,2,192,256]{4,3,2,1,0:T(8,128)(2,1)}, bf16[4,2,2,192,256]{4,3,2,1,0:T(8,128)(2,1)S(1)}, u32[]{:S(2)}, u32[]{:S(2)}) collective-permute-start(bf16[4,2,2,192,256]{4,3,2,1,0:T(8,128)(2,1)} %bitcast.33), channel_id=1, source_target_pairs={{0,1},{1,0},{2,3},{3,2},{4,5},{5,4},{6,7},{7,6},{8,9},{9,8},{10,11... | collective-permute-start | bytes 4718600 | tf_op jit(solution)/shard_map/ppermute | solution.py:362
  130.1 17.1 %collective-permute-start.20 = (bf16[4,2,2,192,256]{4,3,2,1,0:T(8,128)(2,1)}, bf16[4,2,2,192,256]{4,3,2,1,0:T(8,128)(2,1)S(1)}, u32[]{:S(2)}, u32[]{:S(2)}) collective-permute-start(bf16[4,2,2,192,256]{4,3,2,1,0:T(8,128)(2,1)} %bitcast.36), channel_id=1, source_target_pairs={{0,1},{1,0},{2,3},{3,2},{4,5},{5,4},{6,7},{7,6},{8,9},{9,8},{10,11... | collective-permute-start | bytes 4718600 | tf_op jit(solution)/shard_map/ppermute | solution.py:362
  130.7 14.8 %collective-permute-start.18 = (bf16[512,512]{1,0:T(8,128)(2,1)S(1)}, bf16[512,512]{1,0:T(8,128)(2,1)S(1)}, u32[]{:S(2)}, u32[]{:S(2)}) collective-permute-start(bf16[512,512]{1,0:T(8,128)(2,1)S(1)} %collective-permute-done.12.x1.g1), channel_id=1, source_target_pairs={{0,16},{16,32},{32,48},{48,0},{1,17},{17,33},{33,49},{49,1},{2,18}... | collective-permute-start | bytes 1572872 | tf_op jit(solution)/shard_map/ppermute | solution.py:350
  132.0 14.4 %collective-permute-start.19 = (bf16[512,512]{1,0:T(8,128)(2,1)}, bf16[512,512]{1,0:T(8,128)(2,1)S(1)}, u32[]{:S(2)}, u32[]{:S(2)}) collective-permute-start(bf16[512,512]{1,0:T(8,128)(2,1)} %collective-permute-done.15.x4.g4), channel_id=1, source_target_pairs={{0,48},{16,0},{32,16},{48,32},{1,49},{17,1},{33,17},{49,33},{2,50}... | collective-permute-start | bytes 1572872 | tf_op jit(solution)/shard_map/ppermute | solution.py:350
  133.4 23.4 %collective-permute-start.17 = (bf16[1024,384]{1,0:T(8,128)(2,1)}, bf16[1024,384]{1,0:T(8,128)(2,1)S(1)}, u32[]{:S(2)}, u32[]{:S(2)}) collective-permute-start(bf16[1024,384]{1,0:T(8,128)(2,1)} %get-tuple-element.47), channel_id=1, source_target_pairs={{0,64},{64,0},{1,65},{65,1},{2,66},{66,2},{3,67},{67,3},{4,68},{68... | collective-permute-start | bytes 2359304 | tf_op jit(solution)/shard_map/ppermute | solution.py:395
  167.3 4.4 %collective-permute-start.22 = (bf16[4,2,1,2,192,256]{5,4,3,2,1,0:T(8,128)(2,1)}, bf16[4,2,1,2,192,256]{5,4,3,2,1,0:T(8,128)(2,1)S(1)}, u32[]{:S(2)}, u32[]{:S(2)}) collective-permute-start(bf16[4,2,1,2,192,256]{5,4,3,2,1,0:T(8,128)(2,1)} %get-tuple-element.55), channel_id=1, source_target_pairs={{0,1},{1,0},{2,3},{3,2},{4,5},{5,4},{6,7},{7,6},{8,9},{9,8},{10,11... | collective-permute-start | bytes 4718600 | tf_op jit(solution)/shard_map/ppermute | solution.py:401
  168.5 19.1 %collective-permute-start.21 = (bf16[1024,384]{1,0:T(8,128)(2,1)S(1)}, bf16[1024,384]{1,0:T(8,128)(2,1)S(1)}, u32[]{:S(2)}, u32[]{:S(2)}) collective-permute-start(bf16[1024,384]{1,0:T(8,128)(2,1)S(1)} %copy-done.9), channel_id=1, source_target_pairs={{0,64},{64,0},{1,65},{65,1},{2,66},{66,2},{3,67},{67,3},{4,68},{68... | collective-permute-start | bytes 2359304 | tf_op jit(solution)/shard_map/ppermute | solution.py:398
  205.0 6.4 %collective-permute-start.24 = (bf16[4,2,2,2,192,256]{5,4,3,2,1,0:T(8,128)(2,1)}, bf16[4,2,2,2,192,256]{5,4,3,2,1,0:T(8,128)(2,1)S(1)}, u32[]{:S(2)}, u32[]{:S(2)}) collective-permute-start(bf16[4,2,2,2,192,256]{5,4,3,2,1,0:T(8,128)(2,1)} %get-tuple-element.61), channel_id=1, source_target_pairs={{0,1},{1,0},{2,3},{3,2},{4,5},{5,4},{6,7},{7,6},{8,9},{9,8},{10,11... | collective-permute-start | bytes 9437192 | tf_op jit(solution)/shard_map/ppermute | solution.py:405
  205.9 2.7 collective-permute-start.23
  217.0 4.3 %collective-permute-start.25 = (f32[8,128]{1,0:T(8,128)S(1)}, f32[8,128]{1,0:T(8,128)S(1)}, u32[]{:S(2)}, u32[]{:S(2)}) collective-permute-start(f32[8,128]{1,0:T(8,128)S(1)} %add.43), channel_id=1, source_target_pairs={{0,32},{16,48},{32,0},{48,16},{1,33},{17,49},{33,1},{49,17},{2,34}... | collective-permute-start | bytes 12296 | tf_op jit(solution)/shard_map/ppermute | solution.py:411
  232.4 46.6 %copy-start = (bf16[1024,512]{1,0:T(8,128)(2,1)S(1)}, bf16[1024,512]{1,0:T(8,128)(2,1)}, u32[]{:S(2)}) copy-start(bf16[1024,512]{1,0:T(8,128)(2,1)} %get-tuple-element.67) | copy-start | bytes 3145732
  232.5 43.3 %collective-permute-start.26 = (bf16[1024,512]{1,0:T(8,128)(2,1)}, bf16[1024,512]{1,0:T(8,128)(2,1)S(1)}, u32[]{:S(2)}, u32[]{:S(2)}) collective-permute-start(bf16[1024,512]{1,0:T(8,128)(2,1)} %get-tuple-element.68), channel_id=1, source_target_pairs={{0,16},{16,32},{32,48},{48,0},{1,17},{17,33},{33,49},{49,1},{2,18}... | collective-permute-start | bytes 3145736 | tf_op jit(solution)/shard_map/ppermute | solution.py:414
  232.6 43.2 %collective-permute-start.27 = (bf16[1024,512]{1,0:T(8,128)(2,1)}, bf16[1024,512]{1,0:T(8,128)(2,1)S(1)}, u32[]{:S(2)}, u32[]{:S(2)}) collective-permute-start(bf16[1024,512]{1,0:T(8,128)(2,1)} %get-tuple-element.69), channel_id=1, source_target_pairs={{0,48},{16,0},{32,16},{48,32},{1,49},{17,1},{33,17},{49,33},{2,50}... | collective-permute-start | bytes 3145736 | tf_op jit(solution)/shard_map/ppermute | solution.py:415
  235.2 43.9 %collective-permute-start.28 = (bf16[1024,512]{1,0:T(8,128)(2,1)}, bf16[1024,512]{1,0:T(8,128)(2,1)}, u32[]{:S(2)}, u32[]{:S(2)}) collective-permute-start(bf16[1024,512]{1,0:T(8,128)(2,1)} %get-tuple-element.70), channel_id=1, source_target_pairs={{0,32},{16,48},{32,0},{48,16},{1,33},{17,49},{33,1},{49,17},{2,34}... | collective-permute-start | bytes 3145736 | tf_op jit(solution)/shard_map/ppermute | solution.py:416
  235.4 36.4 %collective-permute-start.29 = (f32[8,128]{1,0:T(8,128)S(1)}, f32[8,128]{1,0:T(8,128)S(1)}, u32[]{:S(2)}, u32[]{:S(2)}) collective-permute-start(f32[8,128]{1,0:T(8,128)S(1)} %add.45), channel_id=1, source_target_pairs={{0,64},{64,0},{1,65},{65,1},{2,66},{66,2},{3,67},{67,3},{4,68},{68... | collective-permute-start | bytes 12296 | tf_op jit(solution)/shard_map/ppermute | solution.py:413
  268.7 18.6 %collective-permute-start.30 = (bf16[3,2,192,256]{3,2,1,0:T(8,128)(2,1)S(1)}, bf16[3,2,192,256]{3,2,1,0:T(8,128)(2,1)S(1)}, u32[]{:S(2)}, u32[]{:S(2)}) collective-permute-start(bf16[3,2,192,256]{3,2,1,0:T(8,128)(2,1)S(1)} %get-tuple-element.74), channel_id=1, source_target_pairs={{0,0},{2,2},{4,4},{6,6},{8,64},{10,66},{12,68},{14,70},{64,8},{66,... | collective-permute-start | bytes 1769480 | tf_op jit(solution)/shard_map/ppermute | solution.py:372
  271.8 29.0 %collective-permute-start.31 = (bf16[3,2,192,256]{3,2,1,0:T(8,128)(2,1)S(1)}, bf16[3,2,192,256]{3,2,1,0:T(8,128)(2,1)S(1)}, u32[]{:S(2)}, u32[]{:S(2)}) collective-permute-start(bf16[3,2,192,256]{3,2,1,0:T(8,128)(2,1)S(1)} %get-tuple-element.75), channel_id=1, source_target_pairs={{0,2},{2,0},{4,6},{6,4},{8,66},{10,64},{12,70},{14,68},{64,10},{66... | collective-permute-start | bytes 1769480 | tf_op jit(solution)/shard_map/ppermute | solution.py:373
  (10 other events, 36.2 us)
Sparse Core Ops, SparseCore 0:
  29.1 43.1 all-gather.6
  74.5 26.6 all-gather.8
  103.4 26.6 all-gather.10
  217.2 50.1 reduce-scatter.1
